TPU v7x, 256 devices: a whole 4x4x8 slice. The times are simulated.
256 devices in a mesh: dp: 64 (over y_lo, x, z), mp: 2 (over y_hi), teach: 2 (over core).
Axes of the slice: x: 4, y: 4 (y_hi: 2, y_lo: 2; y = y_hi * 2 + y_lo), z: 8, core: 2. Of those that a mesh axis runs over, the one named last changes fastest.
Arguments:
- image_feats: bfloat16 [8192, 768], P('dp'), may hold values from -6 to 6
- student_text: bfloat16 [8192, 768], P(('dp', 'mp')), may hold values from -40 to 40
- student_head: bfloat16 [768, 768], P(None, 'mp'), may hold values from -2 to 2
- teacher_image: bfloat16 [8192, 1024], P(('dp', 'teach')), may hold values from -6 to 6
- teacher_text: bfloat16 [8192, 1024], P(('dp', 'mp', 'teach')), may hold values from -40 to 40
- group_index: int32 [64], P('dp'), may hold values from 0 to 3
Outputs:
- row_loss: float32 [8192], P('dp')
- image_grad: bfloat16 [8192, 768], P('dp', 'mp')
- text_grad: bfloat16 [8192, 768], P(('dp', 'mp'))
- weight_grad: float32 [768, 768], P(None, 'mp')
All inputs are finite; a program needn't handle non-finite values.
Results may differ from a plain program's by a relative error of at most 0.015.
Values may be sent and summed in bfloat16 or wider, within the bound.
No kernel may reach another device: no remote copies, remote signals or barrier semaphores. Data moves between devices by JAX's collectives and lax.ppermute only.
A program may use at most 64 MiB of HBM per device.

v0:
```python
import math

import jax
import jax.numpy as jnp
from jax import lax
from jax.sharding import PartitionSpec as P

GROUP_ROWS = 32


epsilon = 1e-06
loss_scale = 8.0


def inner_rows(left, right):
    return lax.dot_general(
        left, right, (((1,), (1,)), ((), ())), preferred_element_type=jnp.float32
    )


def shards(image_feats, student_text, student_head, teacher_image, teacher_text, group_index):
    model_width = student_head.shape[0]
    projected = jnp.dot(image_feats, student_head, preferred_element_type=jnp.float32)
    energy = lax.psum(jnp.sum(projected * projected, axis=1), "mp")
    row_factor = lax.rsqrt(energy / model_width + epsilon)[:, None]
    halves = (projected * row_factor).astype(jnp.bfloat16)
    queries = lax.all_gather(halves, "mp", axis=1, tiled=True)
    teach_rows = lax.all_gather(teacher_image, "teach", axis=0, tiled=True)
    text_cols = lax.all_gather(student_text, "dp", axis=0, tiled=True)
    teach_cols = lax.all_gather(teacher_text, ("dp", "teach"), axis=0, tiled=True)
    student_scale = 3.0 / math.sqrt(model_width)
    teacher_scale = 3.0 / math.sqrt(teach_rows.shape[1])
    student = student_scale * inner_rows(queries, text_cols)
    teacher = teacher_scale * inner_rows(teach_rows, teach_cols)
    top_t = jnp.max(teacher, axis=1)
    weights = jnp.exp(teacher - top_t[:, None])
    total_t = jnp.sum(weights, axis=1)
    cross_term = jnp.sum(weights * (teacher - student), axis=1)
    top_s = jnp.max(student, axis=1)
    total_s = jnp.sum(jnp.exp(student - top_s[:, None]), axis=1)
    high_t, high_s = lax.pmax((top_t, top_s), "mp")
    shift_t = jnp.exp(top_t - high_t)
    shift_s = jnp.exp(top_s - high_s)
    total_t, cross_term, total_s = lax.psum(
        (total_t * shift_t, cross_term * shift_t, total_s * shift_s), "mp"
    )
    top_t, top_s = (high_t, high_s)
    lse_t = top_t + jnp.log(total_t)
    lse_s = top_s + jnp.log(total_s)
    row_loss = cross_term / total_t - lse_t + lse_s
    logit_slope = (
        loss_scale * (jnp.exp(student - lse_s[:, None]) - jnp.exp(teacher - lse_t[:, None]))
    ).astype(jnp.bfloat16)
    partial_value = student_scale * jnp.dot(
        logit_slope, text_cols, preferred_element_type=jnp.float32
    )
    query_grad = lax.psum_scatter(
        partial_value.astype(jnp.bfloat16), "mp", scatter_dimension=1, tiled=True
    ).astype(jnp.float32)
    text_grad = lax.psum_scatter(
        student_scale
        * lax.dot_general(
            logit_slope, queries, (((0,), (0,)), ((), ())), preferred_element_type=jnp.float32
        ),
        "dp",
        scatter_dimension=0,
        tiled=True,
    ).astype(jnp.bfloat16)
    first_group = group_index[0] * GROUP_ROWS
    group_feats = lax.dynamic_slice_in_dim(image_feats, first_group, GROUP_ROWS, 0)
    group_grad = lax.dynamic_slice_in_dim(query_grad, first_group, GROUP_ROWS, 0)
    group_proj = jnp.dot(group_feats, student_head, preferred_element_type=jnp.float32)
    group_energy, inner_sum = lax.psum(
        (jnp.sum(group_proj * group_proj, axis=1), jnp.sum(group_grad * group_proj, axis=1)), "mp"
    )
    group_factor = lax.rsqrt(group_energy / model_width + epsilon)[:, None]
    head_slope = (
        group_factor * group_grad
        - group_factor * group_factor * group_factor * group_proj * inner_sum[:, None] / model_width
    ).astype(jnp.bfloat16)
    local_grad = lax.dot_general(
        group_feats, head_slope, (((0,), (0,)), ((), ())), preferred_element_type=jnp.float32
    )
    weight_grad = lax.psum(local_grad, "dp")
    return (row_loss, query_grad.astype(jnp.bfloat16), text_grad, weight_grad)


def solution(mesh):
    in_specs = (
        P("dp", None),
        P(("dp", "mp"), None),
        P(None, "mp"),
        P(("dp", "teach"), None),
        P(("dp", "mp", "teach"), None),
        P("dp"),
    )
    out_specs = (P("dp"), P("dp", "mp"), P(("dp", "mp"), None), P(None, "mp"))
    return jax.shard_map(shards, mesh=mesh, in_specs=in_specs, out_specs=out_specs, check_vma=False)
```

profile of v0, /device:TPU:24, one launch (start us, length us, event | category | flops | bytes accessed | tf_op | source)
XLA Modules:
  0.0 1523.7 jit_solution(1845714874954601775)
XLA Ops:
  7.2 0.0 copy-start
  7.2 0.0 all-gather.5.cloned.1.call-start
  7.2 0.7 all-gather.5.cloned.1.call-update
  7.9 0.0 all-gather.3.cloned.1.call-start
  8.0 0.7 all-gather.3.cloned.1.call-update
  8.7 0.0 reduce-scatter.7.cloned.1.call-start
  8.7 0.0 copy-done
  8.7 1.3 multiply_reduce_fusion.1
  10.0 6.5 psum.49
  16.5 0.1 multiply_convert_fusion.1
  16.6 6.8 all_gather.14
  23.4 2.2 all_gather.12
  25.5 294.3 %all-gather.5.cloned.1.call-done = bf16[4096,768]{1,0:T(8,128)(2,1)} async-done(((bf16[64,768]{1,0:T(8,128)(2,1)}), bf16[4096,768]{1,0:T(8,128)(2,1)}) %all-gather.5.cloned.1.call-update) | async-done | bytes 6291472 | tf_op jit(solution)/shard_map/all_gather | solution.py:29
  319.9 5.0 fusion.20
  324.9 215.5 %all-gather.3.cloned.1.call-done = bf16[4096,1024]{1,0:T(8,128)(2,1)} async-done(((bf16[32,1024]{1,0:T(8,128)(2,1)}), bf16[4096,1024]{1,0:T(8,128)(2,1)}) %all-gather.3.cloned.1.call-update) | async-done | bytes 8388624 | tf_op jit(solution)/shard_map/all_gather | solution.py:30
  540.3 7.6 fusion.21
  547.9 6.4 all-reduce.2
  554.4 2.5 multiply_reduce_fusion
  556.9 6.5 all-reduce.1
  563.3 2.2 multiply_convert_fusion
  565.6 0.0 copy-start.1
  565.6 1.0 copy-done.1
  566.6 3.8 fusion.1
  570.4 0.8 copy.10
  571.2 0.0 reduce-scatter.7.cloned.1.call-update
  571.2 0.0 reduce-scatter.5.cloned.1.call-start
  571.3 7.6 convolution_multiply_fusion
  578.9 0.0 copy-start.2
  578.9 0.0 reduce-scatter.5.cloned.1.call-update
  578.9 0.0 all-reduce.5.cloned.1.call-start
  579.7 7.5 reduce-scatter.7.cloned.1.call-done
  587.2 1.0 copy.11
  588.2 0.0 copy-done.2
  588.2 0.0 copy-start.3
  588.2 0.3 multiply_reduce_fusion.2
  588.5 6.5 all-reduce
  595.0 1.4 fusion.5
  596.4 0.0 all-reduce.5.cloned.1.call-update
  596.4 0.5 subtract_add_fusion
  596.9 338.5 %reduce-scatter.5.cloned.1.call-done = f32[64,768]{1,0:T(8,128)} async-done(((f32[4096,768]{1,0:T(8,128)}), f32[64,768]{1,0:T(8,128)}) %reduce-scatter.5.cloned.1.call-update) | async-done | bytes 196624 | tf_op jit(solution)/shard_map/reduce_scatter | solution.py:60
  935.5 1.6 convert_element_type.22
  937.0 577.8 %all-reduce.5.cloned.1.call-done = f32[768,384]{1,0:T(8,128)} async-done(((f32[768,384]{1,0:T(8,128)}), f32[768,384]{1,0:T(8,128)}) %all-reduce.5.cloned.1.call-update) | async-done | bytes 1179664 | tf_op jit(solution)/shard_map/psum | solution.py:84
  1514.8 2.4 copy.14
  1517.2 0.0 copy-done.3
  (5 shorter events, 0.0 us)
Async XLA Ops:
  7.2 1.5 copy-start
  7.2 312.7 %all-gather.5.cloned.1.call-start = ((), (), s32[]{:S(2)}) async-start(), calls=%async_computation.3 | async-start | bytes 6389760 | tf_op jit(solution)/shard_map/all_gather | solution.py:29
  7.9 532.4 %all-gather.3.cloned.1.call-start = ((), (), s32[]{:S(2)}) async-start(), calls=%async_computation.2 | async-start | bytes 8454144 | tf_op jit(solution)/shard_map/all_gather | solution.py:30
  8.7 578.5 %reduce-scatter.7.cloned.1.call-start = ((), (), s32[]{:S(2)}) async-start(), calls=%async_computation.6 | async-start | bytes 294912
  565.6 1.0 copy-start.1
  571.2 364.2 %reduce-scatter.5.cloned.1.call-start = ((), (), s32[]{:S(2)}) async-start(), calls=%async_computation.4 | async-start | bytes 12779520 | tf_op jit(solution)/shard_map/reduce_scatter | solution.py:60
  578.9 9.3 copy-start.2
  578.9 935.9 %all-reduce.5.cloned.1.call-start = ((), (), s32[]{:S(2)}) async-start(), calls=%async_computation.5 | async-start | bytes 2359296 | tf_op jit(solution)/shard_map/psum | solution.py:84
  588.2 929.0 %copy-start.3 = (bf16[128,384]{1,0:T(8,128)(2,1)}, bf16[128,384]{1,0:T(8,128)(2,1)S(1)}, u32[]{:S(2)}) copy-start(bf16[128,384]{1,0:T(8,128)(2,1)S(1)} %copy.11) | copy-start | bytes 294916
Sparse Core Ops, SparseCore 0:
  9.8 310.0 all-gather.4
  321.7 218.5 all-gather.2
  571.4 15.7 reduce-scatter.6
  589.6 345.8 reduce-scatter.4
  938.5 576.2 all-reduce.4
where the time goes:
time: 1520 us
  waiting for transfers between devices  1430 us (94%)
  blocking collectives  34.8 us (2%)
  matrix products  27 us (2%)
    psum x1, waiting for transfers between devices, shards(): weight_grad = lax.psum(local_grad, 'dp')  578 us
    reduce_scatter x1, waiting for transfers between devices, shards(): lax.psum_scatter(student_scale * lax.dot_general(logit_slope, queries, ((...  339 us
    all_gather x1, waiting for transfers between devices, shards(): text_cols = lax.all_gather(student_text, 'dp', axis=0, tiled=True)  294 us
    all_gather x1, waiting for transfers between devices, shards(): lax.all_gather(teacher_text, ('dp', 'teach'), axis=0, tiled=True)  215 us
  transfers between devices with their start and end apart: 5, of which 5 were waited for; matrix products, arithmetic and copies ran while one was open for 1% of the time, Pallas kernels for 0%

commit v1 on v0

v1 whole, which is shorter than its diff:
```python
import math

import jax
import jax.numpy as jnp
from jax import lax
from jax.sharding import Mesh, PartitionSpec as P

epsilon = 1e-06
loss_scale = 8.0

COLS = ("x", "yl", "yh")
bf16, f32 = jnp.bfloat16, jnp.float32


def to_all(value, axes, count):
    sent = jnp.broadcast_to(value[None], (count, *value.shape))
    return lax.all_to_all(sent, axes, 0, 0, tiled=True)


def pick(value, index, axis):
    return lax.dynamic_index_in_dim(value, index, axis, keepdims=False)


def swap(value, axis):
    return lax.ppermute(value, axis, [(0, 1), (1, 0)])


def sent_round(value):
    return [lax.ppermute(value, "z", [(i, (i + k) % 8) for i in range(8)]) for k in range(1, 8)]


def dot(left, right, left_dim, right_dim):
    return lax.dot_general(
        left, right, (((left_dim,), (right_dim,)), ((), ())), preferred_element_type=f32
    )


def shards(image_feats, student_text, student_head, teacher_image, teacher_text, group_index):
    core, high, here = lax.axis_index("c"), lax.axis_index("yh"), lax.axis_index("z")
    width, wide = student_head.shape[0], teacher_image.shape[1]
    half = width // 2
    student_scale, teacher_scale = 3.0 / math.sqrt(width), 3.0 / math.sqrt(wide)
    group = group_index[0]

    def block_first(value):
        return lax.dynamic_slice_in_dim(jnp.concatenate([value, value], 0), group, 4, 0)

    text_own = pick(student_text.reshape(2, 32, width), core, 0)
    cols_own = jnp.concatenate([text_own, teacher_text], 1)

    teach = pick(teacher_image.reshape(2, 2, 2, 8, wide), high, 1)
    keep, come = pick(teach, core, 1), swap(pick(teach, 1 - core, 1), "c")
    teach_own = jnp.where(core == 0, jnp.stack([keep, come]), jnp.stack([come, keep])).reshape(4, 8, wide)
    feats_own = pick(pick(image_feats.reshape(4, 2, 2, 8, width), high, 1), core, 1)
    own = block_first(jnp.concatenate([feats_own, teach_own], 2)).reshape(32, width + wide)
    sent = jnp.broadcast_to(cols_own[None], (16, 32, width + wide))
    cols = lax.all_to_all(sent, COLS, 0, 0, tiled=True)
    head_come = swap(pick(student_head.reshape(2, half, half), core, 0), "yh")
    cols, head_come, *round_z = lax.optimization_barrier((cols, head_come, *sent_round(own)))
    cols = cols.reshape(512, width + wide)
    rows_own = jnp.zeros((8, 32, width + wide), bf16)
    for k, block in enumerate([own] + round_z):
        rows_own = lax.dynamic_update_slice_in_dim(rows_own, block[None], (here - k) % 8, 0)
    block_z = rows_own[:, :8, :width].reshape(64, width)
    rows_own = rows_own.reshape(256, width + wide)
    block_all = to_all(block_z, COLS, 16).reshape(1024, width)

    rows_come, head_pair = swap(rows_own, "c"), swap(head_come, "c")
    head_other = jnp.where(
        core == 0, jnp.concatenate([head_come, head_pair], 0), jnp.concatenate([head_pair, head_come], 0)
    )
    head = jnp.where(
        high == 0,
        jnp.concatenate([student_head, head_other], 1),
        jnp.concatenate([head_other, student_head], 1),
    )
    text, teach = cols[:, :width], cols[:, width:]
    rows = jnp.concatenate([rows_own, rows_come], 0)

    projected = dot(rows[:, :width], head, 1, 0)
    factor = lax.rsqrt(jnp.sum(projected * projected, axis=1, keepdims=True) / width + epsilon)
    queries = (projected * factor).astype(bf16)
    student = student_scale * dot(text, queries, 1, 1)
    teacher = teacher_scale * dot(teach, rows[:, width:], 1, 1)
    top_t = jnp.max(teacher, axis=0)
    weights = jnp.exp(teacher - top_t)
    total_t = jnp.sum(weights, axis=0)
    cross = jnp.sum(weights * (teacher - student), axis=0)
    top_s = jnp.max(student, axis=0)
    total_s = jnp.sum(jnp.exp(student - top_s), axis=0)
    zero = jnp.zeros_like(top_t)

    def merged(stats):
        tops_t, totals_t, crosses, tops_s, totals_s = (stats[:, i] for i in range(5))
        high_t, high_s = jnp.max(tops_t, axis=0), jnp.max(tops_s, axis=0)
        shift_t = jnp.exp(tops_t - high_t)
        sum_t = jnp.sum(totals_t * shift_t, axis=0)
        sum_s = jnp.sum(totals_s * jnp.exp(tops_s - high_s), axis=0)
        sum_cross = jnp.sum(crosses * shift_t, axis=0)
        return jnp.stack([high_t, sum_t, sum_cross, high_s, sum_s, zero, zero, zero])

    stats = jnp.stack([top_t, total_t, cross, top_s, total_s, zero, zero, zero])
    block_all, *round_z = lax.optimization_barrier((block_all, *sent_round(stats)))
    stats = merged(jnp.stack([stats] + round_z))
    come = swap(stats, "c")
    come = jnp.concatenate([come[:, 256:], come[:, :256]], 1)
    high_t, sum_t, sum_cross, high_s, sum_s = merged(jnp.stack([stats, come]))[:5]
    lse_t, lse_s = high_t + jnp.log(sum_t), high_s + jnp.log(sum_s)
    losses = sum_cross / sum_t - lse_t + lse_s

    slope = (loss_scale * (jnp.exp(student - lse_s) - jnp.exp(teacher - lse_t))).astype(bf16)
    grad = student_scale * dot(slope, text, 0, 0)
    text_part = (student_scale * dot(slope, queries, 1, 0)).astype(bf16)

    grad = grad[:256] + swap(grad[256:].astype(bf16), "c").astype(f32)
    grad = grad.astype(bf16).reshape(8, 32, width)
    blocks = grad[:, :8].reshape(64, width)
    turned = lax.dynamic_slice_in_dim(jnp.concatenate([grad, grad], 0), here, 8, 0)[:, 8:]
    round_z = [
        lax.ppermute(jnp.concatenate([turned[k], blocks], 0), "z", [(i, (i + k) % 8) for i in range(8)])
        for k in range(1, 8)
    ]
    text_part = lax.all_to_all(text_part.reshape(16, 32, width), COLS, 0, 0, tiled=True)
    text_part, *round_z = lax.optimization_barrier((text_part, *round_z))
    grad = jnp.concatenate([turned[0], blocks], 0).astype(f32) + sum(r.astype(f32) for r in round_z)
    block_grad = grad[24:]
    grad = jnp.concatenate([pick(block_grad.reshape(8, 8, width), here, 0), grad[:24]], 0)

    block_proj = dot(block_z, head, 1, 0)
    block_factor = lax.rsqrt(jnp.sum(block_proj * block_proj, axis=1, keepdims=True) / width + epsilon)
    inner = jnp.sum(block_grad * block_proj, axis=1, keepdims=True)
    head_slope = (
        block_factor * block_grad
        - block_factor * block_factor * block_factor * block_proj * inner / width
    ).astype(bf16)
    head_slope = head_slope.reshape(64, 2, half).transpose(1, 0, 2)

    sent = jnp.broadcast_to(head_slope[None], (8, 2, 64, half)).reshape(16, 64, half)
    slopes = lax.all_to_all(sent, COLS, 0, 0, tiled=True)

    text_sum = jnp.sum(text_part.astype(f32), axis=0).astype(bf16)
    text_grad = lax.all_gather(text_sum, "c", axis=0, tiled=True)

    back = lambda value: lax.dynamic_slice_in_dim(jnp.concatenate([value, value], 0), 4 - group, 4, 0)
    halves = back(grad.astype(bf16).reshape(4, 8, width)).reshape(32, 2, half)
    mine, come = pick(halves, high, 1), swap(pick(halves, 1 - high, 1), "yh")
    pair = jnp.where(high == 0, jnp.stack([mine, come]), jnp.stack([come, mine]))
    pair = lax.all_gather(pair, "c", axis=0)
    image_grad = pair.reshape(2, 2, 4, 8, half).transpose(2, 1, 0, 3, 4).reshape(128, half)

    losses = pick(losses.reshape(2, 8, 4, 8), here, 1)
    losses = jnp.where(core == 0, losses, losses[::-1])
    losses = back(losses.transpose(1, 0, 2))
    come = swap(losses, "yh")
    row_loss = jnp.where(high == 0, jnp.stack([losses, come], 1), jnp.stack([come, losses], 1)).reshape(128)
    slopes, row_loss, image_grad, text_grad = lax.optimization_barrier(
        (slopes, row_loss, image_grad, text_grad)
    )
    part = dot(block_all, slopes.reshape(1024, half), 0, 0)
    weight_grad = part + swap(part.astype(bf16), "c").astype(f32)
    return row_loss, image_grad, text_grad, weight_grad


def solution(mesh):
    mesh = Mesh(mesh.devices.reshape(2, 4, 8, 2, 2), ("yl", "x", "z", "yh", "c"))
    dp = ("yl", "x", "z")
    in_specs = (
        P(dp, None),
        P((*dp, "yh"), None),
        P(None, "yh"),
        P((*dp, "c"), None),
        P((*dp, "yh", "c"), None),
        P(dp),
    )
    out_specs = (P(dp), P(dp, "yh"), P((*dp, "yh"), None), P(None, "yh"))
    return jax.shard_map(shards, mesh=mesh, in_specs=in_specs, out_specs=out_specs, check_vma=False)
```

time: 1520 us -> 172 us (0.11)
  the two profiles are of different devices: /device:TPU:24 before, /device:TPU:1 now
where the time goes in v1:
time: 172 us; the launch traced here: 171 us
  starting transfers between devices  80.7 us (47%)
  waiting for transfers between devices  45.9 us (27%)
  local copies, waits for them, and re-layouts  15.6 us (9%)
  matrix products  11.6 us (7%)
  other arithmetic  8.91 us (5%)
  blocking collectives  5.89 us (3%)
  between operations  1.88 us (1%)
    ppermute x14, starting transfers between devices, sent_round(): lax.ppermute(value, 'z', [(i, (i + k) % 8) for i in range(8)])  27.6 us
    ppermute x14, waiting for transfers between devices, sent_round(): lax.ppermute(value, 'z', [(i, (i + k) % 8) for i in range(8)])  19.7 us
    ppermute x7, waiting for transfers between devices, shards(): lax.ppermute(jnp.concatenate([turned[k], blocks], 0), 'z', [(i, (i + k) %...  17.7 us
    ppermute x9, starting transfers between devices, swap(): return lax.ppermute(value, axis, [(0, 1), (1, 0)])  16.1 us
    ppermute x7, starting transfers between devices, shards(): lax.ppermute(jnp.concatenate([turned[k], blocks], 0), 'z', [(i, (i + k) %...  13.3 us
    dot_general x7, matrix products, dot(): lax.dot_general(left, right, (((left_dim,), (right_dim,)), ((), ())), pre...  11.6 us
    all_to_all x1, starting transfers between devices, shards(): cols = lax.all_to_all(sent, COLS, 0, 0, tiled=True)  7.72 us
    dynamic_update_slice x7, local copies, waits for them, and re-layouts, shards(): lax.dynamic_update_slice_in_dim(rows_own, block[None], (here - k) % 8, 0)  6.39 us
  transfers between devices with their start and end apart: 34, of which 15 were waited for; matrix products, arithmetic and copies ran while one was open for 8% of the time, Pallas kernels for 0%

profile of v1, /device:TPU:1, one launch (start us, length us, event | category | flops | bytes accessed | tf_op | source)
XLA Modules:
  0.0 170.6 jit_solution(15908645039432469388)
XLA Ops:
  1.5 0.8 pad_maximum_fusion.10
  2.3 1.5 broadcast_in_dim.23
  3.8 7.7 %all-to-all-start = ((bf16[16,32,1792]{2,1,0:T(8,128)(2,1)}), bf16[16,32,1792]{2,1,0:T(8,128)(2,1)S(1)}, u32[]{:S(2)}, u32[]{:S(2)}) async-start(bf16[16,32,1792]{2,1,0:T(8,128)(2,1)} %broadcast_in_dim.23), calls=%async_computation | async-start | bytes 3670016 | tf_op jit(solution)/shard_map/all_to_all | solution.py:57
  11.6 1.0 collective-permute-start
  12.7 3.2 %collective-permute-start.1 = (bf16[384,384]{1,0:T(8,128)(2,1)S(1)}, bf16[384,384]{1,0:T(8,128)(2,1)S(1)}, u32[]{:S(2)}, u32[]{:S(2)}) collective-permute-start(bf16[384,384]{1,0:T(8,128)(2,1)S(1)} %dynamic-slice_bitcast_fusion), channel_id=1, source_target_pairs={{0,2},{2,0},{1,3},{3,1},{4,6},{6,4},{5,7},{7,5},{8,10},{10,8},{9,1... | collective-permute-start | bytes 884744 | tf_op jit(solution)/shard_map/ppermute | solution.py:25
  17.3 1.6 bitcast_dynamic-update-slice_fusion.7
  18.9 1.7 collective-permute-start.2
  20.5 3.0 %collective-permute-start.3 = (bf16[32,1792]{1,0:T(8,128)(2,1)}, bf16[32,1792]{1,0:T(8,128)(2,1)}, u32[]{:S(2)}, u32[]{:S(2)}) collective-permute-start(bf16[32,1792]{1,0:T(8,128)(2,1)} %bitcast.13), channel_id=1, source_target_pairs={{0,8},{4,12},{8,16},{12,20},{16,24},{20,28},{24,0},{28,4},{1,9},{5... | collective-permute-start | bytes 344072 | tf_op jit(solution)/shard_map/ppermute | solution.py:29
  23.5 3.7 %collective-permute-start.4 = (bf16[32,1792]{1,0:T(8,128)(2,1)}, bf16[32,1792]{1,0:T(8,128)(2,1)}, u32[]{:S(2)}, u32[]{:S(2)}) collective-permute-start(bf16[32,1792]{1,0:T(8,128)(2,1)} %bitcast.13), channel_id=1, source_target_pairs={{0,12},{4,16},{8,20},{12,24},{16,28},{20,0},{24,4},{28,8},{1,13},{... | collective-permute-start | bytes 344072 | tf_op jit(solution)/shard_map/ppermute | solution.py:29
  28.0 4.1 %collective-permute-start.6 = (bf16[32,1792]{1,0:T(8,128)(2,1)}, bf16[32,1792]{1,0:T(8,128)(2,1)}, u32[]{:S(2)}, u32[]{:S(2)}) collective-permute-start(bf16[32,1792]{1,0:T(8,128)(2,1)} %bitcast.13), channel_id=1, source_target_pairs={{0,20},{4,24},{8,28},{12,0},{16,4},{20,8},{24,12},{28,16},{1,21},{... | collective-permute-start | bytes 344072 | tf_op jit(solution)/shard_map/ppermute | solution.py:29
  32.2 2.4 %collective-permute-start.7 = (bf16[32,1792]{1,0:T(8,128)(2,1)}, bf16[32,1792]{1,0:T(8,128)(2,1)}, u32[]{:S(2)}, u32[]{:S(2)}) collective-permute-start(bf16[32,1792]{1,0:T(8,128)(2,1)} %bitcast.13), channel_id=1, source_target_pairs={{0,24},{4,28},{8,0},{12,4},{16,8},{20,12},{24,16},{28,20},{1,25},{... | collective-permute-start | bytes 344072 | tf_op jit(solution)/shard_map/ppermute | solution.py:29
  34.6 8.2 %collective-permute-done.4 = bf16[32,1792]{1,0:T(8,128)(2,1)} collective-permute-done((bf16[32,1792]{1,0:T(8,128)(2,1)}, bf16[32,1792]{1,0:T(8,128)(2,1)}, u32[]{:S(2)}, u32[]{:S(2)}) %collective-permute-start.4) | collective-permute-done | bytes 114720 | tf_op jit(solution)/shard_map/ppermute | solution.py:29
  42.8 7.4 %collective-permute-done.7 = bf16[32,1792]{1,0:T(8,128)(2,1)} collective-permute-done((bf16[32,1792]{1,0:T(8,128)(2,1)}, bf16[32,1792]{1,0:T(8,128)(2,1)}, u32[]{:S(2)}, u32[]{:S(2)}) %collective-permute-start.7) | collective-permute-done | bytes 114720 | tf_op jit(solution)/shard_map/ppermute | solution.py:29
  50.2 1.1 collective-permute-done.8
  51.2 0.9 bitcast_dynamic-update-slice_fusion.6
  52.1 0.9 bitcast_dynamic-update-slice_fusion.5
  53.1 0.9 bitcast_dynamic-update-slice_fusion.4
  54.0 0.9 bitcast_dynamic-update-slice_fusion.3
  54.9 0.9 bitcast_dynamic-update-slice_fusion.2
  55.8 0.9 bitcast_dynamic-update-slice_fusion.1
  56.7 0.9 bitcast_dynamic-update-slice_fusion
  57.7 1.1 collective-permute-start.10
  58.9 1.3 broadcast_in_dim.61
  60.2 4.7 %all-to-all-start.1 = ((bf16[16,64,768]{2,1,0:T(8,128)(2,1)}), bf16[16,64,768]{2,1,0:T(8,128)(2,1)}, u32[]{:S(2)}, u32[]{:S(2)}) async-start(bf16[16,64,768]{2,1,0:T(8,128)(2,1)} %broadcast_in_dim.61), calls=%async_computation.1 | async-start | bytes 3145728 | tf_op jit(solution)/shard_map/all_to_all | solution.py:17
  65.2 2.5 %multiply_reduce_fusion = (f32[512]{0:T(512)S(1)}, f32[512,768]{1,0:T(8,128)S(1)}) fusion(bf16[768,384]{1,0:T(8,128)(2,1)S(1)} %maximum_select_fusion.1, bf16[768,384]{1,0:T(8,128)(2,1)} %param.8, pred[]{:T(512)S(6)} %eq.20, bf16[256,1792]{1,0:T(8,128)(2,1)} %collective-permute-done.10, bf16[256,1792]{1,0:T(8,128)(2,1)S(1)} %bitcast.200), kind=kOutput, calls=%fused_computation.2 | convolution fusion | flops 611646976 | bytes 4589569 | tf_op jit(solution)/shard_map/dot_general | solution.py:33
  67.7 2.2 %fusion.45 = (f32[512]{0:T(512)S(1)}, f32[512,512]{1,0:T(8,128)S(1)}) fusion(bf16[256,1792]{1,0:T(8,128)(2,1)} %collective-permute-done.10, bf16[256,1792]{1,0:T(8,128)(2,1)S(1)} %bitcast.201, bf16[512,1792]{1,0:T(8,128)(2,1)S(1)} %bitcast.193), kind=kOutput, calls=%fused_computation.149 | convolution fusion | flops 539491840 | bytes 3934208 | tf_op jit(solution)/shard_map/dot_general | solution.py:33
  71.3 2.1 %collective-permute-start.11 = (f32[8,512]{1,0:T(8,128)S(1)}, f32[8,512]{1,0:T(8,128)S(1)}, u32[]{:S(2)}, u32[]{:S(2)}) collective-permute-start(f32[8,512]{1,0:T(8,128)S(1)} %stack.123), channel_id=1, source_target_pairs={{0,4},{4,8},{8,12},{12,16},{16,20},{20,24},{24,28},{28,0},{1,5},{5... | collective-permute-start | bytes 49160 | tf_op jit(solution)/shard_map/ppermute | solution.py:29
  73.4 0.9 collective-permute-start.12
  74.3 2.5 %collective-permute-start.13 = (f32[8,512]{1,0:T(8,128)S(1)}, f32[8,512]{1,0:T(8,128)S(1)}, u32[]{:S(2)}, u32[]{:S(2)}) collective-permute-start(f32[8,512]{1,0:T(8,128)S(1)} %stack.123), channel_id=1, source_target_pairs={{0,12},{4,16},{8,20},{12,24},{16,28},{20,0},{24,4},{28,8},{1,13},{... | collective-permute-start | bytes 49160 | tf_op jit(solution)/shard_map/ppermute | solution.py:29
  76.9 2.2 %collective-permute-start.14 = (f32[8,512]{1,0:T(8,128)S(1)}, f32[8,512]{1,0:T(8,128)S(1)}, u32[]{:S(2)}, u32[]{:S(2)}) collective-permute-start(f32[8,512]{1,0:T(8,128)S(1)} %stack.123), channel_id=1, source_target_pairs={{0,16},{4,20},{8,24},{12,28},{16,0},{20,4},{24,8},{28,12},{1,17},{... | collective-permute-start | bytes 49160 | tf_op jit(solution)/shard_map/ppermute | solution.py:29
  79.1 2.1 %collective-permute-start.15 = (f32[8,512]{1,0:T(8,128)S(1)}, f32[8,512]{1,0:T(8,128)S(1)}, u32[]{:S(2)}, u32[]{:S(2)}) collective-permute-start(f32[8,512]{1,0:T(8,128)S(1)} %stack.123), channel_id=1, source_target_pairs={{0,20},{4,24},{8,28},{12,0},{16,4},{20,8},{24,12},{28,16},{1,21},{... | collective-permute-start | bytes 49160 | tf_op jit(solution)/shard_map/ppermute | solution.py:29
  81.2 2.0 %collective-permute-start.16 = (f32[8,512]{1,0:T(8,128)S(1)}, f32[8,512]{1,0:T(8,128)S(1)}, u32[]{:S(2)}, u32[]{:S(2)}) collective-permute-start(f32[8,512]{1,0:T(8,128)S(1)} %stack.123), channel_id=1, source_target_pairs={{0,24},{4,28},{8,0},{12,4},{16,8},{20,12},{24,16},{28,20},{1,25},{... | collective-permute-start | bytes 49160 | tf_op jit(solution)/shard_map/ppermute | solution.py:29
  83.9 1.5 collective-permute-done.16
  85.4 0.9 collective-permute-done.17
  86.4 2.7 %all-to-all-done.1 = bf16[16,64,768]{2,1,0:T(8,128)(2,1)} async-done(((bf16[16,64,768]{2,1,0:T(8,128)(2,1)}), bf16[16,64,768]{2,1,0:T(8,128)(2,1)}, u32[]{:S(2)}, u32[]{:S(2)}) %all-to-all-start.1) | async-done | bytes 1572896 | tf_op jit(solution)/shard_map/all_to_all | solution.py:17
  89.3 1.8 %collective-permute-start.18 = (f32[8,512]{1,0:T(8,128)S(1)}, f32[8,512]{1,0:T(8,128)S(1)}, u32[]{:S(2)}, u32[]{:S(2)}) collective-permute-start(f32[8,512]{1,0:T(8,128)S(1)} %stack.138), channel_id=1, source_target_pairs={{0,1},{1,0},{2,3},{3,2},{4,5},{5,4},{6,7},{7,6},{8,9},{9,8},{10,11... | collective-permute-start | bytes 49160 | tf_op jit(solution)/shard_map/ppermute | solution.py:25
  92.1 1.5 multiply_convert_fusion.2
  94.2 1.2 copy-done.3
  95.9 1.6 multiply_convert_fusion
  97.4 5.4 %all-to-all-start.2 = ((bf16[16,32,768]{2,1,0:T(8,128)(2,1)}), bf16[16,32,768]{2,1,0:T(8,128)(2,1)S(1)}, u32[]{:S(2)}, u32[]{:S(2)}) async-start(bf16[16,32,768]{2,1,0:T(8,128)(2,1)} %bitcast.196), calls=%async_computation.2 | async-start | bytes 1572864 | tf_op jit(solution)/shard_map/all_to_all | solution.py:123
  103.0 1.1 fusion.3
  104.4 1.8 %collective-permute-start.20 = (bf16[88,768]{1,0:T(8,128)(2,1)S(1)}, bf16[88,768]{1,0:T(8,128)(2,1)S(1)}, u32[]{:S(2)}, u32[]{:S(2)}) collective-permute-start(bf16[88,768]{1,0:T(8,128)(2,1)S(1)} %get-tuple-element.96), channel_id=1, source_target_pairs={{0,4},{4,8},{8,12},{12,16},{16,20},{20,24},{24,28},{28,0},{1,5},{5... | collective-permute-start | bytes 405512 | tf_op jit(solution)/shard_map/ppermute | solution.py:120
  106.2 1.0 collective-permute-start.21
  107.1 3.0 %collective-permute-start.27 = (f32[4,2,8]{2,0,1:T(4,128)S(1)}, f32[4,2,8]{2,0,1:T(4,128)S(1)}, u32[]{:S(2)}, u32[]{:S(2)}) collective-permute-start(f32[4,2,8]{2,0,1:T(4,128)S(1)} %fusion.28), channel_id=1, source_target_pairs={{0,2},{2,0},{1,3},{3,1},{4,6},{6,4},{5,7},{7,5},{8,10},{10,8},{9,1... | collective-permute-start | bytes 776 | tf_op jit(solution)/shard_map/ppermute | solution.py:25
  110.1 2.5 %collective-permute-start.22 = (bf16[88,768]{1,0:T(8,128)(2,1)S(1)}, bf16[88,768]{1,0:T(8,128)(2,1)S(1)}, u32[]{:S(2)}, u32[]{:S(2)}) collective-permute-start(bf16[88,768]{1,0:T(8,128)(2,1)S(1)} %get-tuple-element.98), channel_id=1, source_target_pairs={{0,12},{4,16},{8,20},{12,24},{16,28},{20,0},{24,4},{28,8},{1,13},{... | collective-permute-start | bytes 405512 | tf_op jit(solution)/shard_map/ppermute | solution.py:120
  112.6 2.7 %collective-permute-start.23 = (bf16[88,768]{1,0:T(8,128)(2,1)S(1)}, bf16[88,768]{1,0:T(8,128)(2,1)}, u32[]{:S(2)}, u32[]{:S(2)}) collective-permute-start(bf16[88,768]{1,0:T(8,128)(2,1)S(1)} %get-tuple-element.99), channel_id=1, source_target_pairs={{0,16},{4,20},{8,24},{12,28},{16,0},{20,4},{24,8},{28,12},{1,17},{... | collective-permute-start | bytes 405512 | tf_op jit(solution)/shard_map/ppermute | solution.py:120
  115.3 1.5 collective-permute-start.24
  116.9 2.4 %collective-permute-start.25 = (bf16[88,768]{1,0:T(8,128)(2,1)S(1)}, bf16[88,768]{1,0:T(8,128)(2,1)}, u32[]{:S(2)}, u32[]{:S(2)}) collective-permute-start(bf16[88,768]{1,0:T(8,128)(2,1)S(1)} %get-tuple-element.101), channel_id=1, source_target_pairs={{0,24},{4,28},{8,0},{12,4},{16,8},{20,12},{24,16},{28,20},{1,25},{... | collective-permute-start | bytes 405512 | tf_op jit(solution)/shard_map/ppermute | solution.py:120
  119.3 1.4 collective-permute-start.26
  121.3 2.1 %collective-permute-done.22 = bf16[88,768]{1,0:T(8,128)(2,1)S(1)} collective-permute-done((bf16[88,768]{1,0:T(8,128)(2,1)S(1)}, bf16[88,768]{1,0:T(8,128)(2,1)S(1)}, u32[]{:S(2)}, u32[]{:S(2)}) %collective-permute-start.22) | collective-permute-done | bytes 135200 | tf_op jit(solution)/shard_map/ppermute | solution.py:120
  123.3 6.2 %collective-permute-done.23 = bf16[88,768]{1,0:T(8,128)(2,1)} collective-permute-done((bf16[88,768]{1,0:T(8,128)(2,1)S(1)}, bf16[88,768]{1,0:T(8,128)(2,1)}, u32[]{:S(2)}, u32[]{:S(2)}) %collective-permute-start.23) | collective-permute-done | bytes 135200 | tf_op jit(solution)/shard_map/ppermute | solution.py:120
  129.6 8.7 %collective-permute-done.25 = bf16[88,768]{1,0:T(8,128)(2,1)} collective-permute-done((bf16[88,768]{1,0:T(8,128)(2,1)S(1)}, bf16[88,768]{1,0:T(8,128)(2,1)}, u32[]{:S(2)}, u32[]{:S(2)}) %collective-permute-start.25) | collective-permute-done | bytes 135200 | tf_op jit(solution)/shard_map/ppermute | solution.py:120
  139.0 1.4 add_add_fusion
  140.4 1.5 multiply_reduce_fusion.3
  142.0 1.0 broadcast_in_dim.62
  143.0 5.9 %all-to-all-start.3 = ((bf16[16,64,384]{2,1,0:T(8,128)(2,1)}), bf16[16,64,384]{2,1,0:T(8,128)(2,1)}, u32[]{:S(2)}, u32[]{:S(2)}) async-start(bf16[16,64,384]{2,1,0:T(8,128)(2,1)} %bitcast.63), calls=%async_computation.3 | async-start | bytes 1572864 | tf_op jit(solution)/shard_map/all_to_all | solution.py:139
  149.2 2.9 %collective-permute-start.28 = (bf16[32,384]{1,0:T(8,128)(2,1)S(1)}, bf16[32,384]{1,0:T(8,128)(2,1)S(1)}, u32[]{:S(2)}, u32[]{:S(2)}) collective-permute-start(bf16[32,384]{1,0:T(8,128)(2,1)S(1)} %bitcast.213), channel_id=1, source_target_pairs={{0,2},{2,0},{1,3},{3,1},{4,6},{6,4},{5,7},{7,5},{8,10},{10,8},{9,1... | collective-permute-start | bytes 73736 | tf_op jit(solution)/shard_map/ppermute | solution.py:25
  152.2 3.0 %all_gather.8 = bf16[64,768]{1,0:T(8,128)(2,1)S(1)} all-gather(bf16[32,768]{1,0:T(8,128)(2,1)S(1)} %reduce_sum.132), channel_id=1, replica_groups=mesh['yl'=2,'x'=4,'z'=8,'yh'=2,'c'=2] {'c'}, dimensions={0}, use_global_device_ids=true | all-gather | bytes 147456 | tf_op jit(solution)/shard_map/all_gather | solution.py:142
  155.2 2.9 %all_gather.7 = bf16[2,2,32,384]{3,2,1,0:T(8,128)(2,1)S(1)} all-gather(bf16[1,2,32,384]{3,2,1,0:T(8,128)(2,1)S(1)} %maximum_select_fusion.5), channel_id=1, replica_groups=mesh['yl'=2,'x'=4,'z'=8,'yh'=2,'c'=2] {'c'}, dimensions={0}, use_global_device_ids=true | all-gather | bytes 147456 | tf_op jit(solution)/shard_map/all_gather | solution.py:148
  158.8 3.3 %all-to-all-done.3 = bf16[16,64,384]{2,1,0:T(8,128)(2,1)} async-done(((bf16[16,64,384]{2,1,0:T(8,128)(2,1)}), bf16[16,64,384]{2,1,0:T(8,128)(2,1)}, u32[]{:S(2)}, u32[]{:S(2)}) %all-to-all-start.3) | async-done | bytes 786464 | tf_op jit(solution)/shard_map/all_to_all | solution.py:139
  162.1 2.6 %fusion.47 = (bf16[768,384]{1,0:T(8,128)(2,1)S(1)}, f32[768,384]{1,0:T(8,128)S(1)}) fusion(bf16[1024,768]{1,0:T(8,128)(2,1)} %bitcast.30, bf16[1024,384]{1,0:T(8,128)(2,1)} %bitcast.76), kind=kOutput, calls=%fused_computation.151 | convolution fusion | flops 604274688 | bytes 4128768 | tf_op jit(solution)/shard_map/dot_general | solution.py:33
  164.7 2.5 %collective-permute-start.29 = (bf16[768,384]{1,0:T(8,128)(2,1)S(1)}, bf16[768,384]{1,0:T(8,128)(2,1)S(1)}, u32[]{:S(2)}, u32[]{:S(2)}) collective-permute-start(bf16[768,384]{1,0:T(8,128)(2,1)S(1)} %get-tuple-element.116), channel_id=1, source_target_pairs={{0,1},{1,0},{2,3},{3,2},{4,5},{5,4},{6,7},{7,6},{8,9},{9,8},{10,11... | collective-permute-start | bytes 1769480 | tf_op jit(solution)/shard_map/ppermute | solution.py:25
  167.2 1.6 collective-permute-done.29
  168.8 1.1 convert_add_fusion
  (119 shorter events, 10.5 us)
Async XLA Ops:
  0.6 15.2 %copy-start = (bf16[128,768]{1,0:T(8,128)(2,1)S(1)}, bf16[128,768]{1,0:T(8,128)(2,1)}, u32[]{:S(2)}) copy-start(bf16[128,768]{1,0:T(8,128)(2,1)} %param.6) | copy-start | bytes 589828
  3.8 7.7 %copy-start.13 = (bf16[64,1024]{1,0:T(8,128)(2,1)S(1)}, bf16[64,1024]{1,0:T(8,128)(2,1)}, u32[]{:S(2)}) copy-start(bf16[64,1024]{1,0:T(8,128)(2,1)} %param.9) | copy-start | bytes 393220
  3.8 8.8 %copy-start.9 = (bf16[768,384]{1,0:T(8,128)(2,1)S(1)}, bf16[768,384]{1,0:T(8,128)(2,1)}, u32[]{:S(2)}) copy-start(bf16[768,384]{1,0:T(8,128)(2,1)} %param.8) | copy-start | bytes 1769476
  3.8 47.4 %all-to-all-start = ((bf16[16,32,1792]{2,1,0:T(8,128)(2,1)}), bf16[16,32,1792]{2,1,0:T(8,128)(2,1)S(1)}, u32[]{:S(2)}, u32[]{:S(2)}) async-start(bf16[16,32,1792]{2,1,0:T(8,128)(2,1)} %broadcast_in_dim.23), calls=%async_computation | async-start | bytes 3670016 | tf_op jit(solution)/shard_map/all_to_all | solution.py:57
  11.6 5.6 %collective-permute-start = (bf16[2,8,1024]{2,1,0:T(8,128)(2,1)S(1)}, bf16[2,8,1024]{2,1,0:T(8,128)(2,1)S(1)}, u32[]{:S(2)}, u32[]{:S(2)}) collective-permute-start(bf16[2,8,1024]{2,1,0:T(8,128)(2,1)S(1)} %get-tuple-element.94), channel_id=1, source_target_pairs={{0,1},{1,0},{2,3},{3,2},{4,5},{5,4},{6,7},{7,6},{8,9},{9,8},{10,11... | collective-permute-start | bytes 98312 | tf_op jit(solution)/shard_map/ppermute | solution.py:25
  12.7 38.6 %collective-permute-start.1 = (bf16[384,384]{1,0:T(8,128)(2,1)S(1)}, bf16[384,384]{1,0:T(8,128)(2,1)S(1)}, u32[]{:S(2)}, u32[]{:S(2)}) collective-permute-start(bf16[384,384]{1,0:T(8,128)(2,1)S(1)} %dynamic-slice_bitcast_fusion), channel_id=1, source_target_pairs={{0,2},{2,0},{1,3},{3,1},{4,6},{6,4},{5,7},{7,5},{8,10},{10,8},{9,1... | collective-permute-start | bytes 884744 | tf_op jit(solution)/shard_map/ppermute | solution.py:25
  18.9 9.2 %collective-permute-start.2 = (bf16[32,1792]{1,0:T(8,128)(2,1)}, bf16[32,1792]{1,0:T(8,128)(2,1)}, u32[]{:S(2)}, u32[]{:S(2)}) collective-permute-start(bf16[32,1792]{1,0:T(8,128)(2,1)} %bitcast.13), channel_id=1, source_target_pairs={{0,4},{4,8},{8,12},{12,16},{16,20},{20,24},{24,28},{28,0},{1,5},{5... | collective-permute-start | bytes 344072 | tf_op jit(solution)/shard_map/ppermute | solution.py:29
  20.5 11.6 %collective-permute-start.3 = (bf16[32,1792]{1,0:T(8,128)(2,1)}, bf16[32,1792]{1,0:T(8,128)(2,1)}, u32[]{:S(2)}, u32[]{:S(2)}) collective-permute-start(bf16[32,1792]{1,0:T(8,128)(2,1)} %bitcast.13), channel_id=1, source_target_pairs={{0,8},{4,12},{8,16},{12,20},{16,24},{20,28},{24,0},{28,4},{1,9},{5... | collective-permute-start | bytes 344072 | tf_op jit(solution)/shard_map/ppermute | solution.py:29
  23.5 19.3 %collective-permute-start.4 = (bf16[32,1792]{1,0:T(8,128)(2,1)}, bf16[32,1792]{1,0:T(8,128)(2,1)}, u32[]{:S(2)}, u32[]{:S(2)}) collective-permute-start(bf16[32,1792]{1,0:T(8,128)(2,1)} %bitcast.13), channel_id=1, source_target_pairs={{0,12},{4,16},{8,20},{12,24},{16,28},{20,0},{24,4},{28,8},{1,13},{... | collective-permute-start | bytes 344072 | tf_op jit(solution)/shard_map/ppermute | solution.py:29
  27.3 15.5 %collective-permute-start.5 = (bf16[32,1792]{1,0:T(8,128)(2,1)}, bf16[32,1792]{1,0:T(8,128)(2,1)}, u32[]{:S(2)}, u32[]{:S(2)}) collective-permute-start(bf16[32,1792]{1,0:T(8,128)(2,1)} %bitcast.13), channel_id=1, source_target_pairs={{0,16},{4,20},{8,24},{12,28},{16,0},{20,4},{24,8},{28,12},{1,17},{... | collective-permute-start | bytes 344072 | tf_op jit(solution)/shard_map/ppermute | solution.py:29
  28.0 14.8 %collective-permute-start.6 = (bf16[32,1792]{1,0:T(8,128)(2,1)}, bf16[32,1792]{1,0:T(8,128)(2,1)}, u32[]{:S(2)}, u32[]{:S(2)}) collective-permute-start(bf16[32,1792]{1,0:T(8,128)(2,1)} %bitcast.13), channel_id=1, source_target_pairs={{0,20},{4,24},{8,28},{12,0},{16,4},{20,8},{24,12},{28,16},{1,21},{... | collective-permute-start | bytes 344072 | tf_op jit(solution)/shard_map/ppermute | solution.py:29
  32.2 18.0 %collective-permute-start.7 = (bf16[32,1792]{1,0:T(8,128)(2,1)}, bf16[32,1792]{1,0:T(8,128)(2,1)}, u32[]{:S(2)}, u32[]{:S(2)}) collective-permute-start(bf16[32,1792]{1,0:T(8,128)(2,1)} %bitcast.13), channel_id=1, source_target_pairs={{0,24},{4,28},{8,0},{12,4},{16,8},{20,12},{24,16},{28,20},{1,25},{... | collective-permute-start | bytes 344072 | tf_op jit(solution)/shard_map/ppermute | solution.py:29
  42.8 8.4 %collective-permute-start.8 = (bf16[32,1792]{1,0:T(8,128)(2,1)}, bf16[32,1792]{1,0:T(8,128)(2,1)}, u32[]{:S(2)}, u32[]{:S(2)}) collective-permute-start(bf16[32,1792]{1,0:T(8,128)(2,1)} %bitcast.13), channel_id=1, source_target_pairs={{0,28},{4,0},{8,4},{12,8},{16,12},{20,16},{24,20},{28,24},{1,29},{... | collective-permute-start | bytes 344072 | tf_op jit(solution)/shard_map/ppermute | solution.py:29
  57.6 10.1 %copy-start.6 = (bf16[8,32,1792]{2,1,0:T(8,128)(2,1)}, bf16[8,32,1792]{2,1,0:T(8,128)(2,1)S(1)}, u32[]{:S(2)}) copy-start(bf16[8,32,1792]{2,1,0:T(8,128)(2,1)S(1)} %bitcast_dynamic-update-slice_fusion) | copy-start | bytes 2752516
  57.7 7.5 %collective-permute-start.10 = (bf16[256,1792]{1,0:T(8,128)(2,1)S(1)}, bf16[256,1792]{1,0:T(8,128)(2,1)}, u32[]{:S(2)}, u32[]{:S(2)}) collective-permute-start(bf16[256,1792]{1,0:T(8,128)(2,1)S(1)} %bitcast.199), channel_id=1, source_target_pairs={{0,1},{1,0},{2,3},{3,2},{4,5},{5,4},{6,7},{7,6},{8,9},{9,8},{10,11... | collective-permute-start | bytes 2752520 | tf_op jit(solution)/shard_map/ppermute | solution.py:25
  58.8 6.2 %collective-permute-start.9 = (bf16[384,384]{1,0:T(8,128)(2,1)S(1)}, bf16[384,384]{1,0:T(8,128)(2,1)S(1)}, u32[]{:S(2)}, u32[]{:S(2)}) collective-permute-start(bf16[384,384]{1,0:T(8,128)(2,1)S(1)} %collective-permute-done.1), channel_id=1, source_target_pairs={{0,1},{1,0},{2,3},{3,2},{4,5},{5,4},{6,7},{7,6},{8,9},{9,8},{10,11... | collective-permute-start | bytes 884744 | tf_op jit(solution)/shard_map/ppermute | solution.py:25
  60.2 28.9 %all-to-all-start.1 = ((bf16[16,64,768]{2,1,0:T(8,128)(2,1)}), bf16[16,64,768]{2,1,0:T(8,128)(2,1)}, u32[]{:S(2)}, u32[]{:S(2)}) async-start(bf16[16,64,768]{2,1,0:T(8,128)(2,1)} %broadcast_in_dim.61), calls=%async_computation.1 | async-start | bytes 3145728 | tf_op jit(solution)/shard_map/all_to_all | solution.py:17
  65.1 2.5 %copy-start.7 = (bf16[768,384]{1,0:T(8,128)(2,1)}, bf16[768,384]{1,0:T(8,128)(2,1)S(1)}, u32[]{:S(2)}) copy-start(bf16[768,384]{1,0:T(8,128)(2,1)S(1)} %maximum_select_fusion.1) | copy-start | bytes 1769476
  67.7 2.2 %copy-start.1 = (f32[512,768]{1,0:T(8,128)}, f32[512,768]{1,0:T(8,128)S(1)}, u32[]{:S(2)}) copy-start(f32[512,768]{1,0:T(8,128)S(1)} %get-tuple-element.110) | copy-start | bytes 4718596
  69.9 1.0 copy-start.5
  71.3 9.8 %collective-permute-start.11 = (f32[8,512]{1,0:T(8,128)S(1)}, f32[8,512]{1,0:T(8,128)S(1)}, u32[]{:S(2)}, u32[]{:S(2)}) collective-permute-start(f32[8,512]{1,0:T(8,128)S(1)} %stack.123), channel_id=1, source_target_pairs={{0,4},{4,8},{8,12},{12,16},{16,20},{20,24},{24,28},{28,0},{1,5},{5... | collective-permute-start | bytes 49160 | tf_op jit(solution)/shard_map/ppermute | solution.py:29
  73.4 9.8 %collective-permute-start.12 = (f32[8,512]{1,0:T(8,128)S(1)}, f32[8,512]{1,0:T(8,128)S(1)}, u32[]{:S(2)}, u32[]{:S(2)}) collective-permute-start(f32[8,512]{1,0:T(8,128)S(1)} %stack.123), channel_id=1, source_target_pairs={{0,8},{4,12},{8,16},{12,20},{16,24},{20,28},{24,0},{28,4},{1,9},{5... | collective-permute-start | bytes 49160 | tf_op jit(solution)/shard_map/ppermute | solution.py:29
  74.3 9.3 %collective-permute-start.13 = (f32[8,512]{1,0:T(8,128)S(1)}, f32[8,512]{1,0:T(8,128)S(1)}, u32[]{:S(2)}, u32[]{:S(2)}) collective-permute-start(f32[8,512]{1,0:T(8,128)S(1)} %stack.123), channel_id=1, source_target_pairs={{0,12},{4,16},{8,20},{12,24},{16,28},{20,0},{24,4},{28,8},{1,13},{... | collective-permute-start | bytes 49160 | tf_op jit(solution)/shard_map/ppermute | solution.py:29
  76.9 7.1 %collective-permute-start.14 = (f32[8,512]{1,0:T(8,128)S(1)}, f32[8,512]{1,0:T(8,128)S(1)}, u32[]{:S(2)}, u32[]{:S(2)}) collective-permute-start(f32[8,512]{1,0:T(8,128)S(1)} %stack.123), channel_id=1, source_target_pairs={{0,16},{4,20},{8,24},{12,28},{16,0},{20,4},{24,8},{28,12},{1,17},{... | collective-permute-start | bytes 49160 | tf_op jit(solution)/shard_map/ppermute | solution.py:29
  79.1 4.8 %collective-permute-start.15 = (f32[8,512]{1,0:T(8,128)S(1)}, f32[8,512]{1,0:T(8,128)S(1)}, u32[]{:S(2)}, u32[]{:S(2)}) collective-permute-start(f32[8,512]{1,0:T(8,128)S(1)} %stack.123), channel_id=1, source_target_pairs={{0,20},{4,24},{8,28},{12,0},{16,4},{20,8},{24,12},{28,16},{1,21},{... | collective-permute-start | bytes 49160 | tf_op jit(solution)/shard_map/ppermute | solution.py:29
  81.2 4.3 %collective-permute-start.16 = (f32[8,512]{1,0:T(8,128)S(1)}, f32[8,512]{1,0:T(8,128)S(1)}, u32[]{:S(2)}, u32[]{:S(2)}) collective-permute-start(f32[8,512]{1,0:T(8,128)S(1)} %stack.123), channel_id=1, source_target_pairs={{0,24},{4,28},{8,0},{12,4},{16,8},{20,12},{24,16},{28,20},{1,25},{... | collective-permute-start | bytes 49160 | tf_op jit(solution)/shard_map/ppermute | solution.py:29
  83.2 3.2 %collective-permute-start.17 = (f32[8,512]{1,0:T(8,128)S(1)}, f32[8,512]{1,0:T(8,128)S(1)}, u32[]{:S(2)}, u32[]{:S(2)}) collective-permute-start(f32[8,512]{1,0:T(8,128)S(1)} %stack.123), channel_id=1, source_target_pairs={{0,28},{4,0},{8,4},{12,8},{16,12},{20,16},{24,20},{28,24},{1,29},{... | collective-permute-start | bytes 49160 | tf_op jit(solution)/shard_map/ppermute | solution.py:29
  89.3 2.7 %collective-permute-start.18 = (f32[8,512]{1,0:T(8,128)S(1)}, f32[8,512]{1,0:T(8,128)S(1)}, u32[]{:S(2)}, u32[]{:S(2)}) collective-permute-start(f32[8,512]{1,0:T(8,128)S(1)} %stack.138), channel_id=1, source_target_pairs={{0,1},{1,0},{2,3},{3,2},{4,5},{5,4},{6,7},{7,6},{8,9},{9,8},{10,11... | collective-permute-start | bytes 49160 | tf_op jit(solution)/shard_map/ppermute | solution.py:25
  93.6 2.3 %copy-start.2 = (f32[512,768]{1,0:T(8,128)S(1)}, f32[512,768]{1,0:T(8,128)}, u32[]{:S(2)}) copy-start(f32[512,768]{1,0:T(8,128)} %copy-done.1) | copy-start | bytes 4718596
  94.2 1.2 copy-start.3
  95.4 7.5 %copy-start.4 = (f32[512,768]{1,0:T(8,128)S(1)}, f32[512,768]{1,0:T(8,128)}, u32[]{:S(2)}) copy-start(f32[512,768]{1,0:T(8,128)} %copy-done.3) | copy-start | bytes 4718596
  95.4 7.5 %collective-permute-start.19 = (bf16[256,768]{1,0:T(8,128)(2,1)S(1)}, bf16[256,768]{1,0:T(8,128)(2,1)}, u32[]{:S(2)}, u32[]{:S(2)}) collective-permute-start(bf16[256,768]{1,0:T(8,128)(2,1)S(1)} %slice.181), channel_id=1, source_target_pairs={{0,1},{1,0},{2,3},{3,2},{4,5},{5,4},{6,7},{7,6},{8,9},{9,8},{10,11... | collective-permute-start | bytes 1179656 | tf_op jit(solution)/shard_map/ppermute | solution.py:25
  97.4 41.5 %all-to-all-start.2 = ((bf16[16,32,768]{2,1,0:T(8,128)(2,1)}), bf16[16,32,768]{2,1,0:T(8,128)(2,1)S(1)}, u32[]{:S(2)}, u32[]{:S(2)}) async-start(bf16[16,32,768]{2,1,0:T(8,128)(2,1)} %bitcast.196), calls=%async_computation.2 | async-start | bytes 1572864 | tf_op jit(solution)/shard_map/all_to_all | solution.py:123
  104.3 36.1 %copy-start.8 = (bf16[768,384]{1,0:T(8,128)(2,1)S(1)}, bf16[768,384]{1,0:T(8,128)(2,1)}, u32[]{:S(2)}) copy-start(bf16[768,384]{1,0:T(8,128)(2,1)} %copy-done.7) | copy-start | bytes 1769476
  104.3 36.1 %copy-start.10 = (bf16[768,384]{1,0:T(8,128)(2,1)S(1)}, bf16[768,384]{1,0:T(8,128)(2,1)}, u32[]{:S(2)}) copy-start(bf16[768,384]{1,0:T(8,128)(2,1)} %param.8) | copy-start | bytes 1769476
  104.4 12.5 %collective-permute-start.20 = (bf16[88,768]{1,0:T(8,128)(2,1)S(1)}, bf16[88,768]{1,0:T(8,128)(2,1)S(1)}, u32[]{:S(2)}, u32[]{:S(2)}) collective-permute-start(bf16[88,768]{1,0:T(8,128)(2,1)S(1)} %get-tuple-element.96), channel_id=1, source_target_pairs={{0,4},{4,8},{8,12},{12,16},{16,20},{20,24},{24,28},{28,0},{1,5},{5... | collective-permute-start | bytes 405512 | tf_op jit(solution)/shard_map/ppermute | solution.py:120
  106.2 13.1 %collective-permute-start.21 = (bf16[88,768]{1,0:T(8,128)(2,1)S(1)}, bf16[88,768]{1,0:T(8,128)(2,1)S(1)}, u32[]{:S(2)}, u32[]{:S(2)}) collective-permute-start(bf16[88,768]{1,0:T(8,128)(2,1)S(1)} %get-tuple-element.97), channel_id=1, source_target_pairs={{0,8},{4,12},{8,16},{12,20},{16,24},{20,28},{24,0},{28,4},{1,9},{5... | collective-permute-start | bytes 405512 | tf_op jit(solution)/shard_map/ppermute | solution.py:120
  107.1 8.2 %collective-permute-start.27 = (f32[4,2,8]{2,0,1:T(4,128)S(1)}, f32[4,2,8]{2,0,1:T(4,128)S(1)}, u32[]{:S(2)}, u32[]{:S(2)}) collective-permute-start(f32[4,2,8]{2,0,1:T(4,128)S(1)} %fusion.28), channel_id=1, source_target_pairs={{0,2},{2,0},{1,3},{3,1},{4,6},{6,4},{5,7},{7,5},{8,10},{10,8},{9,1... | collective-permute-start | bytes 776 | tf_op jit(solution)/shard_map/ppermute | solution.py:25
  110.1 13.2 %collective-permute-start.22 = (bf16[88,768]{1,0:T(8,128)(2,1)S(1)}, bf16[88,768]{1,0:T(8,128)(2,1)S(1)}, u32[]{:S(2)}, u32[]{:S(2)}) collective-permute-start(bf16[88,768]{1,0:T(8,128)(2,1)S(1)} %get-tuple-element.98), channel_id=1, source_target_pairs={{0,12},{4,16},{8,20},{12,24},{16,28},{20,0},{24,4},{28,8},{1,13},{... | collective-permute-start | bytes 405512 | tf_op jit(solution)/shard_map/ppermute | solution.py:120
  112.6 17.0 %collective-permute-start.23 = (bf16[88,768]{1,0:T(8,128)(2,1)S(1)}, bf16[88,768]{1,0:T(8,128)(2,1)}, u32[]{:S(2)}, u32[]{:S(2)}) collective-permute-start(bf16[88,768]{1,0:T(8,128)(2,1)S(1)} %get-tuple-element.99), channel_id=1, source_target_pairs={{0,16},{4,20},{8,24},{12,28},{16,0},{20,4},{24,8},{28,12},{1,17},{... | collective-permute-start | bytes 405512 | tf_op jit(solution)/shard_map/ppermute | solution.py:120
  115.3 14.3 %collective-permute-start.24 = (bf16[88,768]{1,0:T(8,128)(2,1)S(1)}, bf16[88,768]{1,0:T(8,128)(2,1)}, u32[]{:S(2)}, u32[]{:S(2)}) collective-permute-start(bf16[88,768]{1,0:T(8,128)(2,1)S(1)} %get-tuple-element.100), channel_id=1, source_target_pairs={{0,20},{4,24},{8,28},{12,0},{16,4},{20,8},{24,12},{28,16},{1,21},{... | collective-permute-start | bytes 405512 | tf_op jit(solution)/shard_map/ppermute | solution.py:120
  116.9 21.5 %collective-permute-start.25 = (bf16[88,768]{1,0:T(8,128)(2,1)S(1)}, bf16[88,768]{1,0:T(8,128)(2,1)}, u32[]{:S(2)}, u32[]{:S(2)}) collective-permute-start(bf16[88,768]{1,0:T(8,128)(2,1)S(1)} %get-tuple-element.101), channel_id=1, source_target_pairs={{0,24},{4,28},{8,0},{12,4},{16,8},{20,12},{24,16},{28,20},{1,25},{... | collective-permute-start | bytes 405512 | tf_op jit(solution)/shard_map/ppermute | solution.py:120
  119.3 19.7 %copy-start.11 = (bf16[88,768]{1,0:T(8,128)(2,1)}, bf16[88,768]{1,0:T(8,128)(2,1)S(1)}, u32[]{:S(2)}) copy-start(bf16[88,768]{1,0:T(8,128)(2,1)S(1)} %collective-permute-done.21) | copy-start | bytes 405508
  119.3 19.7 %collective-permute-start.26 = (bf16[88,768]{1,0:T(8,128)(2,1)S(1)}, bf16[88,768]{1,0:T(8,128)(2,1)}, u32[]{:S(2)}, u32[]{:S(2)}) collective-permute-start(bf16[88,768]{1,0:T(8,128)(2,1)S(1)} %get-tuple-element.95), channel_id=1, source_target_pairs={{0,28},{4,0},{8,4},{12,8},{16,12},{20,16},{24,20},{28,24},{1,29},{... | collective-permute-start | bytes 405512 | tf_op jit(solution)/shard_map/ppermute | solution.py:120
  123.3 15.6 %copy-start.12 = (bf16[88,768]{1,0:T(8,128)(2,1)}, bf16[88,768]{1,0:T(8,128)(2,1)S(1)}, u32[]{:S(2)}) copy-start(bf16[88,768]{1,0:T(8,128)(2,1)S(1)} %collective-permute-done.22) | copy-start | bytes 405508
  143.0 19.1 %all-to-all-start.3 = ((bf16[16,64,384]{2,1,0:T(8,128)(2,1)}), bf16[16,64,384]{2,1,0:T(8,128)(2,1)}, u32[]{:S(2)}, u32[]{:S(2)}) async-start(bf16[16,64,384]{2,1,0:T(8,128)(2,1)} %bitcast.63), calls=%async_computation.3 | async-start | bytes 1572864 | tf_op jit(solution)/shard_map/all_to_all | solution.py:139
  149.2 6.1 %collective-permute-start.28 = (bf16[32,384]{1,0:T(8,128)(2,1)S(1)}, bf16[32,384]{1,0:T(8,128)(2,1)S(1)}, u32[]{:S(2)}, u32[]{:S(2)}) collective-permute-start(bf16[32,384]{1,0:T(8,128)(2,1)S(1)} %bitcast.213), channel_id=1, source_target_pairs={{0,2},{2,0},{1,3},{3,1},{4,6},{6,4},{5,7},{7,5},{8,10},{10,8},{9,1... | collective-permute-start | bytes 73736 | tf_op jit(solution)/shard_map/ppermute | solution.py:25
  164.7 4.1 %collective-permute-start.29 = (bf16[768,384]{1,0:T(8,128)(2,1)S(1)}, bf16[768,384]{1,0:T(8,128)(2,1)S(1)}, u32[]{:S(2)}, u32[]{:S(2)}) collective-permute-start(bf16[768,384]{1,0:T(8,128)(2,1)S(1)} %get-tuple-element.116), channel_id=1, source_target_pairs={{0,1},{1,0},{2,3},{3,2},{4,5},{5,4},{6,7},{7,6},{8,9},{9,8},{10,11... | collective-permute-start | bytes 1769480 | tf_op jit(solution)/shard_map/ppermute | solution.py:25

commit v2 on v1

v2 whole, which is shorter than its diff:
```python
import math

import jax
import jax.numpy as jnp
from jax import lax
from jax.experimental import pallas as pl
from jax.experimental.pallas import tpu as pltpu
from jax.sharding import Mesh, PartitionSpec as P

epsilon = 1e-06
loss_scale = 8.0

COLS = ("x", "yl", "yh")
bf16, f32 = jnp.bfloat16, jnp.float32


def to_all(value, axes, count):
    sent = jnp.broadcast_to(value[None], (count, *value.shape))
    return lax.all_to_all(sent, axes, 0, 0, tiled=True)


def pick(value, index, axis):
    return lax.dynamic_index_in_dim(value, index, axis, keepdims=False)


def swap(value, axis):
    return lax.ppermute(value, axis, [(0, 1), (1, 0)])


def turn(value, k):
    pairs = [(2 * i, 2 * ((i + k) % 8)) for i in range(8)]
    pairs += [(2 * i + 1, 2 * ((i - k) % 8) + 1) for i in range(8)]
    return lax.ppermute(value, ("z", "c"), pairs)


def in_order(here, core, whole, halves):
    order = sorted(whole)
    rows, width = halves[0].shape

    def kernel(here_ref, core_ref, *refs):
        out_ref, here, core = refs[-1], here_ref[0], core_ref[0]
        sign = 1 - 2 * core
        for place, ref in zip(order, refs):
            z = (here + sign * place + 8) % 8
            for i in range(2):
                first = pl.multiple_of((core + i) % 2 * rows, rows)
                out_ref[i, z] = ref[pl.ds(first, rows), :]
        for i in range(2):
            out_ref[i, (here + 4) % 8] = refs[len(order) + i][...]

    blocks = [whole[place] for place in order] + list(halves)
    return pl.pallas_call(
        kernel,
        out_shape=jax.ShapeDtypeStruct((2, 8, rows, width), halves[0].dtype),
        in_specs=[pl.BlockSpec(memory_space=pltpu.SMEM)] * 2
        + [pl.BlockSpec(memory_space=pltpu.VMEM)] * len(blocks),
        out_specs=pl.BlockSpec(memory_space=pltpu.VMEM),
        compiler_params=pltpu.CompilerParams(vmem_limit_bytes=16 * 2**20),
    )(here.reshape(1).astype(jnp.int32), core.reshape(1).astype(jnp.int32), *blocks)


def copies(core, text, teach, count):
    rows, width, wide = teach.shape[0], text.shape[1], teach.shape[1]

    def kernel(core_ref, text_ref, teach_ref, out_ref):
        first = pl.multiple_of(core_ref[0] * rows, rows)
        text, teach = text_ref[pl.ds(first, rows), :], teach_ref[...]
        for i in range(count):
            out_ref[i, :, :width] = text
            out_ref[i, :, width:] = teach

    return pl.pallas_call(
        kernel,
        out_shape=jax.ShapeDtypeStruct((count, rows, width + wide), text.dtype),
        in_specs=[
            pl.BlockSpec(memory_space=pltpu.SMEM),
            pl.BlockSpec(memory_space=pltpu.VMEM),
            pl.BlockSpec(memory_space=pltpu.VMEM),
        ],
        out_specs=pl.BlockSpec(memory_space=pltpu.VMEM),
        compiler_params=pltpu.CompilerParams(vmem_limit_bytes=16 * 2**20),
    )(core.reshape(1).astype(jnp.int32), text, teach)


def dot(left, right, left_dim, right_dim):
    return lax.dot_general(
        left, right, (((left_dim,), (right_dim,)), ((), ())), preferred_element_type=f32
    )


def shards(image_feats, student_text, student_head, teacher_image, teacher_text, group_index):
    core, high, here = lax.axis_index("c"), lax.axis_index("yh"), lax.axis_index("z")
    width, wide = student_head.shape[0], teacher_image.shape[1]
    half = width // 2
    student_scale, teacher_scale = 3.0 / math.sqrt(width), 3.0 / math.sqrt(wide)
    group = group_index[0]

    def block_first(value):
        return lax.dynamic_slice_in_dim(jnp.concatenate([value, value], 0), group, 4, 0)


    teach = pick(teacher_image.reshape(2, 2, 16, wide), high, 1)
    come = swap(teach, "c")
    teach = jnp.where(core == 0, jnp.stack([teach, come]), jnp.stack([come, teach])).reshape(4, 2, 8, wide)
    feats = pick(image_feats.reshape(4, 2, 2, 8, width), high, 1)
    own = block_first(jnp.concatenate([feats, teach], 3))
    own = own.transpose(1, 0, 2, 3).reshape(64, width + wide)
    sent = copies(core, student_text, teacher_text, 16)
    head_come = pick(student_head.reshape(2, half, half), core, 0)
    head_come = lax.ppermute(head_come, ("yl", "yh"), [(i, 3 - i) for i in range(4)])
    sent, head_come = lax.optimization_barrier((sent, head_come))
    cols = lax.all_to_all(sent, COLS, 0, 0, tiled=True)
    near = {k: turn(own, k) for k in (3, 1, 2)}
    far = turn(pick(near[3].reshape(2, 32, width + wide), core, 0), 1)
    head_pair = swap(head_come, "c")
    opposite = {k: swap(near[k], "c") for k in (3, 1, 2)}
    beyond = swap(far, "c")
    cols, head_pair, near, opposite, far, beyond = lax.optimization_barrier(
        (cols, head_pair, near, opposite, far, beyond)
    )
    cols = cols.reshape(512, width + wide)
    whole = {0: own} | {-k: near[k] for k in near} | {k: opposite[k] for k in opposite}
    rows = in_order(here, core, whole, (far, beyond)).reshape(512, width + wide)
    head_other = jnp.where(
        core == 0, jnp.concatenate([head_come, head_pair], 0), jnp.concatenate([head_pair, head_come], 0)
    )
    head = jnp.where(
        high == 0,
        jnp.concatenate([student_head, head_other], 1),
        jnp.concatenate([head_other, student_head], 1),
    )
    text, teach = cols[:, :width], cols[:, width:]

    projected = dot(rows[:, :width], head, 1, 0)
    factor = lax.rsqrt(jnp.sum(projected * projected, axis=1, keepdims=True) / width + epsilon)
    queries = (projected * factor).astype(bf16)
    student = student_scale * dot(text, queries, 1, 1)
    teacher = teacher_scale * dot(teach, rows[:, width:], 1, 1)
    top_t = jnp.max(teacher, axis=0)
    weights = jnp.exp(teacher - top_t)
    total_t = jnp.sum(weights, axis=0)
    cross = jnp.sum(weights * (teacher - student), axis=0)
    top_s = jnp.max(student, axis=0)
    total_s = jnp.sum(jnp.exp(student - top_s), axis=0)
    zero = jnp.zeros_like(top_t)

    def merged(stats):
        tops_t, totals_t, crosses, tops_s, totals_s = (stats[:, i] for i in range(5))
        high_t, high_s = jnp.max(tops_t, axis=0), jnp.max(tops_s, axis=0)
        shift_t = jnp.exp(tops_t - high_t)
        sum_t = jnp.sum(totals_t * shift_t, axis=0)
        sum_s = jnp.sum(totals_s * jnp.exp(tops_s - high_s), axis=0)
        sum_cross = jnp.sum(crosses * shift_t, axis=0)
        return jnp.stack([high_t, sum_t, sum_cross, high_s, sum_s, zero, zero, zero])

    stats = jnp.stack([top_t, total_t, cross, top_s, total_s, zero, zero, zero])
    stats = merged(to_all(stats, "z", 8))
    come = swap(stats, "c")
    come = jnp.concatenate([come[:, 256:], come[:, :256]], 1)
    high_t, sum_t, sum_cross, high_s, sum_s = merged(jnp.stack([stats, come]))[:5]
    lse_t, lse_s = high_t + jnp.log(sum_t), high_s + jnp.log(sum_s)
    losses = sum_cross / sum_t - lse_t + lse_s

    slope = (loss_scale * (jnp.exp(student - lse_s) - jnp.exp(teacher - lse_t))).astype(bf16)
    grad = student_scale * dot(slope, text, 0, 0)
    text_part = (student_scale * dot(slope, queries, 1, 0)).astype(bf16)

    def blocks(value):
        return value.reshape(2, 8, 32, value.shape[1])[:, :, :8].reshape(128, value.shape[1])

    block_grad, block_proj, block_factor = blocks(grad), blocks(projected), blocks(factor)
    inner = jnp.sum(block_grad * block_proj, axis=1, keepdims=True)
    head_slope = (
        block_factor * block_grad
        - block_factor * block_factor * block_factor * block_proj * inner / width
    ).astype(bf16)
    share = dot(blocks(rows[:, :width]), head_slope, 0, 0).reshape(2, half, width)
    share = pick(share, core, 0) + swap(pick(share, 1 - core, 0).astype(bf16), "c").astype(f32)
    share = share.astype(bf16).reshape(16, 24, width)

    grad = grad[:256] + swap(grad[256:].astype(bf16), "c").astype(f32)
    grad = grad.astype(bf16).reshape(8, 32, width)
    turned = lax.dynamic_slice_in_dim(jnp.concatenate([grad, grad], 0), here, 8, 0)
    round_z = [
        lax.ppermute(turned[k], "z", [(i, (i + k) % 8) for i in range(8)]) for k in range(1, 8)
    ]
    sent = jnp.concatenate([text_part.reshape(16, 32, width), share], 1)
    sent = lax.all_to_all(sent, COLS, 0, 0, tiled=True)
    sent, losses, *round_z = lax.optimization_barrier((sent, losses, *round_z))
    grad = turned[0].astype(f32) + sum(r.astype(f32) for r in round_z)
    share = jnp.sum(sent[:, 32:].astype(f32), axis=0).astype(bf16)
    share = to_all(share, "z", 8)

    def back(value):
        return lax.dynamic_slice_in_dim(jnp.concatenate([value, value], 0), 4 - group, 4, 0)

    text_sum = jnp.sum(sent[:, :32].astype(f32), axis=0).astype(bf16)
    text_grad = lax.all_gather(text_sum, "c", axis=0, tiled=True)
    halves = back(grad.astype(bf16).reshape(4, 8, width)).reshape(32, 2, half)
    grad_come = swap(pick(halves, 1 - high, 1), "yh")
    losses = pick(losses.reshape(2, 8, 4, 8), here, 1)
    losses = jnp.where(core == 0, losses, losses[::-1])
    losses = back(losses.transpose(1, 0, 2))
    losses_come = swap(losses, "yh")
    share, text_grad, grad_come, losses_come = lax.optimization_barrier(
        (share, text_grad, grad_come, losses_come)
    )

    share = jnp.sum(share.astype(f32), axis=0).astype(bf16)
    share = share.reshape(24, 2, half).transpose(1, 0, 2)
    share = jnp.broadcast_to(share[None], (8, 2, 24, half)).reshape(16, 24, half)
    share = lax.all_to_all(share, COLS, 0, 0, tiled=True).reshape(half, half)

    mine = pick(halves, high, 1)
    pair = jnp.where(high == 0, jnp.stack([mine, grad_come]), jnp.stack([grad_come, mine]))
    pair = lax.all_gather(pair, "c", axis=0)
    image_grad = pair.reshape(2, 2, 4, 8, half).transpose(2, 1, 0, 3, 4).reshape(128, half)
    row_loss = jnp.where(
        high == 0, jnp.stack([losses, losses_come], 1), jnp.stack([losses_come, losses], 1)
    ).reshape(128)
    share, row_loss, image_grad = lax.optimization_barrier((share, row_loss, image_grad))
    weight_grad = lax.all_gather(share, "c", axis=0, tiled=True).astype(f32)
    return row_loss, image_grad, text_grad, weight_grad


def solution(mesh):
    mesh = Mesh(mesh.devices.reshape(2, 4, 8, 2, 2), ("yl", "x", "z", "yh", "c"))
    dp = ("yl", "x", "z")
    in_specs = (
        P(dp, None),
        P((*dp, "yh"), None),
        P(None, "yh"),
        P((*dp, "c"), None),
        P((*dp, "yh", "c"), None),
        P(dp),
    )
    out_specs = (P(dp), P(dp, "yh"), P((*dp, "yh"), None), P(None, "yh"))
    return jax.shard_map(shards, mesh=mesh, in_specs=in_specs, out_specs=out_specs, check_vma=False)
```

time: 172 us -> 149 us (0.87)
  starting transfers between devices: 80.7 us -> 66.7 us
  blocking collectives: 5.89 us -> 15.6 us
  waiting for transfers between devices: 45.9 us -> 36.9 us
  local copies, waits for them, and re-layouts: 15.6 us -> 10 us
  matrix products: 11.6 us -> 8.34 us
  other arithmetic: 8.91 us -> 7.08 us
    ppermute x21 -> x12, starting transfers between devices: 40.9 us -> 21.2 us  [the longest x7 9.42 us: shards(): lax.ppermute(turned[k], 'z', [(i, (i + k) % 8) for i in range(8)])]
    ppermute x21 -> x12, waiting for transfers between devices: 37.4 us -> 20.9 us  [the longest x4 10.3 us: turn(): return lax.ppermute(value, ('z', 'c'), pairs)]
    all_to_all x1 -> x2, waiting for transfers between devices: 2.71 us -> 9.32 us  [to_all(): return lax.all_to_all(sent, axes, 0, 0, tiled=True)]
    dynamic_update_slice x7 -> x0, local copies, waits for them, and re-layouts: 6.39 us -> none  [shards(): lax.dynamic_update_slice_in_dim(rows_own, block[None], (here - k) % 8, 0)]
    all_gather x0 -> x1, blocking collectives: none -> 6.17 us  [shards(): weight_grad = lax.all_gather(share, 'c', axis=0, tiled=True).astype(f32)]
    all_to_all x1 -> x2, starting transfers between devices: 4.73 us -> 9.77 us  [to_all(): return lax.all_to_all(sent, axes, 0, 0, tiled=True)]
    dot_general x7 -> x6, matrix products: 11.6 us -> 8.34 us  [dot(): lax.dot_general(left, right, (((left_dim,), (right_dim,)), ((), ())), pre...]
    unnamed x38 -> x27, local copies, waits for them, and re-layouts: 2.13 us -> 4.73 us
  transfers between devices with their start and end apart: 34 -> 28, of which waited for: 15 -> 17; matrix products, arithmetic and copies ran while one was open for 8% -> 3% of each run, Pallas kernels for 0% -> 1%
where the time goes in v2:
time: 149 us; the launch traced here: 148 us
  starting transfers between devices  66.7 us (45%)
  waiting for transfers between devices  36.9 us (25%)
  blocking collectives  15.6 us (10%)
  local copies, waits for them, and re-layouts  10 us (7%)
  matrix products  8.34 us (6%)
  other arithmetic  7.08 us (5%)
  between operations  1.8 us (1%)
  Pallas kernels  1.63 us (1%)
    ppermute x11, starting transfers between devices, swap(): return lax.ppermute(value, axis, [(0, 1), (1, 0)])  16.9 us
    ppermute x4, waiting for transfers between devices, turn(): return lax.ppermute(value, ('z', 'c'), pairs)  10.3 us
    all_to_all x2, starting transfers between devices, to_all(): return lax.all_to_all(sent, axes, 0, 0, tiled=True)  9.77 us
    ppermute x7, starting transfers between devices, shards(): lax.ppermute(turned[k], 'z', [(i, (i + k) % 8) for i in range(8)])  9.42 us
    all_to_all x2, waiting for transfers between devices, to_all(): return lax.all_to_all(sent, axes, 0, 0, tiled=True)  9.32 us
    dot_general x6, matrix products, dot(): lax.dot_general(left, right, (((left_dim,), (right_dim,)), ((), ())), pre...  8.34 us
    ppermute x4, starting transfers between devices, turn(): return lax.ppermute(value, ('z', 'c'), pairs)  8.11 us
    ppermute x7, waiting for transfers between devices, shards(): lax.ppermute(turned[k], 'z', [(i, (i + k) % 8) for i in range(8)])  8.07 us
  transfers between devices with their start and end apart: 28, of which 17 were waited for; matrix products, arithmetic and copies ran while one was open for 3% of the time, Pallas kernels for 1%

profile of v2, /device:TPU:1, one launch (start us, length us, event | category | flops | bytes accessed | tf_op | source)
XLA Modules:
  0.0 148.1 jit_solution(843861186650227877)
XLA Ops:
  0.7 1.0 dynamic-slice_bitcast_fusion
  1.7 3.7 %collective-permute-start = (bf16[384,384]{1,0:T(8,128)(2,1)S(1)}, bf16[384,384]{1,0:T(8,128)(2,1)S(1)}, u32[]{:S(2)}, u32[]{:S(2)}) collective-permute-start(bf16[384,384]{1,0:T(8,128)(2,1)S(1)} %dynamic-slice_bitcast_fusion), channel_id=1, source_target_pairs={{0,130},{2,128},{128,2},{130,0},{1,131},{3,129},{129,3},{131,1},{4... | collective-permute-start | bytes 884744 | tf_op jit(solution)/shard_map/ppermute | solution.py:110
  5.3 0.9 copy-done.5
  6.2 0.8 copy-done.6
  7.1 1.4 shard_map.93
  8.5 2.5 %collective-permute-done = bf16[384,384]{1,0:T(8,128)(2,1)S(1)} collective-permute-done((bf16[384,384]{1,0:T(8,128)(2,1)S(1)}, bf16[384,384]{1,0:T(8,128)(2,1)S(1)}, u32[]{:S(2)}, u32[]{:S(2)}) %collective-permute-start) | collective-permute-done | bytes 294944 | tf_op jit(solution)/shard_map/ppermute | solution.py:110
  11.0 7.3 %all-to-all-start = ((bf16[16,32,1792]{2,1,0:T(8,128)(2,1)}), bf16[16,32,1792]{2,1,0:T(8,128)(2,1)}, u32[]{:S(2)}, u32[]{:S(2)}) async-start(bf16[16,32,1792]{2,1,0:T(8,128)(2,1)} %shard_map.93), calls=%async_computation | async-start | bytes 3670016 | tf_op jit(solution)/shard_map/all_to_all | solution.py:112
  18.4 1.9 %collective-permute-start.2 = (bf16[2,16,1024]{2,1,0:T(8,128)(2,1)S(1)}, bf16[2,16,1024]{2,1,0:T(8,128)(2,1)S(1)}, u32[]{:S(2)}, u32[]{:S(2)}) collective-permute-start(bf16[2,16,1024]{2,1,0:T(8,128)(2,1)S(1)} %get-tuple-element.87), channel_id=1, source_target_pairs={{0,1},{1,0},{2,3},{3,2},{4,5},{5,4},{6,7},{7,6},{8,9},{9,8},{10,11... | collective-permute-start | bytes 196616 | tf_op jit(solution)/shard_map/ppermute | solution.py:27
  21.2 0.4 fusion.23
  21.6 6.5 %collective-permute-start.5 = (bf16[64,1792]{1,0:T(8,128)(2,1)S(1)}, bf16[64,1792]{1,0:T(8,128)(2,1)S(1)}, u32[]{:S(2)}, u32[]{:S(2)}) collective-permute-start(bf16[64,1792]{1,0:T(8,128)(2,1)S(1)} %bitcast.185), channel_id=1, source_target_pairs={{0,12},{4,16},{8,20},{12,24},{16,28},{20,0},{24,4},{28,8},{1,21},{... | collective-permute-start | bytes 688136 | tf_op jit(solution)/shard_map/ppermute | solution.py:33
  28.4 0.5 collective-permute-start.3
  28.9 2.4 %collective-permute-start.1 = (bf16[384,384]{1,0:T(8,128)(2,1)S(1)}, bf16[384,384]{1,0:T(8,128)(2,1)S(1)}, u32[]{:S(2)}, u32[]{:S(2)}) collective-permute-start(bf16[384,384]{1,0:T(8,128)(2,1)S(1)} %collective-permute-done), channel_id=1, source_target_pairs={{0,1},{1,0},{2,3},{3,2},{4,5},{5,4},{6,7},{7,6},{8,9},{9,8},{10,11... | collective-permute-start | bytes 884744 | tf_op jit(solution)/shard_map/ppermute | solution.py:27
  31.3 7.0 %collective-permute-done.5.refs_0_ = bf16[64,1792]{1,0:T(8,128)(2,1)S(1)} collective-permute-done((bf16[64,1792]{1,0:T(8,128)(2,1)S(1)}, bf16[64,1792]{1,0:T(8,128)(2,1)S(1)}, u32[]{:S(2)}, u32[]{:S(2)}) %collective-permute-start.5) | collective-permute-done | bytes 229408 | tf_op jit(solution)/shard_map/ppermute | solution.py:33
  38.3 0.8 collective-permute-start.9
  39.1 1.8 %collective-permute-done.4.refs_1_ = bf16[64,1792]{1,0:T(8,128)(2,1)S(1)} collective-permute-done((bf16[64,1792]{1,0:T(8,128)(2,1)S(1)}, bf16[64,1792]{1,0:T(8,128)(2,1)S(1)}, u32[]{:S(2)}, u32[]{:S(2)}) %collective-permute-start.4) | collective-permute-done | bytes 229408 | tf_op jit(solution)/shard_map/ppermute | solution.py:33
  41.0 1.3 collective-permute-start.7
  42.3 1.2 collective-permute-done.3.refs_2_
  43.4 0.9 collective-permute-start.6
  44.6 0.9 collective-permute-start.10
  45.5 1.0 collective-permute-done.10.refs_8_
  47.2 0.9 copy-done.2
  48.2 0.9 copy-done.4
  49.3 2.0 %fusion.55 = (f32[512]{0:T(512)S(1)}, f32[512,512]{1,0:T(8,128)S(1)}) fusion(bf16[512,1792]{1,0:T(8,128)(2,1)S(1)} %bitcast.182, bf16[512,1792]{1,0:T(8,128)(2,1)} %bitcast.15), kind=kOutput, calls=%fused_computation.130 | convolution fusion | flops 537394688 | bytes 3147776 | tf_op jit(solution)/shard_map/dot_general | solution.py:86
  51.4 0.9 multiply_reduce_fusion
  52.3 2.4 %fusion.56 = (f32[512]{0:T(512)S(1)}, f32[512,512]{1,0:T(8,128)S(1)}) fusion(f32[512,768]{1,0:T(8,128)S(1)} %get-tuple-element.94, f32[512]{0:T(512)S(1)} %add_rsqrt_fusion, bf16[512,1792]{1,0:T(8,128)(2,1)} %bitcast.15), kind=kOutput, calls=%fused_computation.131 | convolution fusion | flops 403963392 | bytes 3411968 | tf_op jit(solution)/shard_map/dot_general | solution.py:86
  54.7 0.4 multiply_reduce_fusion.1
  55.2 0.7 broadcast_in_dim.6
  55.9 6.3 %all-to-all-start.1 = ((f32[8,8,512]{2,1,0:T(8,128)}), f32[8,8,512]{2,1,0:T(8,128)S(1)}, u32[]{:S(2)}, u32[]{:S(2)}) async-start(f32[8,8,512]{2,1,0:T(8,128)} %broadcast_in_dim.6), calls=%async_computation.1 | async-start | bytes 262144 | tf_op jit(solution)/shard_map/all_to_all | solution.py:19
  62.3 7.8 %all-to-all-done.1 = f32[8,8,512]{2,1,0:T(8,128)S(1)} async-done(((f32[8,8,512]{2,1,0:T(8,128)}), f32[8,8,512]{2,1,0:T(8,128)S(1)}, u32[]{:S(2)}, u32[]{:S(2)}) %all-to-all-start.1) | async-done | bytes 131104 | tf_op jit(solution)/shard_map/all_to_all | solution.py:19
  70.3 5.2 %collective-permute-start.11 = (f32[8,512]{1,0:T(8,128)S(1)}, f32[8,512]{1,0:T(8,128)S(1)}, u32[]{:S(2)}, u32[]{:S(2)}) collective-permute-start(f32[8,512]{1,0:T(8,128)S(1)} %stack.102), channel_id=1, source_target_pairs={{0,1},{1,0},{2,3},{3,2},{4,5},{5,4},{6,7},{7,6},{8,9},{9,8},{10,11... | collective-permute-start | bytes 49160 | tf_op jit(solution)/shard_map/ppermute | solution.py:27
  75.8 0.6 collective-permute-done.11
  76.5 1.5 %multiply_convert_fusion.2 = bf16[512,512]{1,0:T(8,128)(2,1)S(1)} fusion(f32[512,512]{1,0:T(8,128)} %copy-done.9, f32[512,512]{1,0:T(8,128)S(1)} %get-tuple-element.98, f32[512]{0:T(512)S(1)} %get-tuple-element.92, f32[512]{0:T(512)S(1)} %get-tuple-element.73), kind=kLoop, calls=%fused_computation.25 | loop fusion | flops 1310720 | bytes 2625536 | tf_op jit(solution)/shard_map/convert_element_type | solution.py:164
  78.0 1.8 %convolution_multiply_fusion = f32[512,768]{1,0:T(8,128)S(1)} fusion(bf16[512,512]{1,0:T(8,128)(2,1)S(1)} %multiply_convert_fusion.2, bf16[512,1792]{1,0:T(8,128)(2,1)} %bitcast.15), kind=kOutput, calls=%fused_computation.4 | convolution fusion | flops 403046400 | bytes 2883584 | tf_op jit(solution)/shard_map/dot_general | solution.py:86
  80.2 0.5 fusion.57
  80.7 0.4 collective-permute-start.12
  81.1 0.7 multiply_convert_fusion
  81.8 1.0 collective-permute-done.12
  83.0 1.2 pad_maximum_fusion
  84.1 4.1 %all-to-all-start.2 = ((bf16[16,56,768]{2,1,0:T(8,128)(2,1)}), bf16[16,56,768]{2,1,0:T(8,128)(2,1)S(1)}, u32[]{:S(2)}, u32[]{:S(2)}) async-start(bf16[16,56,768]{2,1,0:T(8,128)(2,1)} %pad_maximum_fusion), calls=%async_computation.2 | async-start | bytes 2752512 | tf_op jit(solution)/shard_map/all_to_all | solution.py:188
  88.3 0.7 collective-permute-start.13
  89.0 1.5 %collective-permute-done.13 = bf16[256,768]{1,0:T(8,128)(2,1)} collective-permute-done((bf16[256,768]{1,0:T(8,128)(2,1)S(1)}, bf16[256,768]{1,0:T(8,128)(2,1)}, u32[]{:S(2)}, u32[]{:S(2)}) %collective-permute-start.13) | collective-permute-done | bytes 393248 | tf_op jit(solution)/shard_map/ppermute | solution.py:27
  90.5 1.1 fusion.16
  92.2 3.2 %collective-permute-start.18 = (bf16[32,768]{1,0:T(8,128)(2,1)S(1)}, bf16[32,768]{1,0:T(8,128)(2,1)S(1)}, u32[]{:S(2)}, u32[]{:S(2)}) collective-permute-start(bf16[32,768]{1,0:T(8,128)(2,1)S(1)} %get-tuple-element.76), channel_id=1, source_target_pairs={{0,20},{4,24},{8,28},{12,0},{16,4},{20,8},{24,12},{28,16},{1,21},{... | collective-permute-start | bytes 147464 | tf_op jit(solution)/shard_map/ppermute | solution.py:185
  95.4 2.2 %collective-permute-start.17 = (bf16[32,768]{1,0:T(8,128)(2,1)S(1)}, bf16[32,768]{1,0:T(8,128)(2,1)S(1)}, u32[]{:S(2)}, u32[]{:S(2)}) collective-permute-start(bf16[32,768]{1,0:T(8,128)(2,1)S(1)} %get-tuple-element.77), channel_id=1, source_target_pairs={{0,16},{4,20},{8,24},{12,28},{16,0},{20,4},{24,8},{28,12},{1,17},{... | collective-permute-start | bytes 147464 | tf_op jit(solution)/shard_map/ppermute | solution.py:185
  97.6 2.3 %collective-permute-start.16 = (bf16[32,768]{1,0:T(8,128)(2,1)S(1)}, bf16[32,768]{1,0:T(8,128)(2,1)S(1)}, u32[]{:S(2)}, u32[]{:S(2)}) collective-permute-start(bf16[32,768]{1,0:T(8,128)(2,1)S(1)} %get-tuple-element.78), channel_id=1, source_target_pairs={{0,12},{4,16},{8,20},{12,24},{16,28},{20,0},{24,4},{28,8},{1,13},{... | collective-permute-start | bytes 147464 | tf_op jit(solution)/shard_map/ppermute | solution.py:185
  99.9 1.3 collective-permute-start.15
  101.2 1.0 collective-permute-done.17
  102.2 4.9 %collective-permute-done.16 = bf16[32,768]{1,0:T(8,128)(2,1)S(1)} collective-permute-done((bf16[32,768]{1,0:T(8,128)(2,1)S(1)}, bf16[32,768]{1,0:T(8,128)(2,1)S(1)}, u32[]{:S(2)}, u32[]{:S(2)}) %collective-permute-start.16) | collective-permute-done | bytes 49184 | tf_op jit(solution)/shard_map/ppermute | solution.py:185
  107.2 2.1 %collective-permute-done.14 = bf16[32,768]{1,0:T(8,128)(2,1)S(1)} collective-permute-done((bf16[32,768]{1,0:T(8,128)(2,1)S(1)}, bf16[32,768]{1,0:T(8,128)(2,1)S(1)}, u32[]{:S(2)}, u32[]{:S(2)}) %collective-permute-start.14) | collective-permute-done | bytes 49184 | tf_op jit(solution)/shard_map/ppermute | solution.py:185
  109.3 0.6 all-to-all-done.2
  110.2 0.7 broadcast_in_dim.7
  110.9 3.4 %all-to-all-start.3 = ((bf16[8,24,768]{2,1,0:T(8,128)(2,1)}), bf16[8,24,768]{2,1,0:T(8,128)(2,1)S(1)}, u32[]{:S(2)}, u32[]{:S(2)}) async-start(bf16[8,24,768]{2,1,0:T(8,128)(2,1)} %broadcast_in_dim.7), calls=%async_computation.3 | async-start | bytes 589824 | tf_op jit(solution)/shard_map/all_to_all | solution.py:19
  114.5 2.9 %collective-permute-start.22 = (f32[4,2,8]{2,0,1:T(4,128)S(1)}, f32[4,2,8]{2,0,1:T(4,128)S(1)}, u32[]{:S(2)}, u32[]{:S(2)}) collective-permute-start(f32[4,2,8]{2,0,1:T(4,128)S(1)} %fusion.40), channel_id=1, source_target_pairs={{0,2},{2,0},{1,3},{3,1},{4,6},{6,4},{5,7},{7,5},{8,10},{10,8},{9,1... | collective-permute-start | bytes 776 | tf_op jit(solution)/shard_map/ppermute | solution.py:27
  117.9 4.7 %all_gather.10 = bf16[64,768]{1,0:T(8,128)(2,1)S(1)} all-gather(bf16[32,768]{1,0:T(8,128)(2,1)S(1)} %slice_reduce_fusion), channel_id=1, replica_groups=mesh['yl'=2,'x'=4,'z'=8,'yh'=2,'c'=2] {'c'}, dimensions={0}, use_global_device_ids=true | all-gather | bytes 147456 | tf_op jit(solution)/shard_map/all_gather | solution.py:198
  122.6 1.5 all-to-all-done.3
  124.1 0.7 broadcast_in_dim.8
  124.9 7.5 %all-to-all-start.4 = ((bf16[16,24,384]{2,1,0:T(8,128)(2,1)}), bf16[16,24,384]{2,1,0:T(8,128)(2,1)S(1)}, u32[]{:S(2)}, u32[]{:S(2)}) async-start(bf16[16,24,384]{2,1,0:T(8,128)(2,1)} %bitcast.63), calls=%async_computation.4 | async-start | bytes 589824 | tf_op jit(solution)/shard_map/all_to_all | solution.py:212
  132.4 0.6 select_n.118
  133.1 4.7 %all_gather.11 = bf16[2,2,32,384]{3,2,1,0:T(8,128)(2,1)S(1)} all-gather(bf16[1,2,32,384]{3,2,1,0:T(8,128)(2,1)S(1)} %maximum_select_fusion.4), channel_id=1, replica_groups=mesh['yl'=2,'x'=4,'z'=8,'yh'=2,'c'=2] {'c'}, dimensions={0}, use_global_device_ids=true | all-gather | bytes 147456 | tf_op jit(solution)/shard_map/all_gather | solution.py:216
  137.8 0.7 copy.87
  138.4 1.8 %all-to-all-done.4 = bf16[16,24,384]{2,1,0:T(8,128)(2,1)S(1)} async-done(((bf16[16,24,384]{2,1,0:T(8,128)(2,1)}), bf16[16,24,384]{2,1,0:T(8,128)(2,1)S(1)}, u32[]{:S(2)}, u32[]{:S(2)}) %all-to-all-start.4) | async-done | bytes 294944 | tf_op jit(solution)/shard_map/all_to_all | solution.py:212
  140.2 6.2 %all_gather.12 = bf16[768,384]{1,0:T(8,128)(2,1)S(1)} all-gather(bf16[384,384]{1,0:T(8,128)(2,1)S(1)} %bitcast.196), channel_id=1, replica_groups=mesh['yl'=2,'x'=4,'z'=8,'yh'=2,'c'=2] {'c'}, dimensions={0}, use_global_device_ids=true | all-gather | bytes 884736 | tf_op jit(solution)/shard_map/all_gather | solution.py:222
  146.4 1.1 convert_element_type.94
  147.4 0.6 copy.134
  (92 shorter events, 4.6 us)
Async XLA Ops:
  0.6 20.3 %copy-start = (bf16[128,768]{1,0:T(8,128)(2,1)S(1)}, bf16[128,768]{1,0:T(8,128)(2,1)}, u32[]{:S(2)}) copy-start(bf16[128,768]{1,0:T(8,128)(2,1)} %param.6) | copy-start | bytes 589828
  1.7 9.3 %collective-permute-start = (bf16[384,384]{1,0:T(8,128)(2,1)S(1)}, bf16[384,384]{1,0:T(8,128)(2,1)S(1)}, u32[]{:S(2)}, u32[]{:S(2)}) collective-permute-start(bf16[384,384]{1,0:T(8,128)(2,1)S(1)} %dynamic-slice_bitcast_fusion), channel_id=1, source_target_pairs={{0,130},{2,128},{128,2},{130,0},{1,131},{3,129},{129,3},{131,1},{4... | collective-permute-start | bytes 884744 | tf_op jit(solution)/shard_map/ppermute | solution.py:110
  5.3 0.9 copy-start.5
  6.2 0.8 copy-start.6
  8.5 9.8 %copy-start.11 = (bf16[64,1024]{1,0:T(8,128)(2,1)S(1)}, bf16[64,1024]{1,0:T(8,128)(2,1)}, u32[]{:S(2)}) copy-start(bf16[64,1024]{1,0:T(8,128)(2,1)} %param.9) | copy-start | bytes 393220
  11.0 35.5 %all-to-all-start = ((bf16[16,32,1792]{2,1,0:T(8,128)(2,1)}), bf16[16,32,1792]{2,1,0:T(8,128)(2,1)}, u32[]{:S(2)}, u32[]{:S(2)}) async-start(bf16[16,32,1792]{2,1,0:T(8,128)(2,1)} %shard_map.93), calls=%async_computation | async-start | bytes 3670016 | tf_op jit(solution)/shard_map/all_to_all | solution.py:112
  18.4 2.8 %collective-permute-start.2 = (bf16[2,16,1024]{2,1,0:T(8,128)(2,1)S(1)}, bf16[2,16,1024]{2,1,0:T(8,128)(2,1)S(1)}, u32[]{:S(2)}, u32[]{:S(2)}) collective-permute-start(bf16[2,16,1024]{2,1,0:T(8,128)(2,1)S(1)} %get-tuple-element.87), channel_id=1, source_target_pairs={{0,1},{1,0},{2,3},{3,2},{4,5},{5,4},{6,7},{7,6},{8,9},{9,8},{10,11... | collective-permute-start | bytes 196616 | tf_op jit(solution)/shard_map/ppermute | solution.py:27
  21.6 16.6 %collective-permute-start.5 = (bf16[64,1792]{1,0:T(8,128)(2,1)S(1)}, bf16[64,1792]{1,0:T(8,128)(2,1)S(1)}, u32[]{:S(2)}, u32[]{:S(2)}) collective-permute-start(bf16[64,1792]{1,0:T(8,128)(2,1)S(1)} %bitcast.185), channel_id=1, source_target_pairs={{0,12},{4,16},{8,20},{12,24},{16,28},{20,0},{24,4},{28,8},{1,21},{... | collective-permute-start | bytes 688136 | tf_op jit(solution)/shard_map/ppermute | solution.py:33
  28.2 12.8 %collective-permute-start.4 = (bf16[64,1792]{1,0:T(8,128)(2,1)S(1)}, bf16[64,1792]{1,0:T(8,128)(2,1)S(1)}, u32[]{:S(2)}, u32[]{:S(2)}) collective-permute-start(bf16[64,1792]{1,0:T(8,128)(2,1)S(1)} %bitcast.186), channel_id=1, source_target_pairs={{0,8},{4,12},{8,16},{12,20},{16,24},{20,28},{24,0},{28,4},{1,25},{... | collective-permute-start | bytes 688136 | tf_op jit(solution)/shard_map/ppermute | solution.py:33
  28.4 15.0 %collective-permute-start.3 = (bf16[64,1792]{1,0:T(8,128)(2,1)S(1)}, bf16[64,1792]{1,0:T(8,128)(2,1)S(1)}, u32[]{:S(2)}, u32[]{:S(2)}) collective-permute-start(bf16[64,1792]{1,0:T(8,128)(2,1)S(1)} %bitcast.187), channel_id=1, source_target_pairs={{0,4},{4,8},{8,12},{12,16},{16,20},{20,24},{24,28},{28,0},{1,29},{... | collective-permute-start | bytes 688136 | tf_op jit(solution)/shard_map/ppermute | solution.py:33
  28.9 17.7 %collective-permute-start.1 = (bf16[384,384]{1,0:T(8,128)(2,1)S(1)}, bf16[384,384]{1,0:T(8,128)(2,1)S(1)}, u32[]{:S(2)}, u32[]{:S(2)}) collective-permute-start(bf16[384,384]{1,0:T(8,128)(2,1)S(1)} %collective-permute-done), channel_id=1, source_target_pairs={{0,1},{1,0},{2,3},{3,2},{4,5},{5,4},{6,7},{7,6},{8,9},{9,8},{10,11... | collective-permute-start | bytes 884744 | tf_op jit(solution)/shard_map/ppermute | solution.py:27
  38.3 6.4 %collective-permute-start.9 = (bf16[32,1792]{1,0:T(8,128)(2,1)S(1)}, bf16[32,1792]{1,0:T(8,128)(2,1)S(1)}, u32[]{:S(2)}, u32[]{:S(2)}) collective-permute-start(bf16[32,1792]{1,0:T(8,128)(2,1)S(1)} %dynamic-slice_bitcast_fusion.1), channel_id=1, source_target_pairs={{0,4},{4,8},{8,12},{12,16},{16,20},{20,24},{24,28},{28,0},{1,29},{... | collective-permute-start | bytes 344072 | tf_op jit(solution)/shard_map/ppermute | solution.py:33
  39.1 7.4 %collective-permute-start.8 = (bf16[64,1792]{1,0:T(8,128)(2,1)S(1)}, bf16[64,1792]{1,0:T(8,128)(2,1)S(1)}, u32[]{:S(2)}, u32[]{:S(2)}) collective-permute-start(bf16[64,1792]{1,0:T(8,128)(2,1)S(1)} %collective-permute-done.5.refs_0_), channel_id=1, source_target_pairs={{0,1},{1,0},{2,3},{3,2},{4,5},{5,4},{6,7},{7,6},{8,9},{9,8},{10,11... | collective-permute-start | bytes 688136 | tf_op jit(solution)/shard_map/ppermute | solution.py:27
  41.0 5.6 %collective-permute-start.7 = (bf16[64,1792]{1,0:T(8,128)(2,1)S(1)}, bf16[64,1792]{1,0:T(8,128)(2,1)S(1)}, u32[]{:S(2)}, u32[]{:S(2)}) collective-permute-start(bf16[64,1792]{1,0:T(8,128)(2,1)S(1)} %collective-permute-done.4.refs_1_), channel_id=1, source_target_pairs={{0,1},{1,0},{2,3},{3,2},{4,5},{5,4},{6,7},{7,6},{8,9},{9,8},{10,11... | collective-permute-start | bytes 688136 | tf_op jit(solution)/shard_map/ppermute | solution.py:27
  43.4 3.1 %collective-permute-start.6 = (bf16[64,1792]{1,0:T(8,128)(2,1)S(1)}, bf16[64,1792]{1,0:T(8,128)(2,1)S(1)}, u32[]{:S(2)}, u32[]{:S(2)}) collective-permute-start(bf16[64,1792]{1,0:T(8,128)(2,1)S(1)} %collective-permute-done.3.refs_2_), channel_id=1, source_target_pairs={{0,1},{1,0},{2,3},{3,2},{4,5},{5,4},{6,7},{7,6},{8,9},{9,8},{10,11... | collective-permute-start | bytes 688136 | tf_op jit(solution)/shard_map/ppermute | solution.py:27
  44.6 1.9 %collective-permute-start.10 = (bf16[32,1792]{1,0:T(8,128)(2,1)S(1)}, bf16[32,1792]{1,0:T(8,128)(2,1)S(1)}, u32[]{:S(2)}, u32[]{:S(2)}) collective-permute-start(bf16[32,1792]{1,0:T(8,128)(2,1)S(1)} %collective-permute-done.9.refs_7_), channel_id=1, source_target_pairs={{0,1},{1,0},{2,3},{3,2},{4,5},{5,4},{6,7},{7,6},{8,9},{9,8},{10,11... | collective-permute-start | bytes 344072 | tf_op jit(solution)/shard_map/ppermute | solution.py:27
  46.5 0.6 copy-start.3
  46.5 0.7 copy-start.1
  47.2 0.9 copy-start.2
  48.2 0.9 copy-start.4
  49.3 2.1 %copy-start.10 = (bf16[768,384]{1,0:T(8,128)(2,1)S(1)}, bf16[768,384]{1,0:T(8,128)(2,1)}, u32[]{:S(2)}) copy-start(bf16[768,384]{1,0:T(8,128)(2,1)} %param.8) | copy-start | bytes 1769476
  51.4 3.4 %copy-start.9 = (f32[512,512]{1,0:T(8,128)}, f32[512,512]{1,0:T(8,128)S(1)}, u32[]{:S(2)}) copy-start(f32[512,512]{1,0:T(8,128)S(1)} %get-tuple-element.96) | copy-start | bytes 3145732
  52.3 2.4 %copy-start.7 = (f32[512,768]{1,0:T(8,128)}, f32[512,768]{1,0:T(8,128)S(1)}, u32[]{:S(2)}) copy-start(f32[512,768]{1,0:T(8,128)S(1)} %get-tuple-element.94) | copy-start | bytes 4718596
  55.9 14.3 %all-to-all-start.1 = ((f32[8,8,512]{2,1,0:T(8,128)}), f32[8,8,512]{2,1,0:T(8,128)S(1)}, u32[]{:S(2)}, u32[]{:S(2)}) async-start(f32[8,8,512]{2,1,0:T(8,128)} %broadcast_in_dim.6), calls=%async_computation.1 | async-start | bytes 262144 | tf_op jit(solution)/shard_map/all_to_all | solution.py:19
  70.3 6.0 %collective-permute-start.11 = (f32[8,512]{1,0:T(8,128)S(1)}, f32[8,512]{1,0:T(8,128)S(1)}, u32[]{:S(2)}, u32[]{:S(2)}) collective-permute-start(f32[8,512]{1,0:T(8,128)S(1)} %stack.102), channel_id=1, source_target_pairs={{0,1},{1,0},{2,3},{3,2},{4,5},{5,4},{6,7},{7,6},{8,9},{9,8},{10,11... | collective-permute-start | bytes 49160 | tf_op jit(solution)/shard_map/ppermute | solution.py:27
  78.0 1.9 %copy-start.8 = (f32[512,768]{1,0:T(8,128)S(1)}, f32[512,768]{1,0:T(8,128)}, u32[]{:S(2)}) copy-start(f32[512,768]{1,0:T(8,128)} %copy-done.7) | copy-start | bytes 4718596
  80.7 2.1 %collective-permute-start.12 = (bf16[384,768]{1,0:T(8,128)(2,1)S(1)}, bf16[384,768]{1,0:T(8,128)(2,1)S(1)}, u32[]{:S(2)}, u32[]{:S(2)}) collective-permute-start(bf16[384,768]{1,0:T(8,128)(2,1)S(1)} %fusion.19), channel_id=1, source_target_pairs={{0,1},{1,0},{2,3},{3,2},{4,5},{5,4},{6,7},{7,6},{8,9},{9,8},{10,11... | collective-permute-start | bytes 1769480 | tf_op jit(solution)/shard_map/ppermute | solution.py:27
  84.1 25.8 %all-to-all-start.2 = ((bf16[16,56,768]{2,1,0:T(8,128)(2,1)}), bf16[16,56,768]{2,1,0:T(8,128)(2,1)S(1)}, u32[]{:S(2)}, u32[]{:S(2)}) async-start(bf16[16,56,768]{2,1,0:T(8,128)(2,1)} %pad_maximum_fusion), calls=%async_computation.2 | async-start | bytes 2752512 | tf_op jit(solution)/shard_map/all_to_all | solution.py:188
  88.3 2.2 %collective-permute-start.13 = (bf16[256,768]{1,0:T(8,128)(2,1)S(1)}, bf16[256,768]{1,0:T(8,128)(2,1)}, u32[]{:S(2)}, u32[]{:S(2)}) collective-permute-start(bf16[256,768]{1,0:T(8,128)(2,1)S(1)} %slice.196), channel_id=1, source_target_pairs={{0,1},{1,0},{2,3},{3,2},{4,5},{5,4},{6,7},{7,6},{8,9},{9,8},{10,11... | collective-permute-start | bytes 1179656 | tf_op jit(solution)/shard_map/ppermute | solution.py:27
  91.8 8.1 %collective-permute-start.20 = (bf16[32,768]{1,0:T(8,128)(2,1)S(1)}, bf16[32,768]{1,0:T(8,128)(2,1)S(1)}, u32[]{:S(2)}, u32[]{:S(2)}) collective-permute-start(bf16[32,768]{1,0:T(8,128)(2,1)S(1)} %get-tuple-element.74), channel_id=1, source_target_pairs={{0,28},{4,0},{8,4},{12,8},{16,12},{20,16},{24,20},{28,24},{1,29},{... | collective-permute-start | bytes 147464 | tf_op jit(solution)/shard_map/ppermute | solution.py:185
  91.9 9.3 %collective-permute-start.19 = (bf16[32,768]{1,0:T(8,128)(2,1)S(1)}, bf16[32,768]{1,0:T(8,128)(2,1)S(1)}, u32[]{:S(2)}, u32[]{:S(2)}) collective-permute-start(bf16[32,768]{1,0:T(8,128)(2,1)S(1)} %get-tuple-element.75), channel_id=1, source_target_pairs={{0,24},{4,28},{8,0},{12,4},{16,8},{20,12},{24,16},{28,20},{1,25},{... | collective-permute-start | bytes 147464 | tf_op jit(solution)/shard_map/ppermute | solution.py:185
  92.2 9.0 %collective-permute-start.18 = (bf16[32,768]{1,0:T(8,128)(2,1)S(1)}, bf16[32,768]{1,0:T(8,128)(2,1)S(1)}, u32[]{:S(2)}, u32[]{:S(2)}) collective-permute-start(bf16[32,768]{1,0:T(8,128)(2,1)S(1)} %get-tuple-element.76), channel_id=1, source_target_pairs={{0,20},{4,24},{8,28},{12,0},{16,4},{20,8},{24,12},{28,16},{1,21},{... | collective-permute-start | bytes 147464 | tf_op jit(solution)/shard_map/ppermute | solution.py:185
  95.4 6.8 %collective-permute-start.17 = (bf16[32,768]{1,0:T(8,128)(2,1)S(1)}, bf16[32,768]{1,0:T(8,128)(2,1)S(1)}, u32[]{:S(2)}, u32[]{:S(2)}) collective-permute-start(bf16[32,768]{1,0:T(8,128)(2,1)S(1)} %get-tuple-element.77), channel_id=1, source_target_pairs={{0,16},{4,20},{8,24},{12,28},{16,0},{20,4},{24,8},{28,12},{1,17},{... | collective-permute-start | bytes 147464 | tf_op jit(solution)/shard_map/ppermute | solution.py:185
  97.6 9.6 %collective-permute-start.16 = (bf16[32,768]{1,0:T(8,128)(2,1)S(1)}, bf16[32,768]{1,0:T(8,128)(2,1)S(1)}, u32[]{:S(2)}, u32[]{:S(2)}) collective-permute-start(bf16[32,768]{1,0:T(8,128)(2,1)S(1)} %get-tuple-element.78), channel_id=1, source_target_pairs={{0,12},{4,16},{8,20},{12,24},{16,28},{20,0},{24,4},{28,8},{1,13},{... | collective-permute-start | bytes 147464 | tf_op jit(solution)/shard_map/ppermute | solution.py:185
  99.9 7.3 %collective-permute-start.15 = (bf16[32,768]{1,0:T(8,128)(2,1)S(1)}, bf16[32,768]{1,0:T(8,128)(2,1)S(1)}, u32[]{:S(2)}, u32[]{:S(2)}) collective-permute-start(bf16[32,768]{1,0:T(8,128)(2,1)S(1)} %get-tuple-element.79), channel_id=1, source_target_pairs={{0,8},{4,12},{8,16},{12,20},{16,24},{20,28},{24,0},{28,4},{1,9},{5... | collective-permute-start | bytes 147464 | tf_op jit(solution)/shard_map/ppermute | solution.py:185
  101.2 8.1 %collective-permute-start.14 = (bf16[32,768]{1,0:T(8,128)(2,1)S(1)}, bf16[32,768]{1,0:T(8,128)(2,1)S(1)}, u32[]{:S(2)}, u32[]{:S(2)}) collective-permute-start(bf16[32,768]{1,0:T(8,128)(2,1)S(1)} %get-tuple-element.80), channel_id=1, source_target_pairs={{0,4},{4,8},{8,12},{12,16},{16,20},{20,24},{24,28},{28,0},{1,5},{5... | collective-permute-start | bytes 147464 | tf_op jit(solution)/shard_map/ppermute | solution.py:185
  110.9 13.2 %all-to-all-start.3 = ((bf16[8,24,768]{2,1,0:T(8,128)(2,1)}), bf16[8,24,768]{2,1,0:T(8,128)(2,1)S(1)}, u32[]{:S(2)}, u32[]{:S(2)}) async-start(bf16[8,24,768]{2,1,0:T(8,128)(2,1)} %broadcast_in_dim.7), calls=%async_computation.3 | async-start | bytes 589824 | tf_op jit(solution)/shard_map/all_to_all | solution.py:19
  114.5 8.1 %collective-permute-start.22 = (f32[4,2,8]{2,0,1:T(4,128)S(1)}, f32[4,2,8]{2,0,1:T(4,128)S(1)}, u32[]{:S(2)}, u32[]{:S(2)}) collective-permute-start(f32[4,2,8]{2,0,1:T(4,128)S(1)} %fusion.40), channel_id=1, source_target_pairs={{0,2},{2,0},{1,3},{3,1},{4,6},{6,4},{5,7},{7,5},{8,10},{10,8},{9,1... | collective-permute-start | bytes 776 | tf_op jit(solution)/shard_map/ppermute | solution.py:27
  117.5 5.1 %collective-permute-start.21 = (bf16[32,384]{1,0:T(8,128)(2,1)S(1)}, bf16[32,384]{1,0:T(8,128)(2,1)S(1)}, u32[]{:S(2)}, u32[]{:S(2)}) collective-permute-start(bf16[32,384]{1,0:T(8,128)(2,1)S(1)} %bitcast.210), channel_id=1, source_target_pairs={{0,2},{2,0},{1,3},{3,1},{4,6},{6,4},{5,7},{7,5},{8,10},{10,8},{9,1... | collective-permute-start | bytes 73736 | tf_op jit(solution)/shard_map/ppermute | solution.py:27
  124.9 15.3 %all-to-all-start.4 = ((bf16[16,24,384]{2,1,0:T(8,128)(2,1)}), bf16[16,24,384]{2,1,0:T(8,128)(2,1)S(1)}, u32[]{:S(2)}, u32[]{:S(2)}) async-start(bf16[16,24,384]{2,1,0:T(8,128)(2,1)} %bitcast.63), calls=%async_computation.4 | async-start | bytes 589824 | tf_op jit(solution)/shard_map/all_to_all | solution.py:212

commit v3 on v2

--- a/solution.py
+++ b/solution.py
@@ -176,7 +176,12 @@
     ).astype(bf16)
     share = dot(blocks(rows[:, :width]), head_slope, 0, 0).reshape(2, half, width)
     share = pick(share, core, 0) + swap(pick(share, 1 - core, 0).astype(bf16), "c").astype(f32)
-    share = share.astype(bf16).reshape(16, 24, width)
+    share = share.astype(bf16).reshape(8, 2, 24, width)
+    share = [
+        jnp.concatenate([share[:, 0, :, columns], share[:, 1, :, columns]], 2)
+        for columns in (slice(0, half), slice(half, width))
+    ]
+    share = jnp.stack(share, 1).reshape(16, 24, width)
 
     grad = grad[:256] + swap(grad[256:].astype(bf16), "c").astype(f32)
     grad = grad.astype(bf16).reshape(8, 32, width)
@@ -195,30 +200,35 @@
         return lax.dynamic_slice_in_dim(jnp.concatenate([value, value], 0), 4 - group, 4, 0)
 
     text_sum = jnp.sum(sent[:, :32].astype(f32), axis=0).astype(bf16)
-    text_grad = lax.all_gather(text_sum, "c", axis=0, tiled=True)
+    text_come = swap(text_sum, "c")
     halves = back(grad.astype(bf16).reshape(4, 8, width)).reshape(32, 2, half)
     grad_come = swap(pick(halves, 1 - high, 1), "yh")
     losses = pick(losses.reshape(2, 8, 4, 8), here, 1)
     losses = jnp.where(core == 0, losses, losses[::-1])
     losses = back(losses.transpose(1, 0, 2))
     losses_come = swap(losses, "yh")
-    share, text_grad, grad_come, losses_come = lax.optimization_barrier(
-        (share, text_grad, grad_come, losses_come)
+    share, text_come, grad_come, losses_come = lax.optimization_barrier(
+        (share, text_come, grad_come, losses_come)
     )
 
     share = jnp.sum(share.astype(f32), axis=0).astype(bf16)
-    share = share.reshape(24, 2, half).transpose(1, 0, 2)
-    share = jnp.broadcast_to(share[None], (8, 2, 24, half)).reshape(16, 24, half)
-    share = lax.all_to_all(share, COLS, 0, 0, tiled=True).reshape(half, half)
+    share = jnp.concatenate([share[:, :half], share[:, half:]], 0)
+    share = to_all(share, ("x", "yl"), 8).reshape(half, half)
 
     mine = pick(halves, high, 1)
     pair = jnp.where(high == 0, jnp.stack([mine, grad_come]), jnp.stack([grad_come, mine]))
-    pair = lax.all_gather(pair, "c", axis=0)
+    pair_come = swap(pair, "c")
+    pair = jnp.where(core == 0, jnp.stack([pair, pair_come]), jnp.stack([pair_come, pair]))
     image_grad = pair.reshape(2, 2, 4, 8, half).transpose(2, 1, 0, 3, 4).reshape(128, half)
+    text_grad = jnp.where(
+        core == 0, jnp.concatenate([text_sum, text_come], 0), jnp.concatenate([text_come, text_sum], 0)
+    )
     row_loss = jnp.where(
         high == 0, jnp.stack([losses, losses_come], 1), jnp.stack([losses_come, losses], 1)
     ).reshape(128)
-    share, row_loss, image_grad = lax.optimization_barrier((share, row_loss, image_grad))
+    share, row_loss, image_grad, text_grad = lax.optimization_barrier(
+        (share, row_loss, image_grad, text_grad)
+    )
     weight_grad = lax.all_gather(share, "c", axis=0, tiled=True).astype(f32)
     return row_loss, image_grad, text_grad, weight_grad
 

time: 149 us -> 147 us (0.987)
  blocking collectives: 15.6 us -> 2.92 us
  waiting for transfers between devices: 36.9 us -> 42.9 us
  starting transfers between devices: 66.7 us -> 71 us
    all_gather x2 -> x0, blocking collectives: 9.43 us -> none  [the longest x1 4.72 us: shards(): pair = lax.all_gather(pair, 'c', axis=0)]
    all_to_all x1 -> x0, starting transfers between devices: 7.47 us -> none  [shards(): share = lax.all_to_all(share, COLS, 0, 0, tiled=True).reshape(half, half)]
    ppermute x11 -> x13, starting transfers between devices: 16.9 us -> 23.6 us  [swap(): return lax.ppermute(value, axis, [(0, 1), (1, 0)])]
    all_to_all x2 -> x3, starting transfers between devices: 9.77 us -> 14.8 us  [to_all(): return lax.all_to_all(sent, axes, 0, 0, tiled=True)]
    all_to_all x2 -> x3, waiting for transfers between devices: 9.32 us -> 13.6 us  [to_all(): return lax.all_to_all(sent, axes, 0, 0, tiled=True)]
    ppermute x11 -> x13, waiting for transfers between devices: 4.21 us -> 7.68 us  [swap(): return lax.ppermute(value, axis, [(0, 1), (1, 0)])]
    all_gather x1, blocking collectives: 6.17 us -> 2.92 us  [shards(): weight_grad = lax.all_gather(share, 'c', axis=0, tiled=True).astype(f32)]
    all_to_all x1 -> x0, waiting for transfers between devices: 1.77 us -> none  [shards(): share = lax.all_to_all(share, COLS, 0, 0, tiled=True).reshape(half, half)]
  transfers between devices with their start and end apart: 28 -> 30, of which waited for: 17 -> 17; matrix products, arithmetic and copies ran while one was open for 3% -> 3% of each run, Pallas kernels for 1% -> 1%
where the time goes in v3:
time: 147 us; the launch traced here: 146 us
  starting transfers between devices  71 us (48%)
  waiting for transfers between devices  42.9 us (29%)
  local copies, waits for them, and re-layouts  9.5 us (6%)
  matrix products  8.35 us (6%)
  other arithmetic  7.91 us (5%)
  blocking collectives  2.92 us (2%)
  between operations  1.81 us (1%)
  Pallas kernels  1.63 us (1%)
    ppermute x13, starting transfers between devices, swap(): return lax.ppermute(value, axis, [(0, 1), (1, 0)])  23.6 us
    all_to_all x3, starting transfers between devices, to_all(): return lax.all_to_all(sent, axes, 0, 0, tiled=True)  14.8 us
    all_to_all x3, waiting for transfers between devices, to_all(): return lax.all_to_all(sent, axes, 0, 0, tiled=True)  13.6 us
    ppermute x4, waiting for transfers between devices, turn(): return lax.ppermute(value, ('z', 'c'), pairs)  10.3 us
    ppermute x7, starting transfers between devices, shards(): lax.ppermute(turned[k], 'z', [(i, (i + k) % 8) for i in range(8)])  9.43 us
    dot_general x6, matrix products, dot(): lax.dot_general(left, right, (((left_dim,), (right_dim,)), ((), ())), pre...  8.35 us
    ppermute x4, starting transfers between devices, turn(): return lax.ppermute(value, ('z', 'c'), pairs)  8.11 us
    ppermute x7, waiting for transfers between devices, shards(): lax.ppermute(turned[k], 'z', [(i, (i + k) % 8) for i in range(8)])  8.07 us
  transfers between devices with their start and end apart: 30, of which 17 were waited for; matrix products, arithmetic and copies ran while one was open for 3% of the time, Pallas kernels for 1%

profile of v3, /device:TPU:1, one launch (start us, length us, event | category | flops | bytes accessed | tf_op | source)
XLA Modules:
  0.0 146.0 jit_solution(12077026812706041998)
XLA Ops:
  0.7 1.0 dynamic-slice_bitcast_fusion
  1.7 3.7 %collective-permute-start = (bf16[384,384]{1,0:T(8,128)(2,1)S(1)}, bf16[384,384]{1,0:T(8,128)(2,1)S(1)}, u32[]{:S(2)}, u32[]{:S(2)}) collective-permute-start(bf16[384,384]{1,0:T(8,128)(2,1)S(1)} %dynamic-slice_bitcast_fusion), channel_id=1, source_target_pairs={{0,130},{2,128},{128,2},{130,0},{1,131},{3,129},{129,3},{131,1},{4... | collective-permute-start | bytes 884744 | tf_op jit(solution)/shard_map/ppermute | solution.py:110
  5.3 0.9 copy-done.5
  6.2 0.8 copy-done.6
  7.1 1.4 shard_map.93
  8.5 2.5 %collective-permute-done = bf16[384,384]{1,0:T(8,128)(2,1)S(1)} collective-permute-done((bf16[384,384]{1,0:T(8,128)(2,1)S(1)}, bf16[384,384]{1,0:T(8,128)(2,1)S(1)}, u32[]{:S(2)}, u32[]{:S(2)}) %collective-permute-start) | collective-permute-done | bytes 294944 | tf_op jit(solution)/shard_map/ppermute | solution.py:110
  11.0 7.3 %all-to-all-start = ((bf16[16,32,1792]{2,1,0:T(8,128)(2,1)}), bf16[16,32,1792]{2,1,0:T(8,128)(2,1)}, u32[]{:S(2)}, u32[]{:S(2)}) async-start(bf16[16,32,1792]{2,1,0:T(8,128)(2,1)} %shard_map.93), calls=%async_computation | async-start | bytes 3670016 | tf_op jit(solution)/shard_map/all_to_all | solution.py:112
  18.4 1.9 %collective-permute-start.2 = (bf16[2,16,1024]{2,1,0:T(8,128)(2,1)S(1)}, bf16[2,16,1024]{2,1,0:T(8,128)(2,1)S(1)}, u32[]{:S(2)}, u32[]{:S(2)}) collective-permute-start(bf16[2,16,1024]{2,1,0:T(8,128)(2,1)S(1)} %get-tuple-element.93), channel_id=1, source_target_pairs={{0,1},{1,0},{2,3},{3,2},{4,5},{5,4},{6,7},{7,6},{8,9},{9,8},{10,11... | collective-permute-start | bytes 196616 | tf_op jit(solution)/shard_map/ppermute | solution.py:27
  21.6 6.5 %collective-permute-start.5 = (bf16[64,1792]{1,0:T(8,128)(2,1)S(1)}, bf16[64,1792]{1,0:T(8,128)(2,1)S(1)}, u32[]{:S(2)}, u32[]{:S(2)}) collective-permute-start(bf16[64,1792]{1,0:T(8,128)(2,1)S(1)} %bitcast.205), channel_id=1, source_target_pairs={{0,12},{4,16},{8,20},{12,24},{16,28},{20,0},{24,4},{28,8},{1,21},{... | collective-permute-start | bytes 688136 | tf_op jit(solution)/shard_map/ppermute | solution.py:33
  28.4 0.5 collective-permute-start.3
  28.9 2.4 %collective-permute-start.1 = (bf16[384,384]{1,0:T(8,128)(2,1)S(1)}, bf16[384,384]{1,0:T(8,128)(2,1)S(1)}, u32[]{:S(2)}, u32[]{:S(2)}) collective-permute-start(bf16[384,384]{1,0:T(8,128)(2,1)S(1)} %collective-permute-done), channel_id=1, source_target_pairs={{0,1},{1,0},{2,3},{3,2},{4,5},{5,4},{6,7},{7,6},{8,9},{9,8},{10,11... | collective-permute-start | bytes 884744 | tf_op jit(solution)/shard_map/ppermute | solution.py:27
  31.3 7.0 %collective-permute-done.5.refs_0_ = bf16[64,1792]{1,0:T(8,128)(2,1)S(1)} collective-permute-done((bf16[64,1792]{1,0:T(8,128)(2,1)S(1)}, bf16[64,1792]{1,0:T(8,128)(2,1)S(1)}, u32[]{:S(2)}, u32[]{:S(2)}) %collective-permute-start.5) | collective-permute-done | bytes 229408 | tf_op jit(solution)/shard_map/ppermute | solution.py:33
  38.3 0.8 collective-permute-start.9
  39.1 1.8 %collective-permute-done.4.refs_1_ = bf16[64,1792]{1,0:T(8,128)(2,1)S(1)} collective-permute-done((bf16[64,1792]{1,0:T(8,128)(2,1)S(1)}, bf16[64,1792]{1,0:T(8,128)(2,1)S(1)}, u32[]{:S(2)}, u32[]{:S(2)}) %collective-permute-start.4) | collective-permute-done | bytes 229408 | tf_op jit(solution)/shard_map/ppermute | solution.py:33
  41.0 1.3 collective-permute-start.7
  42.3 1.2 collective-permute-done.3.refs_2_
  43.4 0.9 collective-permute-start.6
  44.6 0.9 collective-permute-start.10
  45.6 1.0 collective-permute-done.10.refs_8_
  47.2 0.9 copy-done.2
  48.2 0.9 copy-done.4
  49.3 2.0 %fusion.57 = (f32[512]{0:T(512)S(1)}, f32[512,512]{1,0:T(8,128)S(1)}) fusion(bf16[512,1792]{1,0:T(8,128)(2,1)S(1)} %bitcast.202, bf16[512,1792]{1,0:T(8,128)(2,1)} %bitcast.15), kind=kOutput, calls=%fused_computation.144 | convolution fusion | flops 537394688 | bytes 3147776 | tf_op jit(solution)/shard_map/dot_general | solution.py:86
  51.4 0.9 multiply_reduce_fusion
  52.3 2.4 %fusion.58 = (f32[512]{0:T(512)S(1)}, f32[512,512]{1,0:T(8,128)S(1)}) fusion(f32[512,768]{1,0:T(8,128)S(1)} %get-tuple-element.104, f32[512]{0:T(512)S(1)} %add_rsqrt_fusion, bf16[512,1792]{1,0:T(8,128)(2,1)} %bitcast.15), kind=kOutput, calls=%fused_computation.145 | convolution fusion | flops 403963392 | bytes 3411968 | tf_op jit(solution)/shard_map/dot_general | solution.py:86
  54.7 0.4 multiply_reduce_fusion.1
  55.2 0.7 broadcast_in_dim.6
  55.9 6.3 %all-to-all-start.1 = ((f32[8,8,512]{2,1,0:T(8,128)}), f32[8,8,512]{2,1,0:T(8,128)S(1)}, u32[]{:S(2)}, u32[]{:S(2)}) async-start(f32[8,8,512]{2,1,0:T(8,128)} %broadcast_in_dim.6), calls=%async_computation.1 | async-start | bytes 262144 | tf_op jit(solution)/shard_map/all_to_all | solution.py:19
  62.3 7.8 %all-to-all-done.1 = f32[8,8,512]{2,1,0:T(8,128)S(1)} async-done(((f32[8,8,512]{2,1,0:T(8,128)}), f32[8,8,512]{2,1,0:T(8,128)S(1)}, u32[]{:S(2)}, u32[]{:S(2)}) %all-to-all-start.1) | async-done | bytes 131104 | tf_op jit(solution)/shard_map/all_to_all | solution.py:19
  70.3 5.2 %collective-permute-start.11 = (f32[8,512]{1,0:T(8,128)S(1)}, f32[8,512]{1,0:T(8,128)S(1)}, u32[]{:S(2)}, u32[]{:S(2)}) collective-permute-start(f32[8,512]{1,0:T(8,128)S(1)} %stack.131), channel_id=1, source_target_pairs={{0,1},{1,0},{2,3},{3,2},{4,5},{5,4},{6,7},{7,6},{8,9},{9,8},{10,11... | collective-permute-start | bytes 49160 | tf_op jit(solution)/shard_map/ppermute | solution.py:27
  75.8 0.6 collective-permute-done.11
  76.5 1.5 %multiply_convert_fusion.2 = bf16[512,512]{1,0:T(8,128)(2,1)S(1)} fusion(f32[512,512]{1,0:T(8,128)} %copy-done.9, f32[512,512]{1,0:T(8,128)S(1)} %get-tuple-element.108, f32[512]{0:T(512)S(1)} %get-tuple-element.102, f32[512]{0:T(512)S(1)} %get-tuple-element.75), kind=kLoop, calls=%fused_computation.25 | loop fusion | flops 1310720 | bytes 2625536 | tf_op jit(solution)/shard_map/convert_element_type | solution.py:164
  78.0 1.9 %convolution_multiply_fusion = f32[512,768]{1,0:T(8,128)S(1)} fusion(bf16[512,512]{1,0:T(8,128)(2,1)S(1)} %multiply_convert_fusion.2, bf16[512,1792]{1,0:T(8,128)(2,1)} %bitcast.15), kind=kOutput, calls=%fused_computation.4 | convolution fusion | flops 403046400 | bytes 2883584 | tf_op jit(solution)/shard_map/dot_general | solution.py:86
  80.2 0.5 fusion.59
  80.7 0.4 collective-permute-start.12
  81.2 0.7 multiply_convert_fusion
  81.8 1.0 collective-permute-done.12
  83.2 1.2 pad_maximum_fusion
  84.4 4.1 %all-to-all-start.2 = ((bf16[16,56,768]{2,1,0:T(8,128)(2,1)}), bf16[16,56,768]{2,1,0:T(8,128)(2,1)S(1)}, u32[]{:S(2)}, u32[]{:S(2)}) async-start(bf16[16,56,768]{2,1,0:T(8,128)(2,1)} %pad_maximum_fusion), calls=%async_computation.2 | async-start | bytes 2752512 | tf_op jit(solution)/shard_map/all_to_all | solution.py:193
  88.6 0.7 collective-permute-start.13
  89.3 1.5 %collective-permute-done.13 = bf16[256,768]{1,0:T(8,128)(2,1)} collective-permute-done((bf16[256,768]{1,0:T(8,128)(2,1)S(1)}, bf16[256,768]{1,0:T(8,128)(2,1)}, u32[]{:S(2)}, u32[]{:S(2)}) %collective-permute-start.13) | collective-permute-done | bytes 393248 | tf_op jit(solution)/shard_map/ppermute | solution.py:27
  90.8 1.1 fusion.16
  92.5 3.2 %collective-permute-start.18 = (bf16[32,768]{1,0:T(8,128)(2,1)S(1)}, bf16[32,768]{1,0:T(8,128)(2,1)S(1)}, u32[]{:S(2)}, u32[]{:S(2)}) collective-permute-start(bf16[32,768]{1,0:T(8,128)(2,1)S(1)} %get-tuple-element.82), channel_id=1, source_target_pairs={{0,20},{4,24},{8,28},{12,0},{16,4},{20,8},{24,12},{28,16},{1,21},{... | collective-permute-start | bytes 147464 | tf_op jit(solution)/shard_map/ppermute | solution.py:190
  95.7 2.2 %collective-permute-start.17 = (bf16[32,768]{1,0:T(8,128)(2,1)S(1)}, bf16[32,768]{1,0:T(8,128)(2,1)S(1)}, u32[]{:S(2)}, u32[]{:S(2)}) collective-permute-start(bf16[32,768]{1,0:T(8,128)(2,1)S(1)} %get-tuple-element.83), channel_id=1, source_target_pairs={{0,16},{4,20},{8,24},{12,28},{16,0},{20,4},{24,8},{28,12},{1,17},{... | collective-permute-start | bytes 147464 | tf_op jit(solution)/shard_map/ppermute | solution.py:190
  97.9 2.3 %collective-permute-start.16 = (bf16[32,768]{1,0:T(8,128)(2,1)S(1)}, bf16[32,768]{1,0:T(8,128)(2,1)S(1)}, u32[]{:S(2)}, u32[]{:S(2)}) collective-permute-start(bf16[32,768]{1,0:T(8,128)(2,1)S(1)} %get-tuple-element.84), channel_id=1, source_target_pairs={{0,12},{4,16},{8,20},{12,24},{16,28},{20,0},{24,4},{28,8},{1,13},{... | collective-permute-start | bytes 147464 | tf_op jit(solution)/shard_map/ppermute | solution.py:190
  100.2 1.3 collective-permute-start.15
  101.5 1.0 collective-permute-done.17
  102.5 5.0 %collective-permute-done.16 = bf16[32,768]{1,0:T(8,128)(2,1)S(1)} collective-permute-done((bf16[32,768]{1,0:T(8,128)(2,1)S(1)}, bf16[32,768]{1,0:T(8,128)(2,1)S(1)}, u32[]{:S(2)}, u32[]{:S(2)}) %collective-permute-start.16) | collective-permute-done | bytes 49184 | tf_op jit(solution)/shard_map/ppermute | solution.py:190
  107.5 2.0 %collective-permute-done.14 = bf16[32,768]{1,0:T(8,128)(2,1)S(1)} collective-permute-done((bf16[32,768]{1,0:T(8,128)(2,1)S(1)}, bf16[32,768]{1,0:T(8,128)(2,1)S(1)}, u32[]{:S(2)}, u32[]{:S(2)}) %collective-permute-start.14) | collective-permute-done | bytes 49184 | tf_op jit(solution)/shard_map/ppermute | solution.py:190
  109.6 0.6 all-to-all-done.2
  110.6 0.7 broadcast_in_dim.7
  111.4 3.4 %all-to-all-start.3 = ((bf16[8,24,768]{2,1,0:T(8,128)(2,1)}), bf16[8,24,768]{2,1,0:T(8,128)(2,1)S(1)}, u32[]{:S(2)}, u32[]{:S(2)}) async-start(bf16[8,24,768]{2,1,0:T(8,128)(2,1)} %broadcast_in_dim.7), calls=%async_computation.3 | async-start | bytes 589824 | tf_op jit(solution)/shard_map/all_to_all | solution.py:19
  114.9 2.9 %collective-permute-start.22 = (bf16[32,384]{1,0:T(8,128)(2,1)S(1)}, bf16[32,384]{1,0:T(8,128)(2,1)S(1)}, u32[]{:S(2)}, u32[]{:S(2)}) collective-permute-start(bf16[32,384]{1,0:T(8,128)(2,1)S(1)} %bitcast.232), channel_id=1, source_target_pairs={{0,2},{2,0},{1,3},{3,1},{4,6},{6,4},{5,7},{7,5},{8,10},{10,8},{9,1... | collective-permute-start | bytes 73736 | tf_op jit(solution)/shard_map/ppermute | solution.py:27
  117.8 2.3 %collective-permute-start.21 = (bf16[32,768]{1,0:T(8,128)(2,1)S(1)}, bf16[32,768]{1,0:T(8,128)(2,1)S(1)}, u32[]{:S(2)}, u32[]{:S(2)}) collective-permute-start(bf16[32,768]{1,0:T(8,128)(2,1)S(1)} %slice_reduce_fusion), channel_id=1, source_target_pairs={{0,1},{1,0},{2,3},{3,2},{4,5},{5,4},{6,7},{7,6},{8,9},{9,8},{10,11... | collective-permute-start | bytes 147464 | tf_op jit(solution)/shard_map/ppermute | solution.py:27
  120.2 0.9 collective-permute-start.23
  121.1 3.5 %collective-permute-done.23 = f32[4,2,8]{2,0,1:T(4,128)S(1)} collective-permute-done((f32[4,2,8]{2,0,1:T(4,128)S(1)}, f32[4,2,8]{2,0,1:T(4,128)S(1)}, u32[]{:S(2)}, u32[]{:S(2)}) %collective-permute-start.23) | collective-permute-done | bytes 288 | tf_op jit(solution)/shard_map/ppermute | solution.py:27
  124.6 0.7 maximum_select_fusion.5
  125.3 3.8 %collective-permute-start.24 = (bf16[2,32,384]{2,1,0:T(8,128)(2,1)S(1)}, bf16[2,32,384]{2,1,0:T(8,128)(2,1)S(1)}, u32[]{:S(2)}, u32[]{:S(2)}) collective-permute-start(bf16[2,32,384]{2,1,0:T(8,128)(2,1)S(1)} %maximum_select_fusion.7), channel_id=1, source_target_pairs={{0,1},{1,0},{2,3},{3,2},{4,5},{5,4},{6,7},{7,6},{8,9},{9,8},{10,11... | collective-permute-start | bytes 147464 | tf_op jit(solution)/shard_map/ppermute | solution.py:27
  129.1 0.7 broadcast_in_dim.8
  129.8 5.1 %all-to-all-start.4 = ((bf16[8,48,384]{2,1,0:T(8,128)(2,1)}), bf16[8,48,384]{2,1,0:T(8,128)(2,1)S(1)}, u32[]{:S(2)}, u32[]{:S(2)}) async-start(bf16[8,48,384]{2,1,0:T(8,128)(2,1)} %broadcast_in_dim.8), calls=%async_computation.4 | async-start | bytes 589824 | tf_op jit(solution)/shard_map/all_to_all | solution.py:19
  135.0 0.6 select_n.140
  135.6 0.7 copy.88
  136.2 5.8 %all-to-all-done.4 = bf16[8,48,384]{2,1,0:T(8,128)(2,1)S(1)} async-done(((bf16[8,48,384]{2,1,0:T(8,128)(2,1)}), bf16[8,48,384]{2,1,0:T(8,128)(2,1)S(1)}, u32[]{:S(2)}, u32[]{:S(2)}) %all-to-all-start.4) | async-done | bytes 294944 | tf_op jit(solution)/shard_map/all_to_all | solution.py:19
  142.0 2.9 %all_gather.3 = bf16[768,384]{1,0:T(8,128)(2,1)S(1)} all-gather(bf16[384,384]{1,0:T(8,128)(2,1)S(1)} %bitcast.217), channel_id=1, replica_groups=mesh['yl'=2,'x'=4,'z'=8,'yh'=2,'c'=2] {'c'}, dimensions={0}, use_global_device_ids=true | all-gather | bytes 884736 | tf_op jit(solution)/shard_map/all_gather | solution.py:232
  144.9 1.1 convert_element_type.94
  (101 shorter events, 4.9 us)
Async XLA Ops:
  0.6 20.3 %copy-start = (bf16[128,768]{1,0:T(8,128)(2,1)S(1)}, bf16[128,768]{1,0:T(8,128)(2,1)}, u32[]{:S(2)}) copy-start(bf16[128,768]{1,0:T(8,128)(2,1)} %param.6) | copy-start | bytes 589828
  1.7 9.3 %collective-permute-start = (bf16[384,384]{1,0:T(8,128)(2,1)S(1)}, bf16[384,384]{1,0:T(8,128)(2,1)S(1)}, u32[]{:S(2)}, u32[]{:S(2)}) collective-permute-start(bf16[384,384]{1,0:T(8,128)(2,1)S(1)} %dynamic-slice_bitcast_fusion), channel_id=1, source_target_pairs={{0,130},{2,128},{128,2},{130,0},{1,131},{3,129},{129,3},{131,1},{4... | collective-permute-start | bytes 884744 | tf_op jit(solution)/shard_map/ppermute | solution.py:110
  5.3 0.9 copy-start.5
  6.2 0.8 copy-start.6
  8.5 9.8 %copy-start.11 = (bf16[64,1024]{1,0:T(8,128)(2,1)S(1)}, bf16[64,1024]{1,0:T(8,128)(2,1)}, u32[]{:S(2)}) copy-start(bf16[64,1024]{1,0:T(8,128)(2,1)} %param.9) | copy-start | bytes 393220
  11.0 35.5 %all-to-all-start = ((bf16[16,32,1792]{2,1,0:T(8,128)(2,1)}), bf16[16,32,1792]{2,1,0:T(8,128)(2,1)}, u32[]{:S(2)}, u32[]{:S(2)}) async-start(bf16[16,32,1792]{2,1,0:T(8,128)(2,1)} %shard_map.93), calls=%async_computation | async-start | bytes 3670016 | tf_op jit(solution)/shard_map/all_to_all | solution.py:112
  18.4 2.8 %collective-permute-start.2 = (bf16[2,16,1024]{2,1,0:T(8,128)(2,1)S(1)}, bf16[2,16,1024]{2,1,0:T(8,128)(2,1)S(1)}, u32[]{:S(2)}, u32[]{:S(2)}) collective-permute-start(bf16[2,16,1024]{2,1,0:T(8,128)(2,1)S(1)} %get-tuple-element.93), channel_id=1, source_target_pairs={{0,1},{1,0},{2,3},{3,2},{4,5},{5,4},{6,7},{7,6},{8,9},{9,8},{10,11... | collective-permute-start | bytes 196616 | tf_op jit(solution)/shard_map/ppermute | solution.py:27
  21.6 16.6 %collective-permute-start.5 = (bf16[64,1792]{1,0:T(8,128)(2,1)S(1)}, bf16[64,1792]{1,0:T(8,128)(2,1)S(1)}, u32[]{:S(2)}, u32[]{:S(2)}) collective-permute-start(bf16[64,1792]{1,0:T(8,128)(2,1)S(1)} %bitcast.205), channel_id=1, source_target_pairs={{0,12},{4,16},{8,20},{12,24},{16,28},{20,0},{24,4},{28,8},{1,21},{... | collective-permute-start | bytes 688136 | tf_op jit(solution)/shard_map/ppermute | solution.py:33
  28.2 12.8 %collective-permute-start.4 = (bf16[64,1792]{1,0:T(8,128)(2,1)S(1)}, bf16[64,1792]{1,0:T(8,128)(2,1)S(1)}, u32[]{:S(2)}, u32[]{:S(2)}) collective-permute-start(bf16[64,1792]{1,0:T(8,128)(2,1)S(1)} %bitcast.206), channel_id=1, source_target_pairs={{0,8},{4,12},{8,16},{12,20},{16,24},{20,28},{24,0},{28,4},{1,25},{... | collective-permute-start | bytes 688136 | tf_op jit(solution)/shard_map/ppermute | solution.py:33
  28.4 15.0 %collective-permute-start.3 = (bf16[64,1792]{1,0:T(8,128)(2,1)S(1)}, bf16[64,1792]{1,0:T(8,128)(2,1)S(1)}, u32[]{:S(2)}, u32[]{:S(2)}) collective-permute-start(bf16[64,1792]{1,0:T(8,128)(2,1)S(1)} %bitcast.207), channel_id=1, source_target_pairs={{0,4},{4,8},{8,12},{12,16},{16,20},{20,24},{24,28},{28,0},{1,29},{... | collective-permute-start | bytes 688136 | tf_op jit(solution)/shard_map/ppermute | solution.py:33
  28.9 17.7 %collective-permute-start.1 = (bf16[384,384]{1,0:T(8,128)(2,1)S(1)}, bf16[384,384]{1,0:T(8,128)(2,1)S(1)}, u32[]{:S(2)}, u32[]{:S(2)}) collective-permute-start(bf16[384,384]{1,0:T(8,128)(2,1)S(1)} %collective-permute-done), channel_id=1, source_target_pairs={{0,1},{1,0},{2,3},{3,2},{4,5},{5,4},{6,7},{7,6},{8,9},{9,8},{10,11... | collective-permute-start | bytes 884744 | tf_op jit(solution)/shard_map/ppermute | solution.py:27
  38.3 6.4 %collective-permute-start.9 = (bf16[32,1792]{1,0:T(8,128)(2,1)S(1)}, bf16[32,1792]{1,0:T(8,128)(2,1)S(1)}, u32[]{:S(2)}, u32[]{:S(2)}) collective-permute-start(bf16[32,1792]{1,0:T(8,128)(2,1)S(1)} %dynamic-slice_bitcast_fusion.1), channel_id=1, source_target_pairs={{0,4},{4,8},{8,12},{12,16},{16,20},{20,24},{24,28},{28,0},{1,29},{... | collective-permute-start | bytes 344072 | tf_op jit(solution)/shard_map/ppermute | solution.py:33
  39.1 7.4 %collective-permute-start.8 = (bf16[64,1792]{1,0:T(8,128)(2,1)S(1)}, bf16[64,1792]{1,0:T(8,128)(2,1)S(1)}, u32[]{:S(2)}, u32[]{:S(2)}) collective-permute-start(bf16[64,1792]{1,0:T(8,128)(2,1)S(1)} %collective-permute-done.5.refs_0_), channel_id=1, source_target_pairs={{0,1},{1,0},{2,3},{3,2},{4,5},{5,4},{6,7},{7,6},{8,9},{9,8},{10,11... | collective-permute-start | bytes 688136 | tf_op jit(solution)/shard_map/ppermute | solution.py:27
  41.0 5.6 %collective-permute-start.7 = (bf16[64,1792]{1,0:T(8,128)(2,1)S(1)}, bf16[64,1792]{1,0:T(8,128)(2,1)S(1)}, u32[]{:S(2)}, u32[]{:S(2)}) collective-permute-start(bf16[64,1792]{1,0:T(8,128)(2,1)S(1)} %collective-permute-done.4.refs_1_), channel_id=1, source_target_pairs={{0,1},{1,0},{2,3},{3,2},{4,5},{5,4},{6,7},{7,6},{8,9},{9,8},{10,11... | collective-permute-start | bytes 688136 | tf_op jit(solution)/shard_map/ppermute | solution.py:27
  43.4 3.1 %collective-permute-start.6 = (bf16[64,1792]{1,0:T(8,128)(2,1)S(1)}, bf16[64,1792]{1,0:T(8,128)(2,1)S(1)}, u32[]{:S(2)}, u32[]{:S(2)}) collective-permute-start(bf16[64,1792]{1,0:T(8,128)(2,1)S(1)} %collective-permute-done.3.refs_2_), channel_id=1, source_target_pairs={{0,1},{1,0},{2,3},{3,2},{4,5},{5,4},{6,7},{7,6},{8,9},{9,8},{10,11... | collective-permute-start | bytes 688136 | tf_op jit(solution)/shard_map/ppermute | solution.py:27
  44.6 1.9 %collective-permute-start.10 = (bf16[32,1792]{1,0:T(8,128)(2,1)S(1)}, bf16[32,1792]{1,0:T(8,128)(2,1)S(1)}, u32[]{:S(2)}, u32[]{:S(2)}) collective-permute-start(bf16[32,1792]{1,0:T(8,128)(2,1)S(1)} %collective-permute-done.9.refs_7_), channel_id=1, source_target_pairs={{0,1},{1,0},{2,3},{3,2},{4,5},{5,4},{6,7},{7,6},{8,9},{9,8},{10,11... | collective-permute-start | bytes 344072 | tf_op jit(solution)/shard_map/ppermute | solution.py:27
  46.5 0.6 copy-start.3
  46.5 0.7 copy-start.1
  47.2 0.9 copy-start.2
  48.2 0.9 copy-start.4
  49.3 2.1 %copy-start.10 = (bf16[768,384]{1,0:T(8,128)(2,1)S(1)}, bf16[768,384]{1,0:T(8,128)(2,1)}, u32[]{:S(2)}) copy-start(bf16[768,384]{1,0:T(8,128)(2,1)} %param.8) | copy-start | bytes 1769476
  51.4 3.4 %copy-start.9 = (f32[512,512]{1,0:T(8,128)}, f32[512,512]{1,0:T(8,128)S(1)}, u32[]{:S(2)}) copy-start(f32[512,512]{1,0:T(8,128)S(1)} %get-tuple-element.106) | copy-start | bytes 3145732
  52.3 2.4 %copy-start.7 = (f32[512,768]{1,0:T(8,128)}, f32[512,768]{1,0:T(8,128)S(1)}, u32[]{:S(2)}) copy-start(f32[512,768]{1,0:T(8,128)S(1)} %get-tuple-element.104) | copy-start | bytes 4718596
  55.9 14.3 %all-to-all-start.1 = ((f32[8,8,512]{2,1,0:T(8,128)}), f32[8,8,512]{2,1,0:T(8,128)S(1)}, u32[]{:S(2)}, u32[]{:S(2)}) async-start(f32[8,8,512]{2,1,0:T(8,128)} %broadcast_in_dim.6), calls=%async_computation.1 | async-start | bytes 262144 | tf_op jit(solution)/shard_map/all_to_all | solution.py:19
  70.3 6.0 %collective-permute-start.11 = (f32[8,512]{1,0:T(8,128)S(1)}, f32[8,512]{1,0:T(8,128)S(1)}, u32[]{:S(2)}, u32[]{:S(2)}) collective-permute-start(f32[8,512]{1,0:T(8,128)S(1)} %stack.131), channel_id=1, source_target_pairs={{0,1},{1,0},{2,3},{3,2},{4,5},{5,4},{6,7},{7,6},{8,9},{9,8},{10,11... | collective-permute-start | bytes 49160 | tf_op jit(solution)/shard_map/ppermute | solution.py:27
  78.0 1.9 %copy-start.8 = (f32[512,768]{1,0:T(8,128)S(1)}, f32[512,768]{1,0:T(8,128)}, u32[]{:S(2)}) copy-start(f32[512,768]{1,0:T(8,128)} %copy-done.7) | copy-start | bytes 4718596
  80.7 2.1 %collective-permute-start.12 = (bf16[384,768]{1,0:T(8,128)(2,1)S(1)}, bf16[384,768]{1,0:T(8,128)(2,1)S(1)}, u32[]{:S(2)}, u32[]{:S(2)}) collective-permute-start(bf16[384,768]{1,0:T(8,128)(2,1)S(1)} %fusion.19), channel_id=1, source_target_pairs={{0,1},{1,0},{2,3},{3,2},{4,5},{5,4},{6,7},{7,6},{8,9},{9,8},{10,11... | collective-permute-start | bytes 1769480 | tf_op jit(solution)/shard_map/ppermute | solution.py:27
  84.4 25.8 %all-to-all-start.2 = ((bf16[16,56,768]{2,1,0:T(8,128)(2,1)}), bf16[16,56,768]{2,1,0:T(8,128)(2,1)S(1)}, u32[]{:S(2)}, u32[]{:S(2)}) async-start(bf16[16,56,768]{2,1,0:T(8,128)(2,1)} %pad_maximum_fusion), calls=%async_computation.2 | async-start | bytes 2752512 | tf_op jit(solution)/shard_map/all_to_all | solution.py:193
  88.6 2.2 %collective-permute-start.13 = (bf16[256,768]{1,0:T(8,128)(2,1)S(1)}, bf16[256,768]{1,0:T(8,128)(2,1)}, u32[]{:S(2)}, u32[]{:S(2)}) collective-permute-start(bf16[256,768]{1,0:T(8,128)(2,1)S(1)} %slice.230), channel_id=1, source_target_pairs={{0,1},{1,0},{2,3},{3,2},{4,5},{5,4},{6,7},{7,6},{8,9},{9,8},{10,11... | collective-permute-start | bytes 1179656 | tf_op jit(solution)/shard_map/ppermute | solution.py:27
  92.0 8.1 %collective-permute-start.20 = (bf16[32,768]{1,0:T(8,128)(2,1)S(1)}, bf16[32,768]{1,0:T(8,128)(2,1)S(1)}, u32[]{:S(2)}, u32[]{:S(2)}) collective-permute-start(bf16[32,768]{1,0:T(8,128)(2,1)S(1)} %get-tuple-element.80), channel_id=1, source_target_pairs={{0,28},{4,0},{8,4},{12,8},{16,12},{20,16},{24,20},{28,24},{1,29},{... | collective-permute-start | bytes 147464 | tf_op jit(solution)/shard_map/ppermute | solution.py:190
  92.1 9.3 %collective-permute-start.19 = (bf16[32,768]{1,0:T(8,128)(2,1)S(1)}, bf16[32,768]{1,0:T(8,128)(2,1)S(1)}, u32[]{:S(2)}, u32[]{:S(2)}) collective-permute-start(bf16[32,768]{1,0:T(8,128)(2,1)S(1)} %get-tuple-element.81), channel_id=1, source_target_pairs={{0,24},{4,28},{8,0},{12,4},{16,8},{20,12},{24,16},{28,20},{1,25},{... | collective-permute-start | bytes 147464 | tf_op jit(solution)/shard_map/ppermute | solution.py:190
  92.5 9.0 %collective-permute-start.18 = (bf16[32,768]{1,0:T(8,128)(2,1)S(1)}, bf16[32,768]{1,0:T(8,128)(2,1)S(1)}, u32[]{:S(2)}, u32[]{:S(2)}) collective-permute-start(bf16[32,768]{1,0:T(8,128)(2,1)S(1)} %get-tuple-element.82), channel_id=1, source_target_pairs={{0,20},{4,24},{8,28},{12,0},{16,4},{20,8},{24,12},{28,16},{1,21},{... | collective-permute-start | bytes 147464 | tf_op jit(solution)/shard_map/ppermute | solution.py:190
  95.7 6.8 %collective-permute-start.17 = (bf16[32,768]{1,0:T(8,128)(2,1)S(1)}, bf16[32,768]{1,0:T(8,128)(2,1)S(1)}, u32[]{:S(2)}, u32[]{:S(2)}) collective-permute-start(bf16[32,768]{1,0:T(8,128)(2,1)S(1)} %get-tuple-element.83), channel_id=1, source_target_pairs={{0,16},{4,20},{8,24},{12,28},{16,0},{20,4},{24,8},{28,12},{1,17},{... | collective-permute-start | bytes 147464 | tf_op jit(solution)/shard_map/ppermute | solution.py:190
  97.9 9.6 %collective-permute-start.16 = (bf16[32,768]{1,0:T(8,128)(2,1)S(1)}, bf16[32,768]{1,0:T(8,128)(2,1)S(1)}, u32[]{:S(2)}, u32[]{:S(2)}) collective-permute-start(bf16[32,768]{1,0:T(8,128)(2,1)S(1)} %get-tuple-element.84), channel_id=1, source_target_pairs={{0,12},{4,16},{8,20},{12,24},{16,28},{20,0},{24,4},{28,8},{1,13},{... | collective-permute-start | bytes 147464 | tf_op jit(solution)/shard_map/ppermute | solution.py:190
  100.2 7.4 %collective-permute-start.15 = (bf16[32,768]{1,0:T(8,128)(2,1)S(1)}, bf16[32,768]{1,0:T(8,128)(2,1)S(1)}, u32[]{:S(2)}, u32[]{:S(2)}) collective-permute-start(bf16[32,768]{1,0:T(8,128)(2,1)S(1)} %get-tuple-element.85), channel_id=1, source_target_pairs={{0,8},{4,12},{8,16},{12,20},{16,24},{20,28},{24,0},{28,4},{1,9},{5... | collective-permute-start | bytes 147464 | tf_op jit(solution)/shard_map/ppermute | solution.py:190
  101.5 8.1 %collective-permute-start.14 = (bf16[32,768]{1,0:T(8,128)(2,1)S(1)}, bf16[32,768]{1,0:T(8,128)(2,1)S(1)}, u32[]{:S(2)}, u32[]{:S(2)}) collective-permute-start(bf16[32,768]{1,0:T(8,128)(2,1)S(1)} %get-tuple-element.86), channel_id=1, source_target_pairs={{0,4},{4,8},{8,12},{12,16},{16,20},{20,24},{24,28},{28,0},{1,5},{5... | collective-permute-start | bytes 147464 | tf_op jit(solution)/shard_map/ppermute | solution.py:190
  111.4 13.2 %all-to-all-start.3 = ((bf16[8,24,768]{2,1,0:T(8,128)(2,1)}), bf16[8,24,768]{2,1,0:T(8,128)(2,1)S(1)}, u32[]{:S(2)}, u32[]{:S(2)}) async-start(bf16[8,24,768]{2,1,0:T(8,128)(2,1)} %broadcast_in_dim.7), calls=%async_computation.3 | async-start | bytes 589824 | tf_op jit(solution)/shard_map/all_to_all | solution.py:19
  114.9 9.6 %collective-permute-start.22 = (bf16[32,384]{1,0:T(8,128)(2,1)S(1)}, bf16[32,384]{1,0:T(8,128)(2,1)S(1)}, u32[]{:S(2)}, u32[]{:S(2)}) collective-permute-start(bf16[32,384]{1,0:T(8,128)(2,1)S(1)} %bitcast.232), channel_id=1, source_target_pairs={{0,2},{2,0},{1,3},{3,1},{4,6},{6,4},{5,7},{7,5},{8,10},{10,8},{9,1... | collective-permute-start | bytes 73736 | tf_op jit(solution)/shard_map/ppermute | solution.py:27
  117.8 6.7 %collective-permute-start.21 = (bf16[32,768]{1,0:T(8,128)(2,1)S(1)}, bf16[32,768]{1,0:T(8,128)(2,1)S(1)}, u32[]{:S(2)}, u32[]{:S(2)}) collective-permute-start(bf16[32,768]{1,0:T(8,128)(2,1)S(1)} %slice_reduce_fusion), channel_id=1, source_target_pairs={{0,1},{1,0},{2,3},{3,2},{4,5},{5,4},{6,7},{7,6},{8,9},{9,8},{10,11... | collective-permute-start | bytes 147464 | tf_op jit(solution)/shard_map/ppermute | solution.py:27
  120.2 4.3 %collective-permute-start.23 = (f32[4,2,8]{2,0,1:T(4,128)S(1)}, f32[4,2,8]{2,0,1:T(4,128)S(1)}, u32[]{:S(2)}, u32[]{:S(2)}) collective-permute-start(f32[4,2,8]{2,0,1:T(4,128)S(1)} %fusion.41), channel_id=1, source_target_pairs={{0,2},{2,0},{1,3},{3,1},{4,6},{6,4},{5,7},{7,5},{8,10},{10,8},{9,1... | collective-permute-start | bytes 776 | tf_op jit(solution)/shard_map/ppermute | solution.py:27
  125.3 10.3 %collective-permute-start.24 = (bf16[2,32,384]{2,1,0:T(8,128)(2,1)S(1)}, bf16[2,32,384]{2,1,0:T(8,128)(2,1)S(1)}, u32[]{:S(2)}, u32[]{:S(2)}) collective-permute-start(bf16[2,32,384]{2,1,0:T(8,128)(2,1)S(1)} %maximum_select_fusion.7), channel_id=1, source_target_pairs={{0,1},{1,0},{2,3},{3,2},{4,5},{5,4},{6,7},{7,6},{8,9},{9,8},{10,11... | collective-permute-start | bytes 147464 | tf_op jit(solution)/shard_map/ppermute | solution.py:27
  129.8 12.2 %all-to-all-start.4 = ((bf16[8,48,384]{2,1,0:T(8,128)(2,1)}), bf16[8,48,384]{2,1,0:T(8,128)(2,1)S(1)}, u32[]{:S(2)}, u32[]{:S(2)}) async-start(bf16[8,48,384]{2,1,0:T(8,128)(2,1)} %broadcast_in_dim.8), calls=%async_computation.4 | async-start | bytes 589824 | tf_op jit(solution)/shard_map/all_to_all | solution.py:19

commit v4 on v3

--- a/solution.py
+++ b/solution.py
@@ -191,7 +191,7 @@
     ]
     sent = jnp.concatenate([text_part.reshape(16, 32, width), share], 1)
     sent = lax.all_to_all(sent, COLS, 0, 0, tiled=True)
-    sent, losses, *round_z = lax.optimization_barrier((sent, losses, *round_z))
+    sent, losses = lax.optimization_barrier((sent, losses))
     grad = turned[0].astype(f32) + sum(r.astype(f32) for r in round_z)
     share = jnp.sum(sent[:, 32:].astype(f32), axis=0).astype(bf16)
     share = to_all(share, "z", 8)
@@ -229,7 +229,10 @@
     share, row_loss, image_grad, text_grad = lax.optimization_barrier(
         (share, row_loss, image_grad, text_grad)
     )
-    weight_grad = lax.all_gather(share, "c", axis=0, tiled=True).astype(f32)
+    come = swap(share, "c")
+    weight_grad = jnp.where(
+        core == 0, jnp.concatenate([share, come], 0), jnp.concatenate([come, share], 0)
+    ).astype(f32)
     return row_loss, image_grad, text_grad, weight_grad
 
 

time: 147 us -> 145 us (0.986)
  starting transfers between devices: 71 us -> 74.3 us
  blocking collectives: 2.92 us -> 0 us
  waiting for transfers between devices: 42.9 us -> 40.9 us
    ppermute x7, waiting for transfers between devices: 8.07 us -> 4.49 us  [shards(): lax.ppermute(turned[k], 'z', [(i, (i + k) % 8) for i in range(8)])]
    all_gather x1 -> x0, blocking collectives: 2.92 us -> none  [shards(): weight_grad = lax.all_gather(share, 'c', axis=0, tiled=True).astype(f32)]
    all_to_all x3, waiting for transfers between devices: 13.6 us -> 16.5 us  [to_all(): return lax.all_to_all(sent, axes, 0, 0, tiled=True)]
    ppermute x13 -> x14, starting transfers between devices: 23.6 us -> 26 us  [swap(): return lax.ppermute(value, axis, [(0, 1), (1, 0)])]
    ppermute x13 -> x14, waiting for transfers between devices: 7.68 us -> 5.66 us  [swap(): return lax.ppermute(value, axis, [(0, 1), (1, 0)])]
    ppermute x7, starting transfers between devices: 9.43 us -> 11.1 us  [shards(): lax.ppermute(turned[k], 'z', [(i, (i + k) % 8) for i in range(8)])]
  transfers between devices with their start and end apart: 30 -> 31, of which waited for: 17 -> 16; matrix products, arithmetic and copies ran while one was open for 3% -> 5% of each run, Pallas kernels for 1% -> 1%
where the time goes in v4:
time: 145 us; the launch traced here: 144 us
  starting transfers between devices  74.3 us (51%)
  waiting for transfers between devices  40.9 us (28%)
  local copies, waits for them, and re-layouts  9.48 us (7%)
  matrix products  8.34 us (6%)
  other arithmetic  7.93 us (5%)
  between operations  1.8 us (1%)
  Pallas kernels  1.63 us (1%)
    ppermute x14, starting transfers between devices, swap(): return lax.ppermute(value, axis, [(0, 1), (1, 0)])  26 us
    all_to_all x3, waiting for transfers between devices, to_all(): return lax.all_to_all(sent, axes, 0, 0, tiled=True)  16.5 us
    all_to_all x3, starting transfers between devices, to_all(): return lax.all_to_all(sent, axes, 0, 0, tiled=True)  14.1 us
    ppermute x7, starting transfers between devices, shards(): lax.ppermute(turned[k], 'z', [(i, (i + k) % 8) for i in range(8)])  11.1 us
    ppermute x4, waiting for transfers between devices, turn(): return lax.ppermute(value, ('z', 'c'), pairs)  10.3 us
    dot_general x6, matrix products, dot(): lax.dot_general(left, right, (((left_dim,), (right_dim,)), ((), ())), pre...  8.34 us
    ppermute x4, starting transfers between devices, turn(): return lax.ppermute(value, ('z', 'c'), pairs)  8.11 us
    all_to_all x1, starting transfers between devices, shards(): cols = lax.all_to_all(sent, COLS, 0, 0, tiled=True)  7.3 us
  transfers between devices with their start and end apart: 31, of which 16 were waited for; matrix products, arithmetic and copies ran while one was open for 5% of the time, Pallas kernels for 1%

profile of v4, /device:TPU:1, one launch (start us, length us, event | category | flops | bytes accessed | tf_op | source)
XLA Modules:
  0.0 144.4 jit_solution(1997272323266459066)
XLA Ops:
  0.7 1.0 dynamic-slice_bitcast_fusion
  1.7 3.7 %collective-permute-start = (bf16[384,384]{1,0:T(8,128)(2,1)S(1)}, bf16[384,384]{1,0:T(8,128)(2,1)S(1)}, u32[]{:S(2)}, u32[]{:S(2)}) collective-permute-start(bf16[384,384]{1,0:T(8,128)(2,1)S(1)} %dynamic-slice_bitcast_fusion), channel_id=1, source_target_pairs={{0,130},{2,128},{128,2},{130,0},{1,131},{3,129},{129,3},{131,1},{4... | collective-permute-start | bytes 884744 | tf_op jit(solution)/shard_map/ppermute | solution.py:110
  5.3 0.9 copy-done.5
  6.2 0.8 copy-done.6
  7.1 1.4 shard_map.93
  8.5 2.5 %collective-permute-done = bf16[384,384]{1,0:T(8,128)(2,1)S(1)} collective-permute-done((bf16[384,384]{1,0:T(8,128)(2,1)S(1)}, bf16[384,384]{1,0:T(8,128)(2,1)S(1)}, u32[]{:S(2)}, u32[]{:S(2)}) %collective-permute-start) | collective-permute-done | bytes 294944 | tf_op jit(solution)/shard_map/ppermute | solution.py:110
  11.0 7.3 %all-to-all-start = ((bf16[16,32,1792]{2,1,0:T(8,128)(2,1)}), bf16[16,32,1792]{2,1,0:T(8,128)(2,1)}, u32[]{:S(2)}, u32[]{:S(2)}) async-start(bf16[16,32,1792]{2,1,0:T(8,128)(2,1)} %shard_map.93), calls=%async_computation | async-start | bytes 3670016 | tf_op jit(solution)/shard_map/all_to_all | solution.py:112
  18.4 1.9 %collective-permute-start.2 = (bf16[2,16,1024]{2,1,0:T(8,128)(2,1)S(1)}, bf16[2,16,1024]{2,1,0:T(8,128)(2,1)S(1)}, u32[]{:S(2)}, u32[]{:S(2)}) collective-permute-start(bf16[2,16,1024]{2,1,0:T(8,128)(2,1)S(1)} %get-tuple-element.79), channel_id=1, source_target_pairs={{0,1},{1,0},{2,3},{3,2},{4,5},{5,4},{6,7},{7,6},{8,9},{9,8},{10,11... | collective-permute-start | bytes 196616 | tf_op jit(solution)/shard_map/ppermute | solution.py:27
  21.2 0.4 fusion.24
  21.6 6.5 %collective-permute-start.5 = (bf16[64,1792]{1,0:T(8,128)(2,1)S(1)}, bf16[64,1792]{1,0:T(8,128)(2,1)S(1)}, u32[]{:S(2)}, u32[]{:S(2)}) collective-permute-start(bf16[64,1792]{1,0:T(8,128)(2,1)S(1)} %bitcast.205), channel_id=1, source_target_pairs={{0,12},{4,16},{8,20},{12,24},{16,28},{20,0},{24,4},{28,8},{1,21},{... | collective-permute-start | bytes 688136 | tf_op jit(solution)/shard_map/ppermute | solution.py:33
  28.4 0.5 collective-permute-start.3
  28.9 2.4 %collective-permute-start.1 = (bf16[384,384]{1,0:T(8,128)(2,1)S(1)}, bf16[384,384]{1,0:T(8,128)(2,1)S(1)}, u32[]{:S(2)}, u32[]{:S(2)}) collective-permute-start(bf16[384,384]{1,0:T(8,128)(2,1)S(1)} %collective-permute-done), channel_id=1, source_target_pairs={{0,1},{1,0},{2,3},{3,2},{4,5},{5,4},{6,7},{7,6},{8,9},{9,8},{10,11... | collective-permute-start | bytes 884744 | tf_op jit(solution)/shard_map/ppermute | solution.py:27
  31.3 7.0 %collective-permute-done.5.refs_0_ = bf16[64,1792]{1,0:T(8,128)(2,1)S(1)} collective-permute-done((bf16[64,1792]{1,0:T(8,128)(2,1)S(1)}, bf16[64,1792]{1,0:T(8,128)(2,1)S(1)}, u32[]{:S(2)}, u32[]{:S(2)}) %collective-permute-start.5) | collective-permute-done | bytes 229408 | tf_op jit(solution)/shard_map/ppermute | solution.py:33
  38.3 0.8 collective-permute-start.9
  39.1 1.8 %collective-permute-done.4.refs_1_ = bf16[64,1792]{1,0:T(8,128)(2,1)S(1)} collective-permute-done((bf16[64,1792]{1,0:T(8,128)(2,1)S(1)}, bf16[64,1792]{1,0:T(8,128)(2,1)S(1)}, u32[]{:S(2)}, u32[]{:S(2)}) %collective-permute-start.4) | collective-permute-done | bytes 229408 | tf_op jit(solution)/shard_map/ppermute | solution.py:33
  41.0 1.3 collective-permute-start.7
  42.3 1.2 collective-permute-done.3.refs_2_
  43.4 0.9 collective-permute-start.6
  44.6 0.9 collective-permute-start.10
  45.6 1.0 collective-permute-done.10.refs_8_
  47.2 0.9 copy-done.2
  48.2 0.9 copy-done.4
  49.3 2.0 %fusion.58 = (f32[512]{0:T(512)S(1)}, f32[512,512]{1,0:T(8,128)S(1)}) fusion(bf16[512,1792]{1,0:T(8,128)(2,1)S(1)} %bitcast.202, bf16[512,1792]{1,0:T(8,128)(2,1)} %bitcast.15), kind=kOutput, calls=%fused_computation.146 | convolution fusion | flops 537394688 | bytes 3147776 | tf_op jit(solution)/shard_map/dot_general | solution.py:86
  51.4 0.9 multiply_reduce_fusion
  52.3 2.4 %fusion.59 = (f32[512]{0:T(512)S(1)}, f32[512,512]{1,0:T(8,128)S(1)}) fusion(f32[512,768]{1,0:T(8,128)S(1)} %get-tuple-element.90, f32[512]{0:T(512)S(1)} %add_rsqrt_fusion, bf16[512,1792]{1,0:T(8,128)(2,1)} %bitcast.15), kind=kOutput, calls=%fused_computation.147 | convolution fusion | flops 403963392 | bytes 3411968 | tf_op jit(solution)/shard_map/dot_general | solution.py:86
  54.7 0.4 multiply_reduce_fusion.1
  55.2 0.7 broadcast_in_dim.6
  55.9 6.3 %all-to-all-start.1 = ((f32[8,8,512]{2,1,0:T(8,128)}), f32[8,8,512]{2,1,0:T(8,128)S(1)}, u32[]{:S(2)}, u32[]{:S(2)}) async-start(f32[8,8,512]{2,1,0:T(8,128)} %broadcast_in_dim.6), calls=%async_computation.1 | async-start | bytes 262144 | tf_op jit(solution)/shard_map/all_to_all | solution.py:19
  62.3 7.8 %all-to-all-done.1 = f32[8,8,512]{2,1,0:T(8,128)S(1)} async-done(((f32[8,8,512]{2,1,0:T(8,128)}), f32[8,8,512]{2,1,0:T(8,128)S(1)}, u32[]{:S(2)}, u32[]{:S(2)}) %all-to-all-start.1) | async-done | bytes 131104 | tf_op jit(solution)/shard_map/all_to_all | solution.py:19
  70.3 5.2 %collective-permute-start.11 = (f32[8,512]{1,0:T(8,128)S(1)}, f32[8,512]{1,0:T(8,128)S(1)}, u32[]{:S(2)}, u32[]{:S(2)}) collective-permute-start(f32[8,512]{1,0:T(8,128)S(1)} %stack.131), channel_id=1, source_target_pairs={{0,1},{1,0},{2,3},{3,2},{4,5},{5,4},{6,7},{7,6},{8,9},{9,8},{10,11... | collective-permute-start | bytes 49160 | tf_op jit(solution)/shard_map/ppermute | solution.py:27
  75.8 0.6 collective-permute-done.11
  76.5 1.5 %multiply_convert_fusion.2 = bf16[512,512]{1,0:T(8,128)(2,1)S(1)} fusion(f32[512,512]{1,0:T(8,128)} %copy-done.9, f32[512,512]{1,0:T(8,128)S(1)} %get-tuple-element.94, f32[512]{0:T(512)S(1)} %get-tuple-element.88, f32[512]{0:T(512)S(1)} %get-tuple-element.61), kind=kLoop, calls=%fused_computation.25 | loop fusion | flops 1310720 | bytes 2625536 | tf_op jit(solution)/shard_map/convert_element_type | solution.py:164
  78.0 1.8 %convolution_multiply_fusion = f32[512,768]{1,0:T(8,128)S(1)} fusion(bf16[512,512]{1,0:T(8,128)(2,1)S(1)} %multiply_convert_fusion.2, bf16[512,1792]{1,0:T(8,128)(2,1)} %bitcast.15), kind=kOutput, calls=%fused_computation.4 | convolution fusion | flops 403046400 | bytes 2883584 | tf_op jit(solution)/shard_map/dot_general | solution.py:86
  80.2 0.5 fusion.60
  80.7 0.4 collective-permute-start.12
  81.4 0.7 multiply_convert_fusion
  82.1 0.7 collective-permute-done.12
  83.2 1.2 pad_maximum_fusion
  84.4 4.1 %all-to-all-start.2 = ((bf16[16,56,768]{2,1,0:T(8,128)(2,1)}), bf16[16,56,768]{2,1,0:T(8,128)(2,1)S(1)}, u32[]{:S(2)}, u32[]{:S(2)}) async-start(bf16[16,56,768]{2,1,0:T(8,128)(2,1)} %pad_maximum_fusion), calls=%async_computation.2 | async-start | bytes 2752512 | tf_op jit(solution)/shard_map/all_to_all | solution.py:193
  88.5 1.1 fusion.16
  90.2 0.9 collective-permute-start.20
  91.1 1.7 %collective-permute-start.19 = (bf16[32,768]{1,0:T(8,128)(2,1)S(1)}, bf16[32,768]{1,0:T(8,128)(2,1)S(1)}, u32[]{:S(2)}, u32[]{:S(2)}) collective-permute-start(bf16[32,768]{1,0:T(8,128)(2,1)S(1)} %get-tuple-element.68), channel_id=1, source_target_pairs={{0,20},{4,24},{8,28},{12,0},{16,4},{20,8},{24,12},{28,16},{1,21},{... | collective-permute-start | bytes 147464 | tf_op jit(solution)/shard_map/ppermute | solution.py:190
  92.8 5.1 %collective-permute-start.18 = (bf16[32,768]{1,0:T(8,128)(2,1)S(1)}, bf16[32,768]{1,0:T(8,128)(2,1)S(1)}, u32[]{:S(2)}, u32[]{:S(2)}) collective-permute-start(bf16[32,768]{1,0:T(8,128)(2,1)S(1)} %get-tuple-element.69), channel_id=1, source_target_pairs={{0,16},{4,20},{8,24},{12,28},{16,0},{20,4},{24,8},{28,12},{1,17},{... | collective-permute-start | bytes 147464 | tf_op jit(solution)/shard_map/ppermute | solution.py:190
  97.9 1.2 collective-permute-start.16
  99.1 1.7 %collective-permute-start.21 = (bf16[32,768]{1,0:T(8,128)(2,1)S(1)}, bf16[32,768]{1,0:T(8,128)(2,1)S(1)}, u32[]{:S(2)}, u32[]{:S(2)}) collective-permute-start(bf16[32,768]{1,0:T(8,128)(2,1)S(1)} %get-tuple-element.72), channel_id=1, source_target_pairs={{0,28},{4,0},{8,4},{12,8},{16,12},{20,16},{24,20},{28,24},{1,29},{... | collective-permute-start | bytes 147464 | tf_op jit(solution)/shard_map/ppermute | solution.py:190
  100.9 4.5 %collective-permute-done.17 = bf16[32,768]{1,0:T(8,128)(2,1)S(1)} collective-permute-done((bf16[32,768]{1,0:T(8,128)(2,1)S(1)}, bf16[32,768]{1,0:T(8,128)(2,1)S(1)}, u32[]{:S(2)}, u32[]{:S(2)}) %collective-permute-start.17) | collective-permute-done | bytes 49184 | tf_op jit(solution)/shard_map/ppermute | solution.py:190
  105.6 3.2 %collective-permute-start.22 = (bf16[32,384]{1,0:T(8,128)(2,1)S(1)}, bf16[32,384]{1,0:T(8,128)(2,1)S(1)}, u32[]{:S(2)}, u32[]{:S(2)}) collective-permute-start(bf16[32,384]{1,0:T(8,128)(2,1)S(1)} %bitcast.233), channel_id=1, source_target_pairs={{0,2},{2,0},{1,3},{3,1},{4,6},{6,4},{5,7},{7,5},{8,10},{10,8},{9,1... | collective-permute-start | bytes 73736 | tf_op jit(solution)/shard_map/ppermute | solution.py:27
  108.8 1.4 all-to-all-done.2
  110.3 0.7 broadcast_in_dim.7
  111.0 3.8 %all-to-all-start.3 = ((bf16[8,24,768]{2,1,0:T(8,128)(2,1)}), bf16[8,24,768]{2,1,0:T(8,128)(2,1)S(1)}, u32[]{:S(2)}, u32[]{:S(2)}) async-start(bf16[8,24,768]{2,1,0:T(8,128)(2,1)} %broadcast_in_dim.7), calls=%async_computation.3 | async-start | bytes 589824 | tf_op jit(solution)/shard_map/all_to_all | solution.py:19
  115.0 2.7 %collective-permute-start.13 = (bf16[32,768]{1,0:T(8,128)(2,1)S(1)}, bf16[32,768]{1,0:T(8,128)(2,1)S(1)}, u32[]{:S(2)}, u32[]{:S(2)}) collective-permute-start(bf16[32,768]{1,0:T(8,128)(2,1)S(1)} %slice_reduce_fusion), channel_id=1, source_target_pairs={{0,1},{1,0},{2,3},{3,2},{4,5},{5,4},{6,7},{7,6},{8,9},{9,8},{10,11... | collective-permute-start | bytes 147464 | tf_op jit(solution)/shard_map/ppermute | solution.py:27
  117.7 2.0 %collective-permute-start.23 = (f32[4,2,8]{2,0,1:T(4,128)S(1)}, f32[4,2,8]{2,0,1:T(4,128)S(1)}, u32[]{:S(2)}, u32[]{:S(2)}) collective-permute-start(f32[4,2,8]{2,0,1:T(4,128)S(1)} %fusion.42), channel_id=1, source_target_pairs={{0,2},{2,0},{1,3},{3,1},{4,6},{6,4},{5,7},{7,5},{8,10},{10,8},{9,1... | collective-permute-start | bytes 776 | tf_op jit(solution)/shard_map/ppermute | solution.py:27
  119.7 2.0 %collective-permute-done.23 = f32[4,2,8]{2,0,1:T(4,128)S(1)} collective-permute-done((f32[4,2,8]{2,0,1:T(4,128)S(1)}, f32[4,2,8]{2,0,1:T(4,128)S(1)}, u32[]{:S(2)}, u32[]{:S(2)}) %collective-permute-start.23) | collective-permute-done | bytes 288 | tf_op jit(solution)/shard_map/ppermute | solution.py:27
  121.7 2.9 %all-to-all-done.3 = bf16[8,24,768]{2,1,0:T(8,128)(2,1)S(1)} async-done(((bf16[8,24,768]{2,1,0:T(8,128)(2,1)}), bf16[8,24,768]{2,1,0:T(8,128)(2,1)S(1)}, u32[]{:S(2)}, u32[]{:S(2)}) %all-to-all-start.3) | async-done | bytes 294944 | tf_op jit(solution)/shard_map/all_to_all | solution.py:19
  124.7 0.7 maximum_select_fusion.6
  125.3 3.8 %collective-permute-start.24 = (bf16[2,32,384]{2,1,0:T(8,128)(2,1)S(1)}, bf16[2,32,384]{2,1,0:T(8,128)(2,1)S(1)}, u32[]{:S(2)}, u32[]{:S(2)}) collective-permute-start(bf16[2,32,384]{2,1,0:T(8,128)(2,1)S(1)} %maximum_select_fusion.8), channel_id=1, source_target_pairs={{0,1},{1,0},{2,3},{3,2},{4,5},{5,4},{6,7},{7,6},{8,9},{9,8},{10,11... | collective-permute-start | bytes 147464 | tf_op jit(solution)/shard_map/ppermute | solution.py:27
  129.1 0.7 broadcast_in_dim.8
  129.9 4.0 %all-to-all-start.4 = ((bf16[8,48,384]{2,1,0:T(8,128)(2,1)}), bf16[8,48,384]{2,1,0:T(8,128)(2,1)S(1)}, u32[]{:S(2)}, u32[]{:S(2)}) async-start(bf16[8,48,384]{2,1,0:T(8,128)(2,1)} %broadcast_in_dim.8), calls=%async_computation.4 | async-start | bytes 589824 | tf_op jit(solution)/shard_map/all_to_all | solution.py:19
  133.9 0.6 select_n.144
  134.5 0.7 copy.88
  135.2 5.8 %all-to-all-done.4 = bf16[8,48,384]{2,1,0:T(8,128)(2,1)S(1)} async-done(((bf16[8,48,384]{2,1,0:T(8,128)(2,1)}), bf16[8,48,384]{2,1,0:T(8,128)(2,1)S(1)}, u32[]{:S(2)}, u32[]{:S(2)}) %all-to-all-start.4) | async-done | bytes 294944 | tf_op jit(solution)/shard_map/all_to_all | solution.py:19
  140.9 1.1 collective-permute-start.25
  142.0 1.2 collective-permute-done.25
  143.2 1.1 fusion.20
  (102 shorter events, 4.7 us)
Async XLA Ops:
  0.6 20.3 %copy-start = (bf16[128,768]{1,0:T(8,128)(2,1)S(1)}, bf16[128,768]{1,0:T(8,128)(2,1)}, u32[]{:S(2)}) copy-start(bf16[128,768]{1,0:T(8,128)(2,1)} %param.6) | copy-start | bytes 589828
  1.7 9.3 %collective-permute-start = (bf16[384,384]{1,0:T(8,128)(2,1)S(1)}, bf16[384,384]{1,0:T(8,128)(2,1)S(1)}, u32[]{:S(2)}, u32[]{:S(2)}) collective-permute-start(bf16[384,384]{1,0:T(8,128)(2,1)S(1)} %dynamic-slice_bitcast_fusion), channel_id=1, source_target_pairs={{0,130},{2,128},{128,2},{130,0},{1,131},{3,129},{129,3},{131,1},{4... | collective-permute-start | bytes 884744 | tf_op jit(solution)/shard_map/ppermute | solution.py:110
  5.3 0.9 copy-start.5
  6.2 0.8 copy-start.6
  8.5 9.8 %copy-start.11 = (bf16[64,1024]{1,0:T(8,128)(2,1)S(1)}, bf16[64,1024]{1,0:T(8,128)(2,1)}, u32[]{:S(2)}) copy-start(bf16[64,1024]{1,0:T(8,128)(2,1)} %param.9) | copy-start | bytes 393220
  11.0 35.5 %all-to-all-start = ((bf16[16,32,1792]{2,1,0:T(8,128)(2,1)}), bf16[16,32,1792]{2,1,0:T(8,128)(2,1)}, u32[]{:S(2)}, u32[]{:S(2)}) async-start(bf16[16,32,1792]{2,1,0:T(8,128)(2,1)} %shard_map.93), calls=%async_computation | async-start | bytes 3670016 | tf_op jit(solution)/shard_map/all_to_all | solution.py:112
  18.4 2.8 %collective-permute-start.2 = (bf16[2,16,1024]{2,1,0:T(8,128)(2,1)S(1)}, bf16[2,16,1024]{2,1,0:T(8,128)(2,1)S(1)}, u32[]{:S(2)}, u32[]{:S(2)}) collective-permute-start(bf16[2,16,1024]{2,1,0:T(8,128)(2,1)S(1)} %get-tuple-element.79), channel_id=1, source_target_pairs={{0,1},{1,0},{2,3},{3,2},{4,5},{5,4},{6,7},{7,6},{8,9},{9,8},{10,11... | collective-permute-start | bytes 196616 | tf_op jit(solution)/shard_map/ppermute | solution.py:27
  21.6 16.6 %collective-permute-start.5 = (bf16[64,1792]{1,0:T(8,128)(2,1)S(1)}, bf16[64,1792]{1,0:T(8,128)(2,1)S(1)}, u32[]{:S(2)}, u32[]{:S(2)}) collective-permute-start(bf16[64,1792]{1,0:T(8,128)(2,1)S(1)} %bitcast.205), channel_id=1, source_target_pairs={{0,12},{4,16},{8,20},{12,24},{16,28},{20,0},{24,4},{28,8},{1,21},{... | collective-permute-start | bytes 688136 | tf_op jit(solution)/shard_map/ppermute | solution.py:33
  28.2 12.8 %collective-permute-start.4 = (bf16[64,1792]{1,0:T(8,128)(2,1)S(1)}, bf16[64,1792]{1,0:T(8,128)(2,1)S(1)}, u32[]{:S(2)}, u32[]{:S(2)}) collective-permute-start(bf16[64,1792]{1,0:T(8,128)(2,1)S(1)} %bitcast.206), channel_id=1, source_target_pairs={{0,8},{4,12},{8,16},{12,20},{16,24},{20,28},{24,0},{28,4},{1,25},{... | collective-permute-start | bytes 688136 | tf_op jit(solution)/shard_map/ppermute | solution.py:33
  28.4 15.0 %collective-permute-start.3 = (bf16[64,1792]{1,0:T(8,128)(2,1)S(1)}, bf16[64,1792]{1,0:T(8,128)(2,1)S(1)}, u32[]{:S(2)}, u32[]{:S(2)}) collective-permute-start(bf16[64,1792]{1,0:T(8,128)(2,1)S(1)} %bitcast.207), channel_id=1, source_target_pairs={{0,4},{4,8},{8,12},{12,16},{16,20},{20,24},{24,28},{28,0},{1,29},{... | collective-permute-start | bytes 688136 | tf_op jit(solution)/shard_map/ppermute | solution.py:33
  28.9 17.7 %collective-permute-start.1 = (bf16[384,384]{1,0:T(8,128)(2,1)S(1)}, bf16[384,384]{1,0:T(8,128)(2,1)S(1)}, u32[]{:S(2)}, u32[]{:S(2)}) collective-permute-start(bf16[384,384]{1,0:T(8,128)(2,1)S(1)} %collective-permute-done), channel_id=1, source_target_pairs={{0,1},{1,0},{2,3},{3,2},{4,5},{5,4},{6,7},{7,6},{8,9},{9,8},{10,11... | collective-permute-start | bytes 884744 | tf_op jit(solution)/shard_map/ppermute | solution.py:27
  38.3 6.4 %collective-permute-start.9 = (bf16[32,1792]{1,0:T(8,128)(2,1)S(1)}, bf16[32,1792]{1,0:T(8,128)(2,1)S(1)}, u32[]{:S(2)}, u32[]{:S(2)}) collective-permute-start(bf16[32,1792]{1,0:T(8,128)(2,1)S(1)} %dynamic-slice_bitcast_fusion.1), channel_id=1, source_target_pairs={{0,4},{4,8},{8,12},{12,16},{16,20},{20,24},{24,28},{28,0},{1,29},{... | collective-permute-start | bytes 344072 | tf_op jit(solution)/shard_map/ppermute | solution.py:33
  39.1 7.4 %collective-permute-start.8 = (bf16[64,1792]{1,0:T(8,128)(2,1)S(1)}, bf16[64,1792]{1,0:T(8,128)(2,1)S(1)}, u32[]{:S(2)}, u32[]{:S(2)}) collective-permute-start(bf16[64,1792]{1,0:T(8,128)(2,1)S(1)} %collective-permute-done.5.refs_0_), channel_id=1, source_target_pairs={{0,1},{1,0},{2,3},{3,2},{4,5},{5,4},{6,7},{7,6},{8,9},{9,8},{10,11... | collective-permute-start | bytes 688136 | tf_op jit(solution)/shard_map/ppermute | solution.py:27
  41.0 5.6 %collective-permute-start.7 = (bf16[64,1792]{1,0:T(8,128)(2,1)S(1)}, bf16[64,1792]{1,0:T(8,128)(2,1)S(1)}, u32[]{:S(2)}, u32[]{:S(2)}) collective-permute-start(bf16[64,1792]{1,0:T(8,128)(2,1)S(1)} %collective-permute-done.4.refs_1_), channel_id=1, source_target_pairs={{0,1},{1,0},{2,3},{3,2},{4,5},{5,4},{6,7},{7,6},{8,9},{9,8},{10,11... | collective-permute-start | bytes 688136 | tf_op jit(solution)/shard_map/ppermute | solution.py:27
  43.4 3.1 %collective-permute-start.6 = (bf16[64,1792]{1,0:T(8,128)(2,1)S(1)}, bf16[64,1792]{1,0:T(8,128)(2,1)S(1)}, u32[]{:S(2)}, u32[]{:S(2)}) collective-permute-start(bf16[64,1792]{1,0:T(8,128)(2,1)S(1)} %collective-permute-done.3.refs_2_), channel_id=1, source_target_pairs={{0,1},{1,0},{2,3},{3,2},{4,5},{5,4},{6,7},{7,6},{8,9},{9,8},{10,11... | collective-permute-start | bytes 688136 | tf_op jit(solution)/shard_map/ppermute | solution.py:27
  44.6 1.9 %collective-permute-start.10 = (bf16[32,1792]{1,0:T(8,128)(2,1)S(1)}, bf16[32,1792]{1,0:T(8,128)(2,1)S(1)}, u32[]{:S(2)}, u32[]{:S(2)}) collective-permute-start(bf16[32,1792]{1,0:T(8,128)(2,1)S(1)} %collective-permute-done.9.refs_7_), channel_id=1, source_target_pairs={{0,1},{1,0},{2,3},{3,2},{4,5},{5,4},{6,7},{7,6},{8,9},{9,8},{10,11... | collective-permute-start | bytes 344072 | tf_op jit(solution)/shard_map/ppermute | solution.py:27
  46.5 0.6 copy-start.3
  46.5 0.7 copy-start.1
  47.2 0.9 copy-start.2
  48.2 0.9 copy-start.4
  49.3 2.1 %copy-start.10 = (bf16[768,384]{1,0:T(8,128)(2,1)S(1)}, bf16[768,384]{1,0:T(8,128)(2,1)}, u32[]{:S(2)}) copy-start(bf16[768,384]{1,0:T(8,128)(2,1)} %param.8) | copy-start | bytes 1769476
  51.4 3.4 %copy-start.9 = (f32[512,512]{1,0:T(8,128)}, f32[512,512]{1,0:T(8,128)S(1)}, u32[]{:S(2)}) copy-start(f32[512,512]{1,0:T(8,128)S(1)} %get-tuple-element.92) | copy-start | bytes 3145732
  52.3 2.4 %copy-start.7 = (f32[512,768]{1,0:T(8,128)}, f32[512,768]{1,0:T(8,128)S(1)}, u32[]{:S(2)}) copy-start(f32[512,768]{1,0:T(8,128)S(1)} %get-tuple-element.90) | copy-start | bytes 4718596
  55.9 14.3 %all-to-all-start.1 = ((f32[8,8,512]{2,1,0:T(8,128)}), f32[8,8,512]{2,1,0:T(8,128)S(1)}, u32[]{:S(2)}, u32[]{:S(2)}) async-start(f32[8,8,512]{2,1,0:T(8,128)} %broadcast_in_dim.6), calls=%async_computation.1 | async-start | bytes 262144 | tf_op jit(solution)/shard_map/all_to_all | solution.py:19
  70.3 6.0 %collective-permute-start.11 = (f32[8,512]{1,0:T(8,128)S(1)}, f32[8,512]{1,0:T(8,128)S(1)}, u32[]{:S(2)}, u32[]{:S(2)}) collective-permute-start(f32[8,512]{1,0:T(8,128)S(1)} %stack.131), channel_id=1, source_target_pairs={{0,1},{1,0},{2,3},{3,2},{4,5},{5,4},{6,7},{7,6},{8,9},{9,8},{10,11... | collective-permute-start | bytes 49160 | tf_op jit(solution)/shard_map/ppermute | solution.py:27
  78.0 1.9 %copy-start.8 = (f32[512,768]{1,0:T(8,128)S(1)}, f32[512,768]{1,0:T(8,128)}, u32[]{:S(2)}) copy-start(f32[512,768]{1,0:T(8,128)} %copy-done.7) | copy-start | bytes 4718596
  80.7 2.1 %collective-permute-start.12 = (bf16[384,768]{1,0:T(8,128)(2,1)S(1)}, bf16[384,768]{1,0:T(8,128)(2,1)S(1)}, u32[]{:S(2)}, u32[]{:S(2)}) collective-permute-start(bf16[384,768]{1,0:T(8,128)(2,1)S(1)} %fusion.19), channel_id=1, source_target_pairs={{0,1},{1,0},{2,3},{3,2},{4,5},{5,4},{6,7},{7,6},{8,9},{9,8},{10,11... | collective-permute-start | bytes 1769480 | tf_op jit(solution)/shard_map/ppermute | solution.py:27
  81.2 7.3 %collective-permute-start.14 = (bf16[256,768]{1,0:T(8,128)(2,1)S(1)}, bf16[256,768]{1,0:T(8,128)(2,1)}, u32[]{:S(2)}, u32[]{:S(2)}) collective-permute-start(bf16[256,768]{1,0:T(8,128)(2,1)S(1)} %slice.230), channel_id=1, source_target_pairs={{0,1},{1,0},{2,3},{3,2},{4,5},{5,4},{6,7},{7,6},{8,9},{9,8},{10,11... | collective-permute-start | bytes 1179656 | tf_op jit(solution)/shard_map/ppermute | solution.py:27
  84.4 25.8 %all-to-all-start.2 = ((bf16[16,56,768]{2,1,0:T(8,128)(2,1)}), bf16[16,56,768]{2,1,0:T(8,128)(2,1)S(1)}, u32[]{:S(2)}, u32[]{:S(2)}) async-start(bf16[16,56,768]{2,1,0:T(8,128)(2,1)} %pad_maximum_fusion), calls=%async_computation.2 | async-start | bytes 2752512 | tf_op jit(solution)/shard_map/all_to_all | solution.py:193
  89.8 8.1 %collective-permute-start.15 = (bf16[32,768]{1,0:T(8,128)(2,1)S(1)}, bf16[32,768]{1,0:T(8,128)(2,1)S(1)}, u32[]{:S(2)}, u32[]{:S(2)}) collective-permute-start(bf16[32,768]{1,0:T(8,128)(2,1)S(1)} %get-tuple-element.66), channel_id=1, source_target_pairs={{0,4},{4,8},{8,12},{12,16},{16,20},{20,24},{24,28},{28,0},{1,5},{5... | collective-permute-start | bytes 147464 | tf_op jit(solution)/shard_map/ppermute | solution.py:190
  90.2 9.0 %collective-permute-start.20 = (bf16[32,768]{1,0:T(8,128)(2,1)S(1)}, bf16[32,768]{1,0:T(8,128)(2,1)S(1)}, u32[]{:S(2)}, u32[]{:S(2)}) collective-permute-start(bf16[32,768]{1,0:T(8,128)(2,1)S(1)} %get-tuple-element.67), channel_id=1, source_target_pairs={{0,24},{4,28},{8,0},{12,4},{16,8},{20,12},{24,16},{28,20},{1,25},{... | collective-permute-start | bytes 147464 | tf_op jit(solution)/shard_map/ppermute | solution.py:190
  91.1 9.8 %collective-permute-start.19 = (bf16[32,768]{1,0:T(8,128)(2,1)S(1)}, bf16[32,768]{1,0:T(8,128)(2,1)S(1)}, u32[]{:S(2)}, u32[]{:S(2)}) collective-permute-start(bf16[32,768]{1,0:T(8,128)(2,1)S(1)} %get-tuple-element.68), channel_id=1, source_target_pairs={{0,20},{4,24},{8,28},{12,0},{16,4},{20,8},{24,12},{28,16},{1,21},{... | collective-permute-start | bytes 147464 | tf_op jit(solution)/shard_map/ppermute | solution.py:190
  92.8 8.1 %collective-permute-start.18 = (bf16[32,768]{1,0:T(8,128)(2,1)S(1)}, bf16[32,768]{1,0:T(8,128)(2,1)S(1)}, u32[]{:S(2)}, u32[]{:S(2)}) collective-permute-start(bf16[32,768]{1,0:T(8,128)(2,1)S(1)} %get-tuple-element.69), channel_id=1, source_target_pairs={{0,16},{4,20},{8,24},{12,28},{16,0},{20,4},{24,8},{28,12},{1,17},{... | collective-permute-start | bytes 147464 | tf_op jit(solution)/shard_map/ppermute | solution.py:190
  97.9 7.4 %collective-permute-start.17 = (bf16[32,768]{1,0:T(8,128)(2,1)S(1)}, bf16[32,768]{1,0:T(8,128)(2,1)S(1)}, u32[]{:S(2)}, u32[]{:S(2)}) collective-permute-start(bf16[32,768]{1,0:T(8,128)(2,1)S(1)} %get-tuple-element.70), channel_id=1, source_target_pairs={{0,12},{4,16},{8,20},{12,24},{16,28},{20,0},{24,4},{28,8},{1,13},{... | collective-permute-start | bytes 147464 | tf_op jit(solution)/shard_map/ppermute | solution.py:190
  97.9 7.4 %collective-permute-start.16 = (bf16[32,768]{1,0:T(8,128)(2,1)S(1)}, bf16[32,768]{1,0:T(8,128)(2,1)S(1)}, u32[]{:S(2)}, u32[]{:S(2)}) collective-permute-start(bf16[32,768]{1,0:T(8,128)(2,1)S(1)} %get-tuple-element.71), channel_id=1, source_target_pairs={{0,8},{4,12},{8,16},{12,20},{16,24},{20,28},{24,0},{28,4},{1,9},{5... | collective-permute-start | bytes 147464 | tf_op jit(solution)/shard_map/ppermute | solution.py:190
  99.1 6.2 %collective-permute-start.21 = (bf16[32,768]{1,0:T(8,128)(2,1)S(1)}, bf16[32,768]{1,0:T(8,128)(2,1)S(1)}, u32[]{:S(2)}, u32[]{:S(2)}) collective-permute-start(bf16[32,768]{1,0:T(8,128)(2,1)S(1)} %get-tuple-element.72), channel_id=1, source_target_pairs={{0,28},{4,0},{8,4},{12,8},{16,12},{20,16},{24,20},{28,24},{1,29},{... | collective-permute-start | bytes 147464 | tf_op jit(solution)/shard_map/ppermute | solution.py:190
  105.6 14.1 %collective-permute-start.22 = (bf16[32,384]{1,0:T(8,128)(2,1)S(1)}, bf16[32,384]{1,0:T(8,128)(2,1)S(1)}, u32[]{:S(2)}, u32[]{:S(2)}) collective-permute-start(bf16[32,384]{1,0:T(8,128)(2,1)S(1)} %bitcast.233), channel_id=1, source_target_pairs={{0,2},{2,0},{1,3},{3,1},{4,6},{6,4},{5,7},{7,5},{8,10},{10,8},{9,1... | collective-permute-start | bytes 73736 | tf_op jit(solution)/shard_map/ppermute | solution.py:27
  111.0 13.6 %all-to-all-start.3 = ((bf16[8,24,768]{2,1,0:T(8,128)(2,1)}), bf16[8,24,768]{2,1,0:T(8,128)(2,1)S(1)}, u32[]{:S(2)}, u32[]{:S(2)}) async-start(bf16[8,24,768]{2,1,0:T(8,128)(2,1)} %broadcast_in_dim.7), calls=%async_computation.3 | async-start | bytes 589824 | tf_op jit(solution)/shard_map/all_to_all | solution.py:19
  115.0 6.8 %collective-permute-start.13 = (bf16[32,768]{1,0:T(8,128)(2,1)S(1)}, bf16[32,768]{1,0:T(8,128)(2,1)S(1)}, u32[]{:S(2)}, u32[]{:S(2)}) collective-permute-start(bf16[32,768]{1,0:T(8,128)(2,1)S(1)} %slice_reduce_fusion), channel_id=1, source_target_pairs={{0,1},{1,0},{2,3},{3,2},{4,5},{5,4},{6,7},{7,6},{8,9},{9,8},{10,11... | collective-permute-start | bytes 147464 | tf_op jit(solution)/shard_map/ppermute | solution.py:27
  117.7 4.0 %collective-permute-start.23 = (f32[4,2,8]{2,0,1:T(4,128)S(1)}, f32[4,2,8]{2,0,1:T(4,128)S(1)}, u32[]{:S(2)}, u32[]{:S(2)}) collective-permute-start(f32[4,2,8]{2,0,1:T(4,128)S(1)} %fusion.42), channel_id=1, source_target_pairs={{0,2},{2,0},{1,3},{3,1},{4,6},{6,4},{5,7},{7,5},{8,10},{10,8},{9,1... | collective-permute-start | bytes 776 | tf_op jit(solution)/shard_map/ppermute | solution.py:27
  125.3 9.2 %collective-permute-start.24 = (bf16[2,32,384]{2,1,0:T(8,128)(2,1)S(1)}, bf16[2,32,384]{2,1,0:T(8,128)(2,1)S(1)}, u32[]{:S(2)}, u32[]{:S(2)}) collective-permute-start(bf16[2,32,384]{2,1,0:T(8,128)(2,1)S(1)} %maximum_select_fusion.8), channel_id=1, source_target_pairs={{0,1},{1,0},{2,3},{3,2},{4,5},{5,4},{6,7},{7,6},{8,9},{9,8},{10,11... | collective-permute-start | bytes 147464 | tf_op jit(solution)/shard_map/ppermute | solution.py:27
  129.9 11.1 %all-to-all-start.4 = ((bf16[8,48,384]{2,1,0:T(8,128)(2,1)}), bf16[8,48,384]{2,1,0:T(8,128)(2,1)S(1)}, u32[]{:S(2)}, u32[]{:S(2)}) async-start(bf16[8,48,384]{2,1,0:T(8,128)(2,1)} %broadcast_in_dim.8), calls=%async_computation.4 | async-start | bytes 589824 | tf_op jit(solution)/shard_map/all_to_all | solution.py:19
  140.9 2.3 %collective-permute-start.25 = (bf16[384,384]{1,0:T(8,128)(2,1)S(1)}, bf16[384,384]{1,0:T(8,128)(2,1)S(1)}, u32[]{:S(2)}, u32[]{:S(2)}) collective-permute-start(bf16[384,384]{1,0:T(8,128)(2,1)S(1)} %bitcast.217), channel_id=1, source_target_pairs={{0,1},{1,0},{2,3},{3,2},{4,5},{5,4},{6,7},{7,6},{8,9},{9,8},{10,11... | collective-permute-start | bytes 884744 | tf_op jit(solution)/shard_map/ppermute | solution.py:27

commit v5 on v4

--- a/solution.py
+++ b/solution.py
@@ -100,15 +100,14 @@
 
 
     teach = pick(teacher_image.reshape(2, 2, 16, wide), high, 1)
-    come = swap(teach, "c")
+    sent = copies(core, student_text, teacher_text, 16)
+    head_come = pick(student_head.reshape(2, half, half), core, 0)
+    head_come = lax.ppermute(head_come, ("yl", "yh"), [(i, 3 - i) for i in range(4)])
+    sent, head_come, come = lax.optimization_barrier((sent, head_come, swap(teach, "c")))
     teach = jnp.where(core == 0, jnp.stack([teach, come]), jnp.stack([come, teach])).reshape(4, 2, 8, wide)
     feats = pick(image_feats.reshape(4, 2, 2, 8, width), high, 1)
     own = block_first(jnp.concatenate([feats, teach], 3))
     own = own.transpose(1, 0, 2, 3).reshape(64, width + wide)
-    sent = copies(core, student_text, teacher_text, 16)
-    head_come = pick(student_head.reshape(2, half, half), core, 0)
-    head_come = lax.ppermute(head_come, ("yl", "yh"), [(i, 3 - i) for i in range(4)])
-    sent, head_come = lax.optimization_barrier((sent, head_come))
     cols = lax.all_to_all(sent, COLS, 0, 0, tiled=True)
     near = {k: turn(own, k) for k in (3, 1, 2)}
     far = turn(pick(near[3].reshape(2, 32, width + wide), core, 0), 1)

time: 145 us -> 145 us (level)
  waiting for transfers between devices: 40.9 us -> 34.6 us
  starting transfers between devices: 74.3 us -> 79.8 us
    ppermute x14, starting transfers between devices: 26 us -> 31.7 us  [swap(): return lax.ppermute(value, axis, [(0, 1), (1, 0)])]
    ppermute x4, waiting for transfers between devices: 10.3 us -> 6.14 us  [turn(): return lax.ppermute(value, ('z', 'c'), pairs)]
    ppermute x1, waiting for transfers between devices: 2.53 us -> 0.63 us  [shards(): lax.ppermute(head_come, ('yl', 'yh'), [(i, 3 - i) for i in range(4)])]
    unnamed x26 -> x24, local copies, waits for them, and re-layouts: 4.09 us -> 4.1 us
  transfers between devices with their start and end apart: 31 -> 31, of which waited for: 16 -> 13; matrix products, arithmetic and copies ran while one was open for 5% -> 6% of each run, Pallas kernels for 1% -> 1%
where the time goes in v5:
time: 145 us; the launch traced here: 144 us
  starting transfers between devices  79.8 us (55%)
  waiting for transfers between devices  34.6 us (24%)
  local copies, waits for them, and re-layouts  10.3 us (7%)
  matrix products  8.35 us (6%)
  other arithmetic  7.93 us (5%)
  between operations  1.78 us (1%)
  Pallas kernels  1.63 us (1%)
    ppermute x14, starting transfers between devices, swap(): return lax.ppermute(value, axis, [(0, 1), (1, 0)])  31.7 us
    all_to_all x3, waiting for transfers between devices, to_all(): return lax.all_to_all(sent, axes, 0, 0, tiled=True)  16.5 us
    all_to_all x3, starting transfers between devices, to_all(): return lax.all_to_all(sent, axes, 0, 0, tiled=True)  14.1 us
    ppermute x7, starting transfers between devices, shards(): lax.ppermute(turned[k], 'z', [(i, (i + k) % 8) for i in range(8)])  11.1 us
    dot_general x6, matrix products, dot(): lax.dot_general(left, right, (((left_dim,), (right_dim,)), ((), ())), pre...  8.35 us
    ppermute x4, starting transfers between devices, turn(): return lax.ppermute(value, ('z', 'c'), pairs)  7.85 us
    all_to_all x1, starting transfers between devices, shards(): cols = lax.all_to_all(sent, COLS, 0, 0, tiled=True)  7.3 us
    ppermute x4, waiting for transfers between devices, turn(): return lax.ppermute(value, ('z', 'c'), pairs)  6.14 us
  transfers between devices with their start and end apart: 31, of which 13 were waited for; matrix products, arithmetic and copies ran while one was open for 6% of the time, Pallas kernels for 1%

profile of v5, /device:TPU:1, one launch (start us, length us, event | category | flops | bytes accessed | tf_op | source)
XLA Modules:
  0.0 144.4 jit_solution(17449514772518991294)
XLA Ops:
  0.7 1.0 dynamic-slice_bitcast_fusion
  1.7 3.7 %collective-permute-start = (bf16[384,384]{1,0:T(8,128)(2,1)S(1)}, bf16[384,384]{1,0:T(8,128)(2,1)S(1)}, u32[]{:S(2)}, u32[]{:S(2)}) collective-permute-start(bf16[384,384]{1,0:T(8,128)(2,1)S(1)} %dynamic-slice_bitcast_fusion), channel_id=1, source_target_pairs={{0,130},{2,128},{128,2},{130,0},{1,131},{3,129},{129,3},{131,1},{4... | collective-permute-start | bytes 884744 | tf_op jit(solution)/shard_map/ppermute | solution.py:105
  5.3 0.8 dynamic-slice_bitcast_fusion.4
  6.2 1.0 collective-permute-start.1
  7.2 0.9 copy-done.5
  8.1 0.8 copy-done.6
  9.0 1.4 shard_map.93
  10.4 0.6 collective-permute-done
  11.0 7.3 %all-to-all-start = ((bf16[16,32,1792]{2,1,0:T(8,128)(2,1)}), bf16[16,32,1792]{2,1,0:T(8,128)(2,1)}, u32[]{:S(2)}, u32[]{:S(2)}) async-start(bf16[16,32,1792]{2,1,0:T(8,128)(2,1)} %shard_map.93), calls=%async_computation | async-start | bytes 3670016 | tf_op jit(solution)/shard_map/all_to_all | solution.py:111
  19.5 6.5 %collective-permute-start.5 = (bf16[64,1792]{1,0:T(8,128)(2,1)S(1)}, bf16[64,1792]{1,0:T(8,128)(2,1)S(1)}, u32[]{:S(2)}, u32[]{:S(2)}) collective-permute-start(bf16[64,1792]{1,0:T(8,128)(2,1)S(1)} %bitcast.205), channel_id=1, source_target_pairs={{0,12},{4,16},{8,20},{12,24},{16,28},{20,0},{24,4},{28,8},{1,21},{... | collective-permute-start | bytes 688136 | tf_op jit(solution)/shard_map/ppermute | solution.py:33
  26.3 0.5 collective-permute-start.3
  26.7 3.9 %collective-permute-start.2 = (bf16[384,384]{1,0:T(8,128)(2,1)S(1)}, bf16[384,384]{1,0:T(8,128)(2,1)S(1)}, u32[]{:S(2)}, u32[]{:S(2)}) collective-permute-start(bf16[384,384]{1,0:T(8,128)(2,1)S(1)} %collective-permute-done), channel_id=1, source_target_pairs={{0,1},{1,0},{2,3},{3,2},{4,5},{5,4},{6,7},{7,6},{8,9},{9,8},{10,11... | collective-permute-start | bytes 884744 | tf_op jit(solution)/shard_map/ppermute | solution.py:27
  30.6 5.5 %collective-permute-done.5.refs_0_ = bf16[64,1792]{1,0:T(8,128)(2,1)S(1)} collective-permute-done((bf16[64,1792]{1,0:T(8,128)(2,1)S(1)}, bf16[64,1792]{1,0:T(8,128)(2,1)S(1)}, u32[]{:S(2)}, u32[]{:S(2)}) %collective-permute-start.5) | collective-permute-done | bytes 229408 | tf_op jit(solution)/shard_map/ppermute | solution.py:33
  36.1 0.6 collective-permute-start.9
  36.7 1.5 %collective-permute-start.8 = (bf16[64,1792]{1,0:T(8,128)(2,1)S(1)}, bf16[64,1792]{1,0:T(8,128)(2,1)S(1)}, u32[]{:S(2)}, u32[]{:S(2)}) collective-permute-start(bf16[64,1792]{1,0:T(8,128)(2,1)S(1)} %collective-permute-done.5.refs_0_), channel_id=1, source_target_pairs={{0,1},{1,0},{2,3},{3,2},{4,5},{5,4},{6,7},{7,6},{8,9},{9,8},{10,11... | collective-permute-start | bytes 688136 | tf_op jit(solution)/shard_map/ppermute | solution.py:27
  38.2 0.6 collective-permute-done.4.refs_1_
  38.8 2.8 %collective-permute-start.7 = (bf16[64,1792]{1,0:T(8,128)(2,1)S(1)}, bf16[64,1792]{1,0:T(8,128)(2,1)S(1)}, u32[]{:S(2)}, u32[]{:S(2)}) collective-permute-start(bf16[64,1792]{1,0:T(8,128)(2,1)S(1)} %collective-permute-done.4.refs_1_), channel_id=1, source_target_pairs={{0,1},{1,0},{2,3},{3,2},{4,5},{5,4},{6,7},{7,6},{8,9},{9,8},{10,11... | collective-permute-start | bytes 688136 | tf_op jit(solution)/shard_map/ppermute | solution.py:27
  41.6 2.1 %collective-permute-start.6 = (bf16[64,1792]{1,0:T(8,128)(2,1)S(1)}, bf16[64,1792]{1,0:T(8,128)(2,1)S(1)}, u32[]{:S(2)}, u32[]{:S(2)}) collective-permute-start(bf16[64,1792]{1,0:T(8,128)(2,1)S(1)} %collective-permute-done.3.refs_2_), channel_id=1, source_target_pairs={{0,1},{1,0},{2,3},{3,2},{4,5},{5,4},{6,7},{7,6},{8,9},{9,8},{10,11... | collective-permute-start | bytes 688136 | tf_op jit(solution)/shard_map/ppermute | solution.py:27
  43.6 1.2 collective-permute-start.10
  44.9 1.0 collective-permute-done.10.refs_8_
  46.6 0.9 copy-done.2
  47.5 0.9 copy-done.4
  48.6 2.0 %fusion.58 = (f32[512]{0:T(512)S(1)}, f32[512,512]{1,0:T(8,128)S(1)}) fusion(bf16[512,1792]{1,0:T(8,128)(2,1)S(1)} %bitcast.202, bf16[512,1792]{1,0:T(8,128)(2,1)} %bitcast.15), kind=kOutput, calls=%fused_computation.146 | convolution fusion | flops 537394688 | bytes 3147776 | tf_op jit(solution)/shard_map/dot_general | solution.py:86
  50.7 0.9 multiply_reduce_fusion
  51.6 2.4 %fusion.59 = (f32[512]{0:T(512)S(1)}, f32[512,512]{1,0:T(8,128)S(1)}) fusion(f32[512,768]{1,0:T(8,128)S(1)} %get-tuple-element.92, f32[512]{0:T(512)S(1)} %add_rsqrt_fusion, bf16[512,1792]{1,0:T(8,128)(2,1)} %bitcast.15), kind=kOutput, calls=%fused_computation.147 | convolution fusion | flops 403963392 | bytes 3411968 | tf_op jit(solution)/shard_map/dot_general | solution.py:86
  54.1 0.4 multiply_reduce_fusion.1
  54.5 0.7 broadcast_in_dim.6
  55.2 6.3 %all-to-all-start.1 = ((f32[8,8,512]{2,1,0:T(8,128)}), f32[8,8,512]{2,1,0:T(8,128)S(1)}, u32[]{:S(2)}, u32[]{:S(2)}) async-start(f32[8,8,512]{2,1,0:T(8,128)} %broadcast_in_dim.6), calls=%async_computation.1 | async-start | bytes 262144 | tf_op jit(solution)/shard_map/all_to_all | solution.py:19
  61.6 7.8 %all-to-all-done.1 = f32[8,8,512]{2,1,0:T(8,128)S(1)} async-done(((f32[8,8,512]{2,1,0:T(8,128)}), f32[8,8,512]{2,1,0:T(8,128)S(1)}, u32[]{:S(2)}, u32[]{:S(2)}) %all-to-all-start.1) | async-done | bytes 131104 | tf_op jit(solution)/shard_map/all_to_all | solution.py:19
  69.6 5.9 %collective-permute-start.11 = (f32[8,512]{1,0:T(8,128)S(1)}, f32[8,512]{1,0:T(8,128)S(1)}, u32[]{:S(2)}, u32[]{:S(2)}) collective-permute-start(f32[8,512]{1,0:T(8,128)S(1)} %stack.131), channel_id=1, source_target_pairs={{0,1},{1,0},{2,3},{3,2},{4,5},{5,4},{6,7},{7,6},{8,9},{9,8},{10,11... | collective-permute-start | bytes 49160 | tf_op jit(solution)/shard_map/ppermute | solution.py:27
  75.8 0.6 collective-permute-done.11
  76.5 1.5 %multiply_convert_fusion.2 = bf16[512,512]{1,0:T(8,128)(2,1)S(1)} fusion(f32[512,512]{1,0:T(8,128)} %copy-done.9, f32[512,512]{1,0:T(8,128)S(1)} %get-tuple-element.96, f32[512]{0:T(512)S(1)} %get-tuple-element.90, f32[512]{0:T(512)S(1)} %get-tuple-element.63), kind=kLoop, calls=%fused_computation.25 | loop fusion | flops 1310720 | bytes 2625536 | tf_op jit(solution)/shard_map/convert_element_type | solution.py:163
  78.0 1.9 %convolution_multiply_fusion = f32[512,768]{1,0:T(8,128)S(1)} fusion(bf16[512,512]{1,0:T(8,128)(2,1)S(1)} %multiply_convert_fusion.2, bf16[512,1792]{1,0:T(8,128)(2,1)} %bitcast.15), kind=kOutput, calls=%fused_computation.4 | convolution fusion | flops 403046400 | bytes 2883584 | tf_op jit(solution)/shard_map/dot_general | solution.py:86
  80.2 0.5 fusion.60
  80.7 0.4 collective-permute-start.12
  81.5 0.7 multiply_convert_fusion
  82.1 0.7 collective-permute-done.12
  83.2 1.2 pad_maximum_fusion
  84.4 4.1 %all-to-all-start.2 = ((bf16[16,56,768]{2,1,0:T(8,128)(2,1)}), bf16[16,56,768]{2,1,0:T(8,128)(2,1)S(1)}, u32[]{:S(2)}, u32[]{:S(2)}) async-start(bf16[16,56,768]{2,1,0:T(8,128)(2,1)} %pad_maximum_fusion), calls=%async_computation.2 | async-start | bytes 2752512 | tf_op jit(solution)/shard_map/all_to_all | solution.py:192
  88.6 1.1 fusion.16
  90.2 1.1 collective-permute-start.20
  91.3 1.6 %collective-permute-start.19 = (bf16[32,768]{1,0:T(8,128)(2,1)S(1)}, bf16[32,768]{1,0:T(8,128)(2,1)S(1)}, u32[]{:S(2)}, u32[]{:S(2)}) collective-permute-start(bf16[32,768]{1,0:T(8,128)(2,1)S(1)} %get-tuple-element.70), channel_id=1, source_target_pairs={{0,20},{4,24},{8,28},{12,0},{16,4},{20,8},{24,12},{28,16},{1,21},{... | collective-permute-start | bytes 147464 | tf_op jit(solution)/shard_map/ppermute | solution.py:189
  92.9 5.1 %collective-permute-start.18 = (bf16[32,768]{1,0:T(8,128)(2,1)S(1)}, bf16[32,768]{1,0:T(8,128)(2,1)S(1)}, u32[]{:S(2)}, u32[]{:S(2)}) collective-permute-start(bf16[32,768]{1,0:T(8,128)(2,1)S(1)} %get-tuple-element.71), channel_id=1, source_target_pairs={{0,16},{4,20},{8,24},{12,28},{16,0},{20,4},{24,8},{28,12},{1,17},{... | collective-permute-start | bytes 147464 | tf_op jit(solution)/shard_map/ppermute | solution.py:189
  98.0 1.2 collective-permute-start.16
  99.1 1.8 %collective-permute-start.21 = (bf16[32,768]{1,0:T(8,128)(2,1)S(1)}, bf16[32,768]{1,0:T(8,128)(2,1)S(1)}, u32[]{:S(2)}, u32[]{:S(2)}) collective-permute-start(bf16[32,768]{1,0:T(8,128)(2,1)S(1)} %get-tuple-element.74), channel_id=1, source_target_pairs={{0,28},{4,0},{8,4},{12,8},{16,12},{20,16},{24,20},{28,24},{1,29},{... | collective-permute-start | bytes 147464 | tf_op jit(solution)/shard_map/ppermute | solution.py:189
  100.9 4.5 %collective-permute-done.17 = bf16[32,768]{1,0:T(8,128)(2,1)S(1)} collective-permute-done((bf16[32,768]{1,0:T(8,128)(2,1)S(1)}, bf16[32,768]{1,0:T(8,128)(2,1)S(1)}, u32[]{:S(2)}, u32[]{:S(2)}) %collective-permute-start.17) | collective-permute-done | bytes 49184 | tf_op jit(solution)/shard_map/ppermute | solution.py:189
  105.7 3.2 %collective-permute-start.22 = (bf16[32,384]{1,0:T(8,128)(2,1)S(1)}, bf16[32,384]{1,0:T(8,128)(2,1)S(1)}, u32[]{:S(2)}, u32[]{:S(2)}) collective-permute-start(bf16[32,384]{1,0:T(8,128)(2,1)S(1)} %bitcast.233), channel_id=1, source_target_pairs={{0,2},{2,0},{1,3},{3,1},{4,6},{6,4},{5,7},{7,5},{8,10},{10,8},{9,1... | collective-permute-start | bytes 73736 | tf_op jit(solution)/shard_map/ppermute | solution.py:27
  108.8 1.4 all-to-all-done.2
  110.3 0.7 broadcast_in_dim.7
  111.0 3.8 %all-to-all-start.3 = ((bf16[8,24,768]{2,1,0:T(8,128)(2,1)}), bf16[8,24,768]{2,1,0:T(8,128)(2,1)S(1)}, u32[]{:S(2)}, u32[]{:S(2)}) async-start(bf16[8,24,768]{2,1,0:T(8,128)(2,1)} %broadcast_in_dim.7), calls=%async_computation.3 | async-start | bytes 589824 | tf_op jit(solution)/shard_map/all_to_all | solution.py:19
  115.0 2.6 %collective-permute-start.13 = (bf16[32,768]{1,0:T(8,128)(2,1)S(1)}, bf16[32,768]{1,0:T(8,128)(2,1)S(1)}, u32[]{:S(2)}, u32[]{:S(2)}) collective-permute-start(bf16[32,768]{1,0:T(8,128)(2,1)S(1)} %slice_reduce_fusion), channel_id=1, source_target_pairs={{0,1},{1,0},{2,3},{3,2},{4,5},{5,4},{6,7},{7,6},{8,9},{9,8},{10,11... | collective-permute-start | bytes 147464 | tf_op jit(solution)/shard_map/ppermute | solution.py:27
  117.7 2.0 %collective-permute-start.23 = (f32[4,2,8]{2,0,1:T(4,128)S(1)}, f32[4,2,8]{2,0,1:T(4,128)S(1)}, u32[]{:S(2)}, u32[]{:S(2)}) collective-permute-start(f32[4,2,8]{2,0,1:T(4,128)S(1)} %fusion.42), channel_id=1, source_target_pairs={{0,2},{2,0},{1,3},{3,1},{4,6},{6,4},{5,7},{7,5},{8,10},{10,8},{9,1... | collective-permute-start | bytes 776 | tf_op jit(solution)/shard_map/ppermute | solution.py:27
  119.7 2.0 %collective-permute-done.23 = f32[4,2,8]{2,0,1:T(4,128)S(1)} collective-permute-done((f32[4,2,8]{2,0,1:T(4,128)S(1)}, f32[4,2,8]{2,0,1:T(4,128)S(1)}, u32[]{:S(2)}, u32[]{:S(2)}) %collective-permute-start.23) | collective-permute-done | bytes 288 | tf_op jit(solution)/shard_map/ppermute | solution.py:27
  121.8 2.9 %all-to-all-done.3 = bf16[8,24,768]{2,1,0:T(8,128)(2,1)S(1)} async-done(((bf16[8,24,768]{2,1,0:T(8,128)(2,1)}), bf16[8,24,768]{2,1,0:T(8,128)(2,1)S(1)}, u32[]{:S(2)}, u32[]{:S(2)}) %all-to-all-start.3) | async-done | bytes 294944 | tf_op jit(solution)/shard_map/all_to_all | solution.py:19
  124.8 0.7 maximum_select_fusion.6
  125.4 3.7 %collective-permute-start.24 = (bf16[2,32,384]{2,1,0:T(8,128)(2,1)S(1)}, bf16[2,32,384]{2,1,0:T(8,128)(2,1)S(1)}, u32[]{:S(2)}, u32[]{:S(2)}) collective-permute-start(bf16[2,32,384]{2,1,0:T(8,128)(2,1)S(1)} %maximum_select_fusion.8), channel_id=1, source_target_pairs={{0,1},{1,0},{2,3},{3,2},{4,5},{5,4},{6,7},{7,6},{8,9},{9,8},{10,11... | collective-permute-start | bytes 147464 | tf_op jit(solution)/shard_map/ppermute | solution.py:27
  129.2 0.7 broadcast_in_dim.8
  129.9 4.0 %all-to-all-start.4 = ((bf16[8,48,384]{2,1,0:T(8,128)(2,1)}), bf16[8,48,384]{2,1,0:T(8,128)(2,1)S(1)}, u32[]{:S(2)}, u32[]{:S(2)}) async-start(bf16[8,48,384]{2,1,0:T(8,128)(2,1)} %broadcast_in_dim.8), calls=%async_computation.4 | async-start | bytes 589824 | tf_op jit(solution)/shard_map/all_to_all | solution.py:19
  134.0 0.6 select_n.144
  134.6 0.7 copy.88
  135.2 5.8 %all-to-all-done.4 = bf16[8,48,384]{2,1,0:T(8,128)(2,1)S(1)} async-done(((bf16[8,48,384]{2,1,0:T(8,128)(2,1)}), bf16[8,48,384]{2,1,0:T(8,128)(2,1)S(1)}, u32[]{:S(2)}, u32[]{:S(2)}) %all-to-all-start.4) | async-done | bytes 294944 | tf_op jit(solution)/shard_map/all_to_all | solution.py:19
  141.0 1.1 collective-permute-start.25
  142.1 1.2 collective-permute-done.25
  143.3 1.1 fusion.20
  (100 shorter events, 4.6 us)
Async XLA Ops:
  0.6 18.3 %copy-start = (bf16[128,768]{1,0:T(8,128)(2,1)S(1)}, bf16[128,768]{1,0:T(8,128)(2,1)}, u32[]{:S(2)}) copy-start(bf16[128,768]{1,0:T(8,128)(2,1)} %param.6) | copy-start | bytes 589828
  1.7 9.3 %collective-permute-start = (bf16[384,384]{1,0:T(8,128)(2,1)S(1)}, bf16[384,384]{1,0:T(8,128)(2,1)S(1)}, u32[]{:S(2)}, u32[]{:S(2)}) collective-permute-start(bf16[384,384]{1,0:T(8,128)(2,1)S(1)} %dynamic-slice_bitcast_fusion), channel_id=1, source_target_pairs={{0,130},{2,128},{128,2},{130,0},{1,131},{3,129},{129,3},{131,1},{4... | collective-permute-start | bytes 884744 | tf_op jit(solution)/shard_map/ppermute | solution.py:105
  6.2 4.2 %collective-permute-start.1 = (bf16[2,16,1024]{2,1,0:T(8,128)(2,1)S(1)}, bf16[2,16,1024]{2,1,0:T(8,128)(2,1)S(1)}, u32[]{:S(2)}, u32[]{:S(2)}) collective-permute-start(bf16[2,16,1024]{2,1,0:T(8,128)(2,1)S(1)} %get-tuple-element.81), channel_id=1, source_target_pairs={{0,1},{1,0},{2,3},{3,2},{4,5},{5,4},{6,7},{7,6},{8,9},{9,8},{10,11... | collective-permute-start | bytes 196616 | tf_op jit(solution)/shard_map/ppermute | solution.py:27
  7.2 0.9 copy-start.5
  8.1 0.8 copy-start.6
  11.0 34.8 %all-to-all-start = ((bf16[16,32,1792]{2,1,0:T(8,128)(2,1)}), bf16[16,32,1792]{2,1,0:T(8,128)(2,1)}, u32[]{:S(2)}, u32[]{:S(2)}) async-start(bf16[16,32,1792]{2,1,0:T(8,128)(2,1)} %shard_map.93), calls=%async_computation | async-start | bytes 3670016 | tf_op jit(solution)/shard_map/all_to_all | solution.py:111
  19.5 16.7 %collective-permute-start.5 = (bf16[64,1792]{1,0:T(8,128)(2,1)S(1)}, bf16[64,1792]{1,0:T(8,128)(2,1)S(1)}, u32[]{:S(2)}, u32[]{:S(2)}) collective-permute-start(bf16[64,1792]{1,0:T(8,128)(2,1)S(1)} %bitcast.205), channel_id=1, source_target_pairs={{0,12},{4,16},{8,20},{12,24},{16,28},{20,0},{24,4},{28,8},{1,21},{... | collective-permute-start | bytes 688136 | tf_op jit(solution)/shard_map/ppermute | solution.py:33
  26.0 12.8 %collective-permute-start.4 = (bf16[64,1792]{1,0:T(8,128)(2,1)S(1)}, bf16[64,1792]{1,0:T(8,128)(2,1)S(1)}, u32[]{:S(2)}, u32[]{:S(2)}) collective-permute-start(bf16[64,1792]{1,0:T(8,128)(2,1)S(1)} %bitcast.206), channel_id=1, source_target_pairs={{0,8},{4,12},{8,16},{12,20},{16,24},{20,28},{24,0},{28,4},{1,25},{... | collective-permute-start | bytes 688136 | tf_op jit(solution)/shard_map/ppermute | solution.py:33
  26.3 15.3 %collective-permute-start.3 = (bf16[64,1792]{1,0:T(8,128)(2,1)S(1)}, bf16[64,1792]{1,0:T(8,128)(2,1)S(1)}, u32[]{:S(2)}, u32[]{:S(2)}) collective-permute-start(bf16[64,1792]{1,0:T(8,128)(2,1)S(1)} %bitcast.207), channel_id=1, source_target_pairs={{0,4},{4,8},{8,12},{12,16},{16,20},{20,24},{24,28},{28,0},{1,29},{... | collective-permute-start | bytes 688136 | tf_op jit(solution)/shard_map/ppermute | solution.py:33
  26.7 18.1 %collective-permute-start.2 = (bf16[384,384]{1,0:T(8,128)(2,1)S(1)}, bf16[384,384]{1,0:T(8,128)(2,1)S(1)}, u32[]{:S(2)}, u32[]{:S(2)}) collective-permute-start(bf16[384,384]{1,0:T(8,128)(2,1)S(1)} %collective-permute-done), channel_id=1, source_target_pairs={{0,1},{1,0},{2,3},{3,2},{4,5},{5,4},{6,7},{7,6},{8,9},{9,8},{10,11... | collective-permute-start | bytes 884744 | tf_op jit(solution)/shard_map/ppermute | solution.py:27
  36.1 7.5 %collective-permute-start.9 = (bf16[32,1792]{1,0:T(8,128)(2,1)S(1)}, bf16[32,1792]{1,0:T(8,128)(2,1)S(1)}, u32[]{:S(2)}, u32[]{:S(2)}) collective-permute-start(bf16[32,1792]{1,0:T(8,128)(2,1)S(1)} %dynamic-slice_bitcast_fusion.1), channel_id=1, source_target_pairs={{0,4},{4,8},{8,12},{12,16},{16,20},{20,24},{24,28},{28,0},{1,29},{... | collective-permute-start | bytes 344072 | tf_op jit(solution)/shard_map/ppermute | solution.py:33
  36.7 9.1 %collective-permute-start.8 = (bf16[64,1792]{1,0:T(8,128)(2,1)S(1)}, bf16[64,1792]{1,0:T(8,128)(2,1)S(1)}, u32[]{:S(2)}, u32[]{:S(2)}) collective-permute-start(bf16[64,1792]{1,0:T(8,128)(2,1)S(1)} %collective-permute-done.5.refs_0_), channel_id=1, source_target_pairs={{0,1},{1,0},{2,3},{3,2},{4,5},{5,4},{6,7},{7,6},{8,9},{9,8},{10,11... | collective-permute-start | bytes 688136 | tf_op jit(solution)/shard_map/ppermute | solution.py:27
  38.8 7.0 %collective-permute-start.7 = (bf16[64,1792]{1,0:T(8,128)(2,1)S(1)}, bf16[64,1792]{1,0:T(8,128)(2,1)S(1)}, u32[]{:S(2)}, u32[]{:S(2)}) collective-permute-start(bf16[64,1792]{1,0:T(8,128)(2,1)S(1)} %collective-permute-done.4.refs_1_), channel_id=1, source_target_pairs={{0,1},{1,0},{2,3},{3,2},{4,5},{5,4},{6,7},{7,6},{8,9},{9,8},{10,11... | collective-permute-start | bytes 688136 | tf_op jit(solution)/shard_map/ppermute | solution.py:27
  41.6 4.3 %collective-permute-start.6 = (bf16[64,1792]{1,0:T(8,128)(2,1)S(1)}, bf16[64,1792]{1,0:T(8,128)(2,1)S(1)}, u32[]{:S(2)}, u32[]{:S(2)}) collective-permute-start(bf16[64,1792]{1,0:T(8,128)(2,1)S(1)} %collective-permute-done.3.refs_2_), channel_id=1, source_target_pairs={{0,1},{1,0},{2,3},{3,2},{4,5},{5,4},{6,7},{7,6},{8,9},{9,8},{10,11... | collective-permute-start | bytes 688136 | tf_op jit(solution)/shard_map/ppermute | solution.py:27
  43.6 2.2 %collective-permute-start.10 = (bf16[32,1792]{1,0:T(8,128)(2,1)S(1)}, bf16[32,1792]{1,0:T(8,128)(2,1)S(1)}, u32[]{:S(2)}, u32[]{:S(2)}) collective-permute-start(bf16[32,1792]{1,0:T(8,128)(2,1)S(1)} %collective-permute-done.9.refs_7_), channel_id=1, source_target_pairs={{0,1},{1,0},{2,3},{3,2},{4,5},{5,4},{6,7},{7,6},{8,9},{9,8},{10,11... | collective-permute-start | bytes 344072 | tf_op jit(solution)/shard_map/ppermute | solution.py:27
  45.8 0.6 copy-start.3
  45.8 0.7 copy-start.1
  46.6 0.9 copy-start.2
  47.5 0.9 copy-start.4
  48.6 2.1 %copy-start.10 = (bf16[768,384]{1,0:T(8,128)(2,1)S(1)}, bf16[768,384]{1,0:T(8,128)(2,1)}, u32[]{:S(2)}) copy-start(bf16[768,384]{1,0:T(8,128)(2,1)} %param.8) | copy-start | bytes 1769476
  50.7 3.4 %copy-start.9 = (f32[512,512]{1,0:T(8,128)}, f32[512,512]{1,0:T(8,128)S(1)}, u32[]{:S(2)}) copy-start(f32[512,512]{1,0:T(8,128)S(1)} %get-tuple-element.94) | copy-start | bytes 3145732
  51.6 2.4 %copy-start.7 = (f32[512,768]{1,0:T(8,128)}, f32[512,768]{1,0:T(8,128)S(1)}, u32[]{:S(2)}) copy-start(f32[512,768]{1,0:T(8,128)S(1)} %get-tuple-element.92) | copy-start | bytes 4718596
  55.2 14.3 %all-to-all-start.1 = ((f32[8,8,512]{2,1,0:T(8,128)}), f32[8,8,512]{2,1,0:T(8,128)S(1)}, u32[]{:S(2)}, u32[]{:S(2)}) async-start(f32[8,8,512]{2,1,0:T(8,128)} %broadcast_in_dim.6), calls=%async_computation.1 | async-start | bytes 262144 | tf_op jit(solution)/shard_map/all_to_all | solution.py:19
  69.6 6.7 %collective-permute-start.11 = (f32[8,512]{1,0:T(8,128)S(1)}, f32[8,512]{1,0:T(8,128)S(1)}, u32[]{:S(2)}, u32[]{:S(2)}) collective-permute-start(f32[8,512]{1,0:T(8,128)S(1)} %stack.131), channel_id=1, source_target_pairs={{0,1},{1,0},{2,3},{3,2},{4,5},{5,4},{6,7},{7,6},{8,9},{9,8},{10,11... | collective-permute-start | bytes 49160 | tf_op jit(solution)/shard_map/ppermute | solution.py:27
  78.0 1.9 %copy-start.8 = (f32[512,768]{1,0:T(8,128)S(1)}, f32[512,768]{1,0:T(8,128)}, u32[]{:S(2)}) copy-start(f32[512,768]{1,0:T(8,128)} %copy-done.7) | copy-start | bytes 4718596
  80.7 2.1 %collective-permute-start.12 = (bf16[384,768]{1,0:T(8,128)(2,1)S(1)}, bf16[384,768]{1,0:T(8,128)(2,1)S(1)}, u32[]{:S(2)}, u32[]{:S(2)}) collective-permute-start(bf16[384,768]{1,0:T(8,128)(2,1)S(1)} %fusion.19), channel_id=1, source_target_pairs={{0,1},{1,0},{2,3},{3,2},{4,5},{5,4},{6,7},{7,6},{8,9},{9,8},{10,11... | collective-permute-start | bytes 1769480 | tf_op jit(solution)/shard_map/ppermute | solution.py:27
  81.2 7.3 %collective-permute-start.14 = (bf16[256,768]{1,0:T(8,128)(2,1)S(1)}, bf16[256,768]{1,0:T(8,128)(2,1)}, u32[]{:S(2)}, u32[]{:S(2)}) collective-permute-start(bf16[256,768]{1,0:T(8,128)(2,1)S(1)} %slice.230), channel_id=1, source_target_pairs={{0,1},{1,0},{2,3},{3,2},{4,5},{5,4},{6,7},{7,6},{8,9},{9,8},{10,11... | collective-permute-start | bytes 1179656 | tf_op jit(solution)/shard_map/ppermute | solution.py:27
  84.4 25.8 %all-to-all-start.2 = ((bf16[16,56,768]{2,1,0:T(8,128)(2,1)}), bf16[16,56,768]{2,1,0:T(8,128)(2,1)S(1)}, u32[]{:S(2)}, u32[]{:S(2)}) async-start(bf16[16,56,768]{2,1,0:T(8,128)(2,1)} %pad_maximum_fusion), calls=%async_computation.2 | async-start | bytes 2752512 | tf_op jit(solution)/shard_map/all_to_all | solution.py:192
  89.8 8.1 %collective-permute-start.15 = (bf16[32,768]{1,0:T(8,128)(2,1)S(1)}, bf16[32,768]{1,0:T(8,128)(2,1)S(1)}, u32[]{:S(2)}, u32[]{:S(2)}) collective-permute-start(bf16[32,768]{1,0:T(8,128)(2,1)S(1)} %get-tuple-element.68), channel_id=1, source_target_pairs={{0,4},{4,8},{8,12},{12,16},{16,20},{20,24},{24,28},{28,0},{1,5},{5... | collective-permute-start | bytes 147464 | tf_op jit(solution)/shard_map/ppermute | solution.py:189
  90.2 9.0 %collective-permute-start.20 = (bf16[32,768]{1,0:T(8,128)(2,1)S(1)}, bf16[32,768]{1,0:T(8,128)(2,1)S(1)}, u32[]{:S(2)}, u32[]{:S(2)}) collective-permute-start(bf16[32,768]{1,0:T(8,128)(2,1)S(1)} %get-tuple-element.69), channel_id=1, source_target_pairs={{0,24},{4,28},{8,0},{12,4},{16,8},{20,12},{24,16},{28,20},{1,25},{... | collective-permute-start | bytes 147464 | tf_op jit(solution)/shard_map/ppermute | solution.py:189
  91.3 9.7 %collective-permute-start.19 = (bf16[32,768]{1,0:T(8,128)(2,1)S(1)}, bf16[32,768]{1,0:T(8,128)(2,1)S(1)}, u32[]{:S(2)}, u32[]{:S(2)}) collective-permute-start(bf16[32,768]{1,0:T(8,128)(2,1)S(1)} %get-tuple-element.70), channel_id=1, source_target_pairs={{0,20},{4,24},{8,28},{12,0},{16,4},{20,8},{24,12},{28,16},{1,21},{... | collective-permute-start | bytes 147464 | tf_op jit(solution)/shard_map/ppermute | solution.py:189
  92.9 8.1 %collective-permute-start.18 = (bf16[32,768]{1,0:T(8,128)(2,1)S(1)}, bf16[32,768]{1,0:T(8,128)(2,1)S(1)}, u32[]{:S(2)}, u32[]{:S(2)}) collective-permute-start(bf16[32,768]{1,0:T(8,128)(2,1)S(1)} %get-tuple-element.71), channel_id=1, source_target_pairs={{0,16},{4,20},{8,24},{12,28},{16,0},{20,4},{24,8},{28,12},{1,17},{... | collective-permute-start | bytes 147464 | tf_op jit(solution)/shard_map/ppermute | solution.py:189
  98.0 7.4 %collective-permute-start.17 = (bf16[32,768]{1,0:T(8,128)(2,1)S(1)}, bf16[32,768]{1,0:T(8,128)(2,1)S(1)}, u32[]{:S(2)}, u32[]{:S(2)}) collective-permute-start(bf16[32,768]{1,0:T(8,128)(2,1)S(1)} %get-tuple-element.72), channel_id=1, source_target_pairs={{0,12},{4,16},{8,20},{12,24},{16,28},{20,0},{24,4},{28,8},{1,13},{... | collective-permute-start | bytes 147464 | tf_op jit(solution)/shard_map/ppermute | solution.py:189
  98.0 7.4 %collective-permute-start.16 = (bf16[32,768]{1,0:T(8,128)(2,1)S(1)}, bf16[32,768]{1,0:T(8,128)(2,1)S(1)}, u32[]{:S(2)}, u32[]{:S(2)}) collective-permute-start(bf16[32,768]{1,0:T(8,128)(2,1)S(1)} %get-tuple-element.73), channel_id=1, source_target_pairs={{0,8},{4,12},{8,16},{12,20},{16,24},{20,28},{24,0},{28,4},{1,9},{5... | collective-permute-start | bytes 147464 | tf_op jit(solution)/shard_map/ppermute | solution.py:189
  99.1 6.2 %collective-permute-start.21 = (bf16[32,768]{1,0:T(8,128)(2,1)S(1)}, bf16[32,768]{1,0:T(8,128)(2,1)S(1)}, u32[]{:S(2)}, u32[]{:S(2)}) collective-permute-start(bf16[32,768]{1,0:T(8,128)(2,1)S(1)} %get-tuple-element.74), channel_id=1, source_target_pairs={{0,28},{4,0},{8,4},{12,8},{16,12},{20,16},{24,20},{28,24},{1,29},{... | collective-permute-start | bytes 147464 | tf_op jit(solution)/shard_map/ppermute | solution.py:189
  105.7 14.1 %collective-permute-start.22 = (bf16[32,384]{1,0:T(8,128)(2,1)S(1)}, bf16[32,384]{1,0:T(8,128)(2,1)S(1)}, u32[]{:S(2)}, u32[]{:S(2)}) collective-permute-start(bf16[32,384]{1,0:T(8,128)(2,1)S(1)} %bitcast.233), channel_id=1, source_target_pairs={{0,2},{2,0},{1,3},{3,1},{4,6},{6,4},{5,7},{7,5},{8,10},{10,8},{9,1... | collective-permute-start | bytes 73736 | tf_op jit(solution)/shard_map/ppermute | solution.py:27
  111.0 13.7 %all-to-all-start.3 = ((bf16[8,24,768]{2,1,0:T(8,128)(2,1)}), bf16[8,24,768]{2,1,0:T(8,128)(2,1)S(1)}, u32[]{:S(2)}, u32[]{:S(2)}) async-start(bf16[8,24,768]{2,1,0:T(8,128)(2,1)} %broadcast_in_dim.7), calls=%async_computation.3 | async-start | bytes 589824 | tf_op jit(solution)/shard_map/all_to_all | solution.py:19
  115.0 6.7 %collective-permute-start.13 = (bf16[32,768]{1,0:T(8,128)(2,1)S(1)}, bf16[32,768]{1,0:T(8,128)(2,1)S(1)}, u32[]{:S(2)}, u32[]{:S(2)}) collective-permute-start(bf16[32,768]{1,0:T(8,128)(2,1)S(1)} %slice_reduce_fusion), channel_id=1, source_target_pairs={{0,1},{1,0},{2,3},{3,2},{4,5},{5,4},{6,7},{7,6},{8,9},{9,8},{10,11... | collective-permute-start | bytes 147464 | tf_op jit(solution)/shard_map/ppermute | solution.py:27
  117.7 4.0 %collective-permute-start.23 = (f32[4,2,8]{2,0,1:T(4,128)S(1)}, f32[4,2,8]{2,0,1:T(4,128)S(1)}, u32[]{:S(2)}, u32[]{:S(2)}) collective-permute-start(f32[4,2,8]{2,0,1:T(4,128)S(1)} %fusion.42), channel_id=1, source_target_pairs={{0,2},{2,0},{1,3},{3,1},{4,6},{6,4},{5,7},{7,5},{8,10},{10,8},{9,1... | collective-permute-start | bytes 776 | tf_op jit(solution)/shard_map/ppermute | solution.py:27
  125.4 9.1 %collective-permute-start.24 = (bf16[2,32,384]{2,1,0:T(8,128)(2,1)S(1)}, bf16[2,32,384]{2,1,0:T(8,128)(2,1)S(1)}, u32[]{:S(2)}, u32[]{:S(2)}) collective-permute-start(bf16[2,32,384]{2,1,0:T(8,128)(2,1)S(1)} %maximum_select_fusion.8), channel_id=1, source_target_pairs={{0,1},{1,0},{2,3},{3,2},{4,5},{5,4},{6,7},{7,6},{8,9},{9,8},{10,11... | collective-permute-start | bytes 147464 | tf_op jit(solution)/shard_map/ppermute | solution.py:27
  129.9 11.1 %all-to-all-start.4 = ((bf16[8,48,384]{2,1,0:T(8,128)(2,1)}), bf16[8,48,384]{2,1,0:T(8,128)(2,1)S(1)}, u32[]{:S(2)}, u32[]{:S(2)}) async-start(bf16[8,48,384]{2,1,0:T(8,128)(2,1)} %broadcast_in_dim.8), calls=%async_computation.4 | async-start | bytes 589824 | tf_op jit(solution)/shard_map/all_to_all | solution.py:19
  141.0 2.3 %collective-permute-start.25 = (bf16[384,384]{1,0:T(8,128)(2,1)S(1)}, bf16[384,384]{1,0:T(8,128)(2,1)S(1)}, u32[]{:S(2)}, u32[]{:S(2)}) collective-permute-start(bf16[384,384]{1,0:T(8,128)(2,1)S(1)} %bitcast.217), channel_id=1, source_target_pairs={{0,1},{1,0},{2,3},{3,2},{4,5},{5,4},{6,7},{7,6},{8,9},{9,8},{10,11... | collective-permute-start | bytes 884744 | tf_op jit(solution)/shard_map/ppermute | solution.py:27
